TPU v7x, 256 devices: a whole 4x4x8 slice. The times are simulated.
256 devices in a mesh: seq: 32 (over z, y), mp: 8 (over x, core).
Axes of the slice: x: 4, y: 4, z: 8, core: 2. Of those that a mesh axis runs over, the one named last changes fastest.
Arguments:
- tokens: bfloat16 [65536, 2048], P('seq'), may hold values from -6 to 6
- w_proj: bfloat16 [2048, 4, 2048], P(None, None, 'mp')
- gain: float32 [2048], P('mp'), may hold values from 0.25 to 1.75
- level_codes: int32 [11, 16, 65536], P(None, 'mp', 'seq'), may hold values from 0 to 255
- w_codes: int32 [2048, 2048], P('mp'), may hold values from 40 to 199, as said below
- block_exponent: int32 [16, 16], P('mp'), may hold values from -7 to -5
Outputs:
- mixed: bfloat16 [65536, 2048], P(('seq', 'mp'))
Inputs may be any that keep to these rules, and one draw needn't show every extreme that they name: `w_codes`: each code is 128 s + 8 e + m with s of 0 or 1, e from 5 to 8 and m from 0 to 7.
All inputs are finite; a program needn't handle non-finite values.
Results may differ from a plain program's by a relative error of at most 0.015.
Values may be sent and summed in bfloat16 or wider, within the bound.
No kernel may reach another device: no remote copies, remote signals or barrier semaphores. Data moves between devices by JAX's collectives and lax.ppermute only.
A program may use at most 128 MiB of HBM per device.

v0:
```python
import math

import jax
import jax.numpy as jnp
from jax import lax
from jax.sharding import PartitionSpec as P

D = 2048
HEAD_DIM = 128
STRETCH = 64
BLOCK = 128


def power_of_two(field, bits):
    result = jnp.ones(field.shape, jnp.float32)
    for bit in range(bits):
        result = result * jnp.where(
            field // 2**bit % 2 == 1, jnp.float32(2.0**2**bit), jnp.float32(1.0)
        )
    return result


def decode_weight(codes, exponents, block):
    negative = codes // 128
    exponent = codes // 8 % 16
    mantissa = codes % 8
    magnitude = (8 + mantissa).astype(jnp.float32) * (1 - 2 * negative).astype(jnp.float32)
    magnitude = magnitude * power_of_two(exponent, 4) * jnp.float32(2.0 ** (-10))
    scales = power_of_two(exponents + 16, 5) * jnp.float32(2.0 ** (-16))
    rows, columns = codes.shape
    shaped = (
        magnitude.reshape(rows // block, block, columns // block, block) * scales[:, None, :, None]
    )
    return shaped.reshape(rows, columns).astype(jnp.bfloat16)


def body(tokens, w_proj, gain, level_codes, w_codes, block_exponent):
    tok_rows = tokens.shape[0]
    group_width = w_proj.shape[2]
    heads_here = group_width // HEAD_DIM
    stretches = tok_rows // STRETCH
    stretch_bits = stretches.bit_length() - 1
    weight = decode_weight(w_codes, block_exponent, BLOCK)
    projected = jnp.dot(
        tokens, w_proj.reshape(D, 4 * group_width), preferred_element_type=jnp.float32
    )
    projected = projected.reshape(tok_rows, 4, heads_here, HEAD_DIM)
    query = projected[:, 0].astype(jnp.bfloat16)
    keys = projected[:, 1].astype(jnp.bfloat16)
    values = projected[:, 2].astype(jnp.bfloat16)
    gate = jax.nn.silu(projected[:, 3].reshape(tok_rows, group_width))
    level_weight = (level_codes.astype(jnp.float32) / 128.0).transpose(0, 2, 1)
    level_count = level_codes.shape[0]
    query_blocks = query.reshape(stretches, STRETCH, heads_here, HEAD_DIM)
    key_blocks = keys.reshape(stretches, STRETCH, heads_here, HEAD_DIM)
    value_blocks = values.reshape(stretches, STRETCH, heads_here, HEAD_DIM)
    scores = jnp.einsum(
        "nthd,nshd->nhts", query_blocks, key_blocks, preferred_element_type=jnp.float32
    )
    causal = jnp.tril(jnp.ones((STRETCH, STRETCH), bool))
    weights = (
        jnp.where(causal[None, None], scores, 0.0) * (1.0 / math.sqrt(HEAD_DIM * STRETCH))
    ).astype(jnp.bfloat16)
    local = jnp.einsum("nhts,nshd->nthd", weights, value_blocks, preferred_element_type=jnp.float32)
    weight_tokens = level_weight.reshape(level_count, stretches, STRETCH, heads_here)
    total = weight_tokens[0][..., None] * local
    blocks = jnp.einsum(
        "nthd,nthe->nhde", key_blocks, value_blocks, preferred_element_type=jnp.float32
    )
    for level in range(stretch_bits):
        count = stretches >> level + 1
        span = STRETCH << level
        pairs = blocks.reshape(count, 2, heads_here, HEAD_DIM, HEAD_DIM)
        sibling = pairs[:, 0].astype(jnp.bfloat16)
        second = query_blocks.reshape(count, 2, span, heads_here, HEAD_DIM)[:, 1]
        term = jnp.einsum("pthd,phde->pthe", second, sibling, preferred_element_type=jnp.float32)
        term = term * (1.0 / math.sqrt(HEAD_DIM * span))
        weight_second = weight_tokens[level + 1].reshape(count, 2, span, heads_here)[:, 1]
        placed = jnp.stack([jnp.zeros_like(term), weight_second[..., None] * term], 1)
        total = total + placed.reshape(stretches, STRETCH, heads_here, HEAD_DIM)
        blocks = pairs[:, 0] + pairs[:, 1]
    device_state = blocks[0]
    seq_bits = lax.axis_size("seq").bit_length() - 1
    position = lax.axis_index("seq")
    start_value = jnp.zeros((seq_bits, heads_here, HEAD_DIM, HEAD_DIM), jnp.float32)
    piece = lax.all_gather(
        device_state[None].astype(jnp.bfloat16), "seq", axis=0, tiled=True
    ).astype(jnp.float32)
    sources = jnp.arange(piece.shape[0], dtype=jnp.int32)
    digits = jnp.arange(seq_bits, dtype=jnp.int32)
    lower = jnp.left_shift(jnp.right_shift(position, digits + 1), digits + 1)
    later_half = jnp.right_shift(position, digits) & 1 == 1
    widths = jnp.left_shift(jnp.int32(1), digits)
    inside = (
        (sources[None] >= lower[:, None])
        & (sources[None] < lower[:, None] + widths[:, None])
        & later_half[:, None]
    )
    earlier = start_value + jnp.einsum(
        "jn,nhde->jhde", inside.astype(jnp.float32), piece, precision=lax.Precision.HIGHEST
    )
    reads = earlier.astype(jnp.bfloat16)
    terms = jnp.einsum("thd,jhde->jthe", query, reads, preferred_element_type=jnp.float32)
    scale_list = jnp.array(
        [1.0 / math.sqrt(HEAD_DIM * (tok_rows << level)) for level in range(seq_bits)], jnp.float32
    )
    device_weight = level_weight[stretch_bits + 1 :] * scale_list[:, None, None]
    memory = total.reshape(tok_rows, heads_here, HEAD_DIM) + jnp.sum(
        device_weight[..., None] * terms, axis=0
    )
    normed = memory * lax.rsqrt(jnp.mean(memory * memory, axis=-1, keepdims=True) + 1e-06)
    attended = (normed.reshape(tok_rows, group_width) * gain * gate).astype(jnp.bfloat16)
    return lax.psum_scatter(
        jnp.dot(attended, weight, preferred_element_type=jnp.float32).astype(jnp.bfloat16),
        "mp",
        scatter_dimension=0,
        tiled=True,
    )


def solution(mesh):
    placed = (
        P("seq", None),
        P(None, None, "mp"),
        P("mp"),
        P(None, "mp", "seq"),
        P("mp", None),
        P("mp", None),
    )
    return jax.shard_map(
        body, mesh=mesh, in_specs=placed, out_specs=P(("seq", "mp"), None), check_vma=False
    )
```

profile of v0, /device:TPU:1, one launch (start us, length us, event | category | flops | bytes accessed | tf_op | source)
XLA Modules:
  0.0 218.0 jit_solution(1063128950867705044)
XLA Ops:
  6.5 5.2 %copy.237 = bf16[256,8,4,256]{3,1,2,0:T(8,128)(2,1)} copy(bf16[256,8,4,256]{3,2,1,0:T(4,128)(2,1)} %bitcast.255) | data formatting | bytes 8388608
  11.7 6.5 %copy.165 = bf16[1024,2048]{1,0:T(8,128)(2,1)} copy(bf16[1024,2048]{0,1:T(8,128)(2,1)} %bitcast.239) | data formatting | bytes 8388608 | tf_op jit(solution)/shard_map/dot_general | solution.py:44
  18.2 14.0 %fusion.151 = (bf16[2048,4,2,128]{3,0,2,1:T(8,128)(2,1)S(1)}, f32[2048,4,2,128]{3,0,2,1:T(8,128)}) fusion(bf16[4,2,128,2048]{3,2,1,0:T(8,128)(2,1)} %bitcast.256, bf16[2048,2048]{1,0:T(8,128)(2,1)} %param.7), kind=kOutput, calls=%fused_computation.245 | convolution fusion | flops 8592031744 | bytes 25165824 | tf_op jit(solution)/shard_map/dot_general | solution.py:44
  32.2 0.1 fusion.148
  32.4 0.0 copy-start.2
  32.4 0.0 copy-start.3
  32.4 0.8 fusion.88
  33.2 0.2 copy-done.2
  33.4 0.4 copy-done.3
  33.8 0.2 fusion.27
  34.1 1.7 copy-done
  35.8 0.1 fusion.62
  35.9 0.1 fusion.149
  36.0 1.0 copy.226
  37.0 0.2 copy.223
  37.2 1.3 add.195
  38.5 0.0 copy-start.8
  38.6 0.8 copy.200
  39.4 0.0 all-gather.3.cloned.1.call-update
  39.4 0.0 reduce-scatter.2.cloned.1.call-start
  39.5 1.7 slice.218
  41.2 3.1 %slice.167 = f32[2048,1,2,128]{3,0,2,1:T(8,128)} slice(f32[2048,4,2,128]{3,0,2,1:T(8,128)} %get-tuple-element.16), slice={[0:2048], [3:4], [0:2], [0:128]} | slice | bytes 4194304 | tf_op jit(solution)/shard_map/slice | solution.py:51
  44.3 1.0 multiply_bitcast_fusion
  45.3 0.7 copy-done.13
  46.0 0.1 mul.198
  46.1 0.6 slice.159
  46.8 0.1 reshape_squeeze.18
  46.9 1.0 slice_multiply_fusion
  47.9 0.7 copy.199
  48.6 2.9 %copy.208 = f32[2048,1,2,128]{0,3,2,1:T(8,128)} copy(f32[2048,1,2,128]{3,0,2,1:T(8,128)} %slice.167) | data formatting | bytes 4194304 | tf_op jit(solution)/shard_map/slice | solution.py:51
  51.5 2.9 %copy.210 = f32[2048,256]{1,0:T(8,128)} copy(f32[2048,256]{0,1:T(8,128)} %bitcast.252) | data formatting | bytes 4194304 | tf_op jit(solution)/shard_map/reshape;squeeze | solution.py:51
  54.5 0.0 copy-start.9
  54.5 0.5 fusion.46
  55.0 1.1 copy.233
  56.1 0.3 fusion.48
  56.4 1.4 copy.235
  57.8 0.3 fusion.50
  58.1 0.3 copy.234
  58.4 0.3 fusion.54
  58.7 1.3 copy.236
  60.0 2.7 %stack.39.clone = f32[1,2,1024,2,128]{4,2,1,3,0:T(8,128)} pad(f32[1,1,1024,2,128]{4,2,1,3,0:T(8,128)} %copy.236, f32[]{:T(128)} %constant.206.clone.1), padding=0_0x1_0x0_0x0_0x0_0 | pad | bytes 3145732 | tf_op jit(solution)/shard_map/stack | solution.py:79
  62.7 1.5 stack.35.clone
  64.2 0.0 copy-done.7
  64.3 1.5 stack.37.clone
  65.7 1.6 stack.33.clone
  67.4 0.5 copy-done.1
  67.9 0.4 fusion.52
  68.3 1.7 stack.31.clone
  70.0 6.1 %fusion.33 = f32[32,64,2,128]{3,1,2,0:T(8,128)S(1)} fusion(f32[16,2,64,2,128]{4,2,3,1,0:T(8,128)} %stack.31.clone, f32[32,64,2,128]{3,1,0,2:T(8,128)} %bitcast.246, f32[32,64,2,128]{3,1,0,2:T(8,128)} %bitcast.248, f32[32,64,2,128]{3,1,0,2:T(8,128)} %bitcast.247, f32[32,64,2,128]{3,1,0,2:T(8,128)} %bitcast.249, bf16[32,64,2,128]{3,1,0,2:T(8,128)(2,1)S(1)} %bitcast.238, ...), kind=kOutput, calls=%fused_computation.72 | convolution fusion | flops 138149888 | bytes 15749120 | tf_op jit(solution)/shard_map/nhts,nshd->nthd/dot_general | solution.py:64
  76.1 0.0 copy-start.16
  76.1 3.0 %copy.198 = f32[32,64,2,128]{3,2,1,0:T(2,128)} copy(f32[32,64,2,128]{3,1,2,0:T(8,128)S(1)} %fusion.33) | data formatting | bytes 4194304 | tf_op jit(solution)/shard_map/add | solution.py:80
  79.2 38.2 %all-gather.3.cloned.1.call-done = bf16[32,1,2,128,128]{4,3,2,1,0:T(8,128)(2,1)} async-done(((bf16[1,1,2,128,128]{4,3,2,1,0:T(8,128)(2,1)}), bf16[32,1,2,128,128]{4,3,2,1,0:T(8,128)(2,1)}) %all-gather.3.cloned.1.call-update) | async-done | bytes 2097168 | tf_op jit(solution)/shard_map/all_gather | solution.py:86
  117.4 2.8 %fusion.55 = bf16[5,2,128,128]{3,0,2,1:T(8,128)(2,1)S(1)} fusion(bf16[32,1,2,128,128]{4,3,2,1,0:T(8,128)(2,1)} %all-gather.3.cloned.1.call-done, s32[5]{0:T(128)S(1)} %get-tuple-element.18, s32[5]{0:T(128)S(1)} %get-tuple-element.17, pred[5]{0:T(512)(128)(4,1)S(1)} %and_compare_fusion), kind=kOutput, calls=%fused_computation.104 | convolution fusion | flops 10650240 | bytes 2424877 | tf_op jit(solution)/shard_map/jn,nhde->jhde/dot_general | solution.py:99
  120.2 4.7 %fusion = f32[2048,2,128]{0,2,1:T(8,128)} fusion(f32[5,2048,2]{1,0,2:T(8,128)S(1)} %copy-done.14, bf16[5,2,128,128]{3,0,2,1:T(8,128)(2,1)S(1)} %fusion.55, f32[2048,4,2,128]{3,0,2,1:T(8,128)} %get-tuple-element.16), kind=kOutput, calls=%fused_computation.1 | convolution fusion | flops 675807232 | bytes 3555328 | tf_op jit(solution)/shard_map/thd,jhde->jthe/dot_general | solution.py:103
  124.9 2.9 %copy.204 = f32[2048,2,128]{2,0,1:T(8,128)} copy(f32[2048,2,128]{0,2,1:T(8,128)} %fusion) | data formatting | bytes 4194304 | tf_op jit(solution)/shard_map/reduce_sum | solution.py:108
  127.8 2.9 %copy.203 = f32[2048,256]{1,0:T(8,128)} copy(f32[2048,256]{0,1:T(8,128)} %bitcast.250) | data formatting | bytes 4194304 | tf_op jit(solution)/shard_map/reduce_sum | solution.py:108
  130.7 2.2 %fusion.35 = f32[32,64,2]{1,2,0:T(2,128)S(1)} fusion(f32[32,64,2,128]{3,1,2,0:T(8,128)S(1)} %fusion.33, f32[32,64,2,128]{3,1,0,2:T(8,128)} %bitcast.251), kind=kLoop, calls=%fused_computation.76 | loop fusion | flops 1568768 | bytes 4210688 | tf_op jit(solution)/shard_map/reduce_sum | solution.py:111
  132.9 0.4 copy.214
  133.4 0.2 mul.255
  133.6 0.0 copy-start.17
  133.6 4.7 %mul.233 = f32[2048,2,128]{2,1,0:T(2,128)S(1)} broadcast(f32[2048,2]{1,0:T(8,128)S(1)} %bitcast.253), dimensions={0,1} | broadcast | bytes 2113536 | tf_op jit(solution)/shard_map/mul | solution.py:111
  138.3 17.2 %convolution_convert_fusion = bf16[2048,2048]{1,0:T(8,128)(2,1)} fusion(f32[32,8,16,128]{3,2,1,0:T(8,128)S(1)} %bitcast.261, s32[256,2048]{1,0:T(8,128)} %param.11, f32[256,8,2,128]{3,2,1,0:T(2,128)S(1)} %bitcast.259, f32[2048,256]{1,0:T(8,128)S(1)} %copy-done.12, f32[256,8,2,128]{3,2,1,0:T(2,128)S(1)} %bitcast.260, f32[2048,256]{1,0:T(8,128)S(1)} %copy-done.10, ...), kind=kOutput, calls=%fused_computation.4 | convolution fusion | flops 2226126848 | bytes 20972544 | tf_op jit(solution)/shard_map/dot_general | solution.py:114
  155.5 0.0 reduce-scatter.2.cloned.1.call-update
  155.5 55.7 %reduce-scatter.2.cloned.1.call-done = bf16[256,2048]{1,0:T(8,128)(2,1)} async-done(((bf16[2048,2048]{1,0:T(8,128)(2,1)}), bf16[256,2048]{1,0:T(8,128)(2,1)}) %reduce-scatter.2.cloned.1.call-update) | async-done | bytes 1048592 | tf_op jit(solution)/shard_map/reduce_scatter | solution.py:113
  (45 shorter events, 0.4 us)
Async XLA Ops:
  6.5 110.9 %all-gather.3.cloned.1.call-start = ((), (), s32[]{:S(2)}) async-start(), calls=%async_computation.2 | async-start | bytes 2162688 | tf_op jit(solution)/shard_map/all_gather | solution.py:86
  32.4 1.0 copy-start.2
  32.4 1.4 copy-start.3
  33.8 2.0 copy-start
  37.2 2.2 %copy-start.4 = (f32[4,1,2,128,128]{3,4,2,0,1:T(8,128)}, f32[4,1,2,128,128]{3,4,2,0,1:T(8,128)S(1)}, u32[]{:S(2)}) copy-start(f32[4,1,2,128,128]{3,4,2,0,1:T(8,128)S(1)} %copy.223) | copy-start | bytes 1572868
  38.5 0.9 copy-start.8
  39.4 171.8 %reduce-scatter.2.cloned.1.call-start = ((), (), s32[]{:S(2)}) async-start(), calls=%async_computation.1 | async-start | bytes 9437184 | tf_op jit(solution)/shard_map/reduce_scatter | solution.py:113
  45.3 0.7 copy-start.13
  54.5 1.6 copy-start.15
  54.5 1.6 copy-start.9
  56.0 1.7 copy-start.5
  62.7 1.5 copy-start.7
  62.7 3.0 %copy-start.6 = (f32[8,1,128,2,128]{4,2,1,0,3:T(8,128)S(1)}, f32[8,1,128,2,128]{4,2,1,0,3:T(8,128)}, u32[]{:S(2)}) copy-start(f32[8,1,128,2,128]{4,2,1,0,3:T(8,128)} %copy.233) | copy-start | bytes 3145732
  64.3 3.6 %copy-start.1 = (f32[32,2,128,128]{3,2,1,0:T(8,128)S(1)}, f32[32,2,128,128]{3,2,1,0:T(8,128)}, u32[]{:S(2)}) copy-start(f32[32,2,128,128]{3,2,1,0:T(8,128)} %copy-done) | copy-start | bytes 12582916
  76.1 3.1 %copy-start.16 = (s32[2,16]{1,0:T(2,128)S(1)}, s32[2,16]{1,0:T(2,128)}, u32[]{:S(2)}) copy-start(s32[2,16]{1,0:T(2,128)} %param.12) | copy-start | bytes 388
  79.1 41.1 %copy-start.14 = (f32[5,2048,2]{1,0,2:T(8,128)S(1)}, f32[5,2048,2]{1,0,2:T(8,128)}, u32[]{:S(2)}) copy-start(f32[5,2048,2]{1,0,2:T(8,128)} %copy.199) | copy-start | bytes 245764
  132.9 5.3 %copy-start.12 = (f32[2048,256]{1,0:T(8,128)S(1)}, f32[2048,256]{1,0:T(8,128)}, u32[]{:S(2)}) copy-start(f32[2048,256]{1,0:T(8,128)} %copy.203) | copy-start | bytes 6291460
  133.4 4.9 %copy-start.11 = (f32[32,64,2,128]{3,2,1,0:T(2,128)S(1)}, f32[32,64,2,128]{3,2,1,0:T(2,128)}, u32[]{:S(2)}) copy-start(f32[32,64,2,128]{3,2,1,0:T(2,128)} %copy.198) | copy-start | bytes 6291460
  133.6 4.7 %copy-start.10 = (f32[2048,256]{1,0:T(8,128)S(1)}, f32[2048,256]{1,0:T(8,128)}, u32[]{:S(2)}) copy-start(f32[2048,256]{1,0:T(8,128)} %copy.210) | copy-start | bytes 6291460
  133.6 4.7 %copy-start.17 = (f32[256]{0:T(256)S(1)}, f32[256]{0:T(256)}, u32[]{:S(2)}) copy-start(f32[256]{0:T(256)} %param.9) | copy-start | bytes 3076
Sparse Core Ops, SparseCore 0:
  39.5 77.8 all-gather.2
  155.7 55.4 reduce-scatter.1
where the time goes:
time: 219 us; the launch traced here: 218 us
  waiting for transfers between devices  93.9 us (43%)
  local copies, waits for them, and re-layouts  56.9 us (26%)
  matrix products  47.4 us (22%)
  between operations  13.8 us (6%)
  other arithmetic  6.03 us (3%)
    reduce_scatter x1, waiting for transfers between devices, body(): lax.psum_scatter(jnp.dot(attended, weight, preferred_element_type=jnp.flo...  55.7 us
    all_gather x1, waiting for transfers between devices, body(): lax.all_gather(device_state[None].astype(jnp.bfloat16), 'seq', axis=0, ti...  38.2 us
    dot_general x1, matrix products, body(): jnp.dot(attended, weight, preferred_element_type=jnp.float32)  17.2 us
    unnamed x43, local copies, waits for them, and re-layouts  14.1 us
    dot_general x1, matrix products, body(): jnp.dot(tokens, w_proj.reshape(D, 4 * group_width), preferred_element_typ...  14 us
    another operation x5, local copies, waits for them, and re-layouts, body(): jnp.stack([jnp.zeros_like(term), weight_second[..., None] * term], 1)  8.94 us
    dot_general x1, local copies, waits for them, and re-layouts, body(): jnp.dot(tokens, w_proj.reshape(D, 4 * group_width), preferred_element_typ...  6.52 us
    dot_general x1, matrix products, body(): jnp.einsum('nhts,nshd->nthd', weights, value_blocks, preferred_element_ty...  6.08 us
  transfers between devices with their start and end apart: 2, of which 2 were waited for; matrix products, arithmetic and copies ran while one was open for 18% of the time, Pallas kernels for 0%

commit v1 on v0

v1 whole, which is shorter than its diff:
```python
import math

import jax
import jax.numpy as jnp
from jax import lax
from jax.experimental import pallas as pl
from jax.experimental.pallas import tpu as pltpu
from jax.sharding import PartitionSpec as P

D = 2048
HEAD_DIM = 128
STRETCH = 64
BLOCK = 128
TILE = 256
F32 = jnp.float32
BF16 = jnp.bfloat16
VMEM_LIMIT = 56 * 1024 * 1024


def cost(flops, size):
    return pl.CostEstimate(flops=int(flops), bytes_accessed=int(size), transcendentals=0)


def full(shape):
    zeros = (0,) * len(shape)
    return pl.BlockSpec(shape, lambda *_: zeros)


def dot(a, b):
    return jnp.dot(a, b, preferred_element_type=F32)


def dot_nt(a, b):
    return lax.dot_general(a, b, (((1,), (1,)), ((), ())), preferred_element_type=F32)


def power_of_two(field, bits):
    result = jnp.ones(field.shape, F32)
    for bit in range(bits):
        result = result * jnp.where(
            (field >> bit) & 1 == 1, jnp.float32(2.0**2**bit), jnp.float32(1.0)
        )
    return result


def decode_weight(codes, exponents, block):
    negative = codes >> 7
    exponent = (codes >> 3) & 15
    mantissa = codes & 7
    magnitude = (8 + mantissa).astype(F32) * (1 - 2 * negative).astype(F32)
    magnitude = magnitude * power_of_two(exponent, 4) * jnp.float32(2.0 ** (-10))
    scales = power_of_two(exponents + 16, 5) * jnp.float32(2.0 ** (-16))
    rows, columns = codes.shape
    shaped = (
        magnitude.reshape(rows // block, block, columns // block, block) * scales[:, None, :, None]
    )
    return shaped.reshape(rows, columns).astype(BF16)


def unpack_parts(r_ref, w_ref, f_ref, parts):
    chunk = f_ref.shape[1]
    for step in range(r_ref.shape[0] // chunk):
        slot = step % 2
        f_ref[slot] = r_ref[pl.ds(step * chunk, chunk), :].astype(F32)
        rows = chunk // 8
        for at, part in enumerate(parts):
            for half in range(2):
                piece = f_ref[slot, pl.ds(half * 4 + part, rows, stride=8), :]
                w_ref[pl.ds(step * rows, rows), pl.ds(at * 256 + half * 128, 128)] = piece.astype(BF16)


def keys_values_kernel(r_ref, x_ref, k_ref, vt_ref, sr_ref, tot_ref, w_ref, f_ref, u_ref):
    step = pl.program_id(0)

    @pl.when(step == 0)
    def _():
        unpack_parts(r_ref, w_ref, f_ref, (1, 2))

    projected = dot(x_ref[...], w_ref[...])
    keys = projected[:, :256].astype(BF16)
    k_ref[...] = keys
    vt = projected[:, 256:].T.astype(BF16)
    vt_ref[...] = vt
    subs = x_ref.shape[0] // TILE
    for sub in range(subs):
        at = slice(sub * TILE, (sub + 1) * TILE)
        u = dot(vt[:, at], keys[at])
        for head in range(2):
            lanes = slice(head * 128, (head + 1) * 128)
            u_ref[step * subs + sub, head] = u[lanes, lanes]

    @pl.when(step == pl.num_programs(0) - 1)
    def _():
        u01 = u_ref[0] + u_ref[1]
        u03 = u01 + (u_ref[2] + u_ref[3])
        u45 = u_ref[4] + u_ref[5]
        for at, tile in enumerate((0, 2, 4, 6)):
            sr_ref[at] = u_ref[tile].astype(BF16)
        sr_ref[4] = u01.astype(BF16)
        sr_ref[5] = u45.astype(BF16)
        sr_ref[6] = u03.astype(BF16)
        tot_ref[...] = (u03 + (u45 + (u_ref[6] + u_ref[7]))).astype(BF16)


def keys_values(r, tokens):
    rows = tokens.shape[0]
    tile = 512
    return pl.pallas_call(
        keys_values_kernel,
        grid=(rows // tile,),
        in_specs=[full(r.shape), pl.BlockSpec((tile, D), lambda i: (i, 0))],
        out_specs=[
            pl.BlockSpec((tile, 256), lambda i: (i, 0)),
            pl.BlockSpec((256, tile), lambda i: (0, i)),
            full((7, 2, 128, 128)),
            full((2, 128, 128)),
        ],
        out_shape=[
            jax.ShapeDtypeStruct((rows, 256), BF16),
            jax.ShapeDtypeStruct((256, rows), BF16),
            jax.ShapeDtypeStruct((7, 2, 128, 128), BF16),
            jax.ShapeDtypeStruct((2, 128, 128), BF16),
        ],
        scratch_shapes=[
            pltpu.VMEM((D, 512), BF16),
            pltpu.VMEM((2, 2048, 128), F32),
            pltpu.VMEM((8, 2, 128, 128), F32),
        ],
        compiler_params=pltpu.CompilerParams(vmem_limit_bytes=VMEM_LIMIT),
        cost_estimate=cost(2 * rows * D * 512, 14 * 2**20),
        name="keys_values",
    )(r, tokens)


def query_gate_kernel(r_ref, gain_ref, x_ref, q_ref, gg_ref, w_ref, f_ref):
    @pl.when(pl.program_id(0) == 0)
    def _():
        unpack_parts(r_ref, w_ref, f_ref, (0, 3))

    projected = dot(x_ref[...], w_ref[...])
    q_ref[...] = projected[:, :256].astype(BF16)
    g = projected[:, 256:]
    gg_ref[...] = gain_ref[...] * (g / (1.0 + jnp.exp(-g)))


def query_gate(r, gain, tokens):
    rows = tokens.shape[0]
    tile = 512
    return pl.pallas_call(
        query_gate_kernel,
        grid=(rows // tile,),
        in_specs=[full(r.shape), full((1, 256)), pl.BlockSpec((tile, D), lambda i: (i, 0))],
        out_specs=[
            pl.BlockSpec((tile, 256), lambda i: (i, 0)),
            pl.BlockSpec((tile, 256), lambda i: (i, 0)),
        ],
        out_shape=[
            jax.ShapeDtypeStruct((rows, 256), BF16),
            jax.ShapeDtypeStruct((rows, 256), F32),
        ],
        scratch_shapes=[pltpu.VMEM((D, 512), BF16), pltpu.VMEM((2, 2048, 128), F32)],
        compiler_params=pltpu.CompilerParams(vmem_limit_bytes=VMEM_LIMIT),
        cost_estimate=cost(2 * rows * D * 512, 15 * 2**20),
        name="query_gate",
    )(r, gain, tokens)


def level_scale(span):
    return 1.0 / (128.0 * math.sqrt(HEAD_DIM * span))


def local_kernel(q_ref, k_ref, vt_ref, codes_ref, sr_ref, out_ref):
    step = pl.program_id(0)
    subs = q_ref.shape[0] // TILE
    s = lax.broadcasted_iota(jnp.int32, (TILE, TILE), 0)
    t = lax.broadcasted_iota(jnp.int32, (TILE, TILE), 1)
    gap = (t >> 6) - (s >> 6)
    inside = (gap == 0) & (s <= t)
    odd = (gap == 1) & ((t >> 6) & 1 == 1)
    second = ((t >> 7) - (s >> 7) == 1)
    for sub in range(subs):
        tile = step * subs + sub
        at = slice(sub * TILE, (sub + 1) * TILE)
        flags = [((tile >> bit) & 1).astype(F32) for bit in range(3)]
        reads = (tile >> 1, 4 + (tile >> 2), 6)
        for head in range(2):
            lanes = slice(head * 128, (head + 1) * 128)

            def row(level, span, head=head, at=at):
                return codes_ref[level, head : head + 1, at].astype(F32) * level_scale(span)

            left = jnp.concatenate([k_ref[at, lanes]] + [sr_ref[r, head] for r in reads], axis=0)
            product = dot_nt(left, q_ref[at, lanes])
            weight = jnp.where(
                inside,
                row(0, STRETCH),
                jnp.where(
                    odd, row(1, STRETCH), jnp.where(second, row(2, 2 * STRETCH), 0.0)
                ),
            )
            masked = (product[:TILE] * weight).astype(BF16)
            total = dot(vt_ref[lanes, at], masked)
            for j in range(3):
                total += (row(3 + j, TILE << j) * flags[j]) * product[TILE + j * 128 : TILE + (j + 1) * 128]
            out_ref[lanes, at] = total


def local_levels(query, keys, vt, codes, sr):
    rows = query.shape[0]
    tile = 512
    return pl.pallas_call(
        local_kernel,
        grid=(rows // tile,),
        in_specs=[
            pl.BlockSpec((tile, 256), lambda i: (i, 0)),
            pl.BlockSpec((tile, 256), lambda i: (i, 0)),
            pl.BlockSpec((256, tile), lambda i: (0, i)),
            pl.BlockSpec((11, 2, tile), lambda i: (0, 0, i)),
            full(sr.shape),
        ],
        out_specs=pl.BlockSpec((256, tile), lambda i: (0, i)),
        out_shape=jax.ShapeDtypeStruct((256, rows), F32),
        compiler_params=pltpu.CompilerParams(vmem_limit_bytes=VMEM_LIMIT),
        cost_estimate=cost(6e9, 6 * 2**20),
        name="local_levels",
    )(query, keys, vt, codes, sr)


def attend_kernel(rows_here, flags_ref, q_ref, m_ref, gg_ref, codes_ref, r1, r2, r3, g1, g2, g3, h1, out_ref, sd_ref):
    @pl.when(pl.program_id(0) == 0)
    def _():
        for head in range(2):
            sd_ref[head, pl.ds(0, 128), :] = r1[head]
            sd_ref[head, pl.ds(128, 128), :] = (r2[head].astype(F32) + r3[head].astype(F32)).astype(BF16)
            sd_ref[head, pl.ds(256, 128), :] = g1[head]
            sd_ref[head, pl.ds(384, 128), :] = (g2[head].astype(F32) + g3[head].astype(F32)).astype(BF16)
            sd_ref[head, pl.ds(512, 128), :] = h1[head]

    for head in range(2):
        lanes = slice(head * 128, (head + 1) * 128)
        product = dot_nt(sd_ref[head], q_ref[:, lanes])
        memory = m_ref[lanes, :]
        for j in range(5):
            scale = flags_ref[j] * level_scale(rows_here << j)
            row = codes_ref[6 + j, head : head + 1, :].astype(F32) * scale
            memory += row * product[j * 128 : (j + 1) * 128]
        mean = jnp.mean(memory * memory, axis=0, keepdims=True)
        normed = memory * lax.rsqrt(mean + 1e-06)
        out_ref[:, lanes] = (normed.T * gg_ref[:, lanes]).astype(BF16)


def attend(flags, query, local, gg, codes, reads):
    rows = query.shape[0]
    tile = 512
    return pl.pallas_call(
        lambda *refs: attend_kernel(rows, *refs),
        grid=(rows // tile,),
        in_specs=[
            pl.BlockSpec(memory_space=pltpu.SMEM),
            pl.BlockSpec((tile, 256), lambda i: (i, 0)),
            pl.BlockSpec((256, tile), lambda i: (0, i)),
            pl.BlockSpec((tile, 256), lambda i: (i, 0)),
            pl.BlockSpec((11, 2, tile), lambda i: (0, 0, i)),
        ]
        + [full((2, 128, 128))] * 7,
        out_specs=pl.BlockSpec((tile, 256), lambda i: (i, 0)),
        out_shape=jax.ShapeDtypeStruct((rows, 256), BF16),
        scratch_shapes=[pltpu.VMEM((2, 640, 128), BF16)],
        compiler_params=pltpu.CompilerParams(vmem_limit_bytes=VMEM_LIMIT),
        cost_estimate=cost(3e9, 6 * 2**20),
        name="attend",
    )(flags, query, local, gg, codes, *reads)


def project_kernel(at_ref, a_ref, *refs):
    out_ref = refs[-1]
    total = None
    for place, (first, w_ref) in enumerate(zip((0, 0, 0, 0, 128) * 2, refs[:-1], strict=True)):
        block = a_ref[at_ref[place]]
        width = w_ref.shape[0]
        term = dot(block[:, first : first + width], w_ref[...])
        total = term if total is None else total + term
    out_ref[...] = total.astype(BF16)


def project(places, attended, pieces):
    columns = 512
    return pl.pallas_call(
        project_kernel,
        grid=(D // columns,),
        in_specs=[pl.BlockSpec(memory_space=pltpu.SMEM), full(attended.shape)]
        + [pl.BlockSpec((p.shape[0], columns), lambda i: (0, i)) for p in pieces],
        out_specs=pl.BlockSpec((attended.shape[1], columns), lambda i: (0, i)),
        out_shape=jax.ShapeDtypeStruct((attended.shape[1], D), BF16),
        compiler_params=pltpu.CompilerParams(vmem_limit_bytes=VMEM_LIMIT),
        cost_estimate=cost(2 * 256 * 2048 * 2048, 10 * 2**20),
        name="project",
    )(places, attended, *pieces)


def body(tokens, w_proj, gain, level_codes, w_codes, block_exponent):
    place = lax.axis_index("mp")
    position = lax.axis_index("seq")

    def along_x(block, by):
        return lax.ppermute(block, "mp", [(m, (m // 2 + by) % 4 * 2 + m % 2) for m in range(8)])

    def other_core(block):
        return lax.ppermute(block, "mp", [(m, m ^ 1) for m in range(8)])

    weight = decode_weight(w_codes, block_exponent, BLOCK)
    from_left = along_x(weight, 1)
    from_right = along_x(weight, -1)
    far_top = along_x(from_left[:128], 1)
    far_low = along_x(from_right[128:], -1)
    pieces = [weight, from_left, from_right, far_top, far_low]
    pieces = pieces + [other_core(piece) for piece in pieces]
    x, core = place // 2, place % 2
    ways = jnp.stack([x, (x + 3) % 4, (x + 1) % 4, (x + 2) % 4, (x + 2) % 4])
    places = jnp.concatenate([ways * 2 + core, ways * 2 + 1 - core]).astype(jnp.int32)

    r = w_proj.reshape(D, 4, 2, 128).transpose(0, 2, 1, 3).reshape(D * 8, 128)
    keys, vt, sr, state = keys_values(r, tokens)

    def across(block, pairs):
        return lax.ppermute(block, "seq", pairs)

    r1, r2, r3 = [across(state, [(i, i ^ k) for i in range(32)]) for k in (1, 2, 3)]
    group = state.astype(F32) + r1.astype(F32) + (r2.astype(F32) + r3.astype(F32))
    sent = group.astype(BF16)
    g1, g2, g3 = [across(sent, [(i, i ^ (4 * k)) for i in range(32)]) for k in (1, 2, 3)]
    half = group + g1.astype(F32) + (g2.astype(F32) + g3.astype(F32))
    h1 = across(half.astype(BF16), [(i, i + 16) for i in range(16)])
    flags = (position >> jnp.arange(5, dtype=jnp.int32) & 1).astype(F32)

    query, gg = query_gate(r, gain.reshape(1, 256), tokens)
    local = local_levels(query, keys, vt, level_codes, sr)
    attended = attend(flags, query, local, gg, level_codes, (r1, r2, r3, g1, g2, g3, h1))
    attended = lax.all_to_all(attended.reshape(8, 256, 256), "mp", 0, 0, tiled=True)
    return project(places, attended, pieces)


def solution(mesh):
    placed = (
        P("seq", None),
        P(None, None, "mp"),
        P("mp"),
        P(None, "mp", "seq"),
        P("mp", None),
        P("mp", None),
    )
    return jax.shard_map(
        body, mesh=mesh, in_specs=placed, out_specs=P(("seq", "mp"), None), check_vma=False
    )
```

time: 219 us -> 96.4 us (0.44)
  waiting for transfers between devices: 93.9 us -> 12.5 us
  local copies, waits for them, and re-layouts: 56.9 us -> 4.61 us
  matrix products: 47.4 us -> 0 us
  Pallas kernels: 0 us -> 42.6 us
  starting transfers between devices: 0.04 us -> 32.2 us
  between operations: 13.8 us -> 0.22 us
  other arithmetic: 6.03 us -> 3.63 us
    reduce_scatter x1 -> x0, waiting for transfers between devices: 55.7 us -> none  [body(): lax.psum_scatter(jnp.dot(attended, weight, preferred_element_type=jnp.flo...]
    dot_general x11 -> x0, matrix products: 47.4 us -> none  [the longest x1 17.2 us: body(): jnp.dot(attended, weight, preferred_element_type=jnp.float32)]
    pallas_call x0 -> x5, Pallas kernels: none -> 42.6 us  [the longest x1 11.7 us: keys_values(): pl.pallas_call(keys_values_kernel, grid=(rows // tile,), in_specs=[full(r...]
    all_gather x1 -> x0, waiting for transfers between devices: 38.2 us -> none  [body(): lax.all_gather(device_state[None].astype(jnp.bfloat16), 'seq', axis=0, ti...]
    ppermute x0 -> x16, starting transfers between devices: none -> 28.7 us  [the longest x7 16.6 us: across(): return lax.ppermute(block, 'seq', pairs)]
    unnamed x43 -> x26, local copies, waits for them, and re-layouts: 14.1 us -> 1.51 us
    all_to_all x0 -> x1, waiting for transfers between devices: none -> 12.4 us  [body(): lax.all_to_all(attended.reshape(8, 256, 256), 'mp', 0, 0, tiled=True)]
    another operation x10 -> x1, local copies, waits for them, and re-layouts: 12 us -> 0.08 us  [body(): ways = jnp.stack([x, (x + 3) % 4, (x + 1) % 4, (x + 2) % 4, (x + 2) % 4])]
  transfers between devices with their start and end apart: 2 -> 17, of which waited for: 2 -> 1; matrix products, arithmetic and copies ran while one was open for 18% -> 7% of each run, Pallas kernels for 0% -> 25%
where the time goes in v1:
time: 96.4 us; the launch traced here: 95.8 us
  Pallas kernels  42.6 us (44%)
  starting transfers between devices  32.2 us (33%)
  waiting for transfers between devices  12.5 us (13%)
  local copies, waits for them, and re-layouts  4.61 us (5%)
  other arithmetic  3.63 us (4%)
    ppermute x7, starting transfers between devices, across(): return lax.ppermute(block, 'seq', pairs)  16.6 us
    all_to_all x1, waiting for transfers between devices, body(): lax.all_to_all(attended.reshape(8, 256, 256), 'mp', 0, 0, tiled=True)  12.4 us
    pallas_call x1, Pallas kernels, keys_values(): pl.pallas_call(keys_values_kernel, grid=(rows // tile,), in_specs=[full(r...  11.7 us
    pallas_call x1, Pallas kernels, query_gate(): pl.pallas_call(query_gate_kernel, grid=(rows // tile,), in_specs=[full(r....  10.9 us
    pallas_call x1, Pallas kernels, project(): pl.pallas_call(project_kernel, grid=(D // columns,), in_specs=[pl.BlockSp...  7.3 us
    pallas_call x1, Pallas kernels, local_levels(): pl.pallas_call(local_kernel, grid=(rows // tile,), in_specs=[pl.BlockSpec...  6.91 us
    ppermute x5, starting transfers between devices, other_core(): return lax.ppermute(block, 'mp', [(m, m ^ 1) for m in range(8)])  6.65 us
    pallas_call x1, Pallas kernels, attend(): pl.pallas_call(lambda *refs: attend_kernel(rows, *refs), grid=(rows // ti...  5.83 us
  transfers between devices with their start and end apart: 17, of which 1 were waited for; matrix products, arithmetic and copies ran while one was open for 7% of the time, Pallas kernels for 25%

profile of v1, /device:TPU:1, one launch (start us, length us, event | category | flops | bytes accessed | tf_op | source)
XLA Modules:
  0.0 95.8 jit_solution(13865578156226968880)
XLA Ops:
  0.0 11.7 %keys_values.1 = (bf16[2048,256]{1,0:T(8,128)(2,1)}, bf16[256,2048]{1,0:T(8,128)(2,1)}, bf16[7,2,128,128]{3,2,1,0:T(8,128)(2,1)}, bf16[2,128,128]{2,1,0:T(8,128)(2,1)}) custom-call(bf16[16384,128]{1,0:T(8,128)(2,1)} %bitcast.19, bf16[2048,2048]{1,0:T(8,128)(2,1)} %x_ref.3), custom_call_target="tpu_custom_call" | custom-call | flops 4294967296 | bytes 14680064 | tf_op jit(solution)/shard_map/keys_values/pallas_call | solution.py:108
  11.7 0.0 copy-start.3
  11.7 2.2 %collective-permute-start = (bf16[2,128,128]{2,1,0:T(8,128)(2,1)}, bf16[2,128,128]{2,1,0:T(8,128)(2,1)S(1)}, u32[]{:S(2)}, u32[]{:S(2)}) collective-permute-start(bf16[2,128,128]{2,1,0:T(8,128)(2,1)} %get-tuple-element.16), channel_id=1, source_target_pairs={{0,8},{8,0},{16,24},{24,16},{32,40},{40,32},{48,56},{56,48},{64,72... | collective-permute-start | bytes 196616 | tf_op jit(solution)/shard_map/ppermute | solution.py:326
  13.9 2.6 %collective-permute-start.1 = (bf16[2,128,128]{2,1,0:T(8,128)(2,1)}, bf16[2,128,128]{2,1,0:T(8,128)(2,1)S(1)}, u32[]{:S(2)}, u32[]{:S(2)}) collective-permute-start(bf16[2,128,128]{2,1,0:T(8,128)(2,1)} %get-tuple-element.16), channel_id=1, source_target_pairs={{0,16},{8,24},{16,0},{24,8},{32,48},{40,56},{48,32},{56,40},{64,80... | collective-permute-start | bytes 196616 | tf_op jit(solution)/shard_map/ppermute | solution.py:326
  16.5 0.0 collective-permute-start.2
  16.5 0.0 copy-done.11
  16.6 0.2 mul.72
  16.8 0.0 copy-done.3
  16.8 2.4 %fusion.refs_0_ = bf16[256,2048]{1,0:T(8,128)(2,1)S(1)} fusion(f32[32,8,16,128]{3,2,1,0:T(8,128)S(1)} %bitcast.17, s32[256,2048]{1,0:T(8,128)S(1)} %copy-done.3), kind=kLoop, calls=%fused_computation.1 | loop fusion | flops 17301504 | bytes 5242880 | tf_op jit(solution)/shard_map/convert_element_type | solution.py:57
  19.2 0.0 copy-start
  19.2 1.3 %collective-permute-start.7 = (bf16[256,2048]{1,0:T(8,128)(2,1)S(1)}, bf16[256,2048]{1,0:T(8,128)(2,1)S(1)}, u32[]{:S(2)}, u32[]{:S(2)}) collective-permute-start(bf16[256,2048]{1,0:T(8,128)(2,1)S(1)} %fusion.refs_0_), channel_id=1, source_target_pairs={{0,2},{1,3},{2,4},{3,5},{4,6},{5,7},{6,0},{7,1},{8,10},{9,11},{10,... | collective-permute-start | bytes 3145736 | tf_op jit(solution)/shard_map/ppermute | solution.py:306
  20.5 1.5 %collective-permute-start.8 = (bf16[256,2048]{1,0:T(8,128)(2,1)S(1)}, bf16[256,2048]{1,0:T(8,128)(2,1)}, u32[]{:S(2)}, u32[]{:S(2)}) collective-permute-start(bf16[256,2048]{1,0:T(8,128)(2,1)S(1)} %fusion.refs_0_), channel_id=1, source_target_pairs={{0,6},{1,7},{2,0},{3,1},{4,2},{5,3},{6,4},{7,5},{8,14},{9,15},{10,... | collective-permute-start | bytes 3145736 | tf_op jit(solution)/shard_map/ppermute | solution.py:306
  22.0 10.9 %query_gate.1 = (bf16[2048,256]{1,0:T(8,128)(2,1)}, f32[2048,256]{1,0:T(8,128)}) custom-call(bf16[16384,128]{1,0:T(8,128)(2,1)} %bitcast.20, f32[1,256]{1,0:T(1,128)} %bitcast.21, bf16[2048,2048]{1,0:T(8,128)(2,1)} %x_ref.3), custom_call_target="tpu_custom_call" | custom-call | flops 4294967296 | bytes 15728640 | tf_op jit(solution)/shard_map/query_gate/pallas_call | solution.py:149
  32.9 0.0 collective-permute-done.refs_5_
  32.9 0.0 collective-permute-done.1.refs_6_
  32.9 0.0 copy-start.5
  32.9 0.0 collective-permute-done.2.refs_7_
  32.9 0.0 copy-done.7
  32.9 0.0 copy-start.6
  33.0 1.7 %collective-permute-start.3 = (bf16[2,128,128]{2,1,0:T(8,128)(2,1)S(1)}, bf16[2,128,128]{2,1,0:T(8,128)(2,1)S(1)}, u32[]{:S(2)}, u32[]{:S(2)}) collective-permute-start(bf16[2,128,128]{2,1,0:T(8,128)(2,1)S(1)} %fusion.1), channel_id=1, source_target_pairs={{0,32},{8,40},{16,48},{24,56},{32,0},{40,8},{48,16},{56,24},{64,96... | collective-permute-start | bytes 196616 | tf_op jit(solution)/shard_map/ppermute | solution.py:326
  34.7 3.0 %collective-permute-start.4 = (bf16[2,128,128]{2,1,0:T(8,128)(2,1)S(1)}, bf16[2,128,128]{2,1,0:T(8,128)(2,1)S(1)}, u32[]{:S(2)}, u32[]{:S(2)}) collective-permute-start(bf16[2,128,128]{2,1,0:T(8,128)(2,1)S(1)} %fusion.1), channel_id=1, source_target_pairs={{0,64},{8,72},{16,80},{24,88},{32,96},{40,104},{48,112},{56,120},{... | collective-permute-start | bytes 196616 | tf_op jit(solution)/shard_map/ppermute | solution.py:326
  37.7 0.0 collective-permute-start.5
  37.7 6.9 %local_levels.1.refs_2_ = f32[256,2048]{1,0:T(8,128)} custom-call(bf16[2048,256]{1,0:T(8,128)(2,1)} %get-tuple-element.11.q_ref.refs_1_, bf16[2048,256]{1,0:T(8,128)(2,1)} %get-tuple-element.12.k_ref, bf16[256,2048]{1,0:T(8,128)(2,1)} %get-tuple-element.13.vt_ref, s32[11,2,2048]{2,1,0:T(2,128)} %refs_4_.1, bf16[7,2,128,128]{3,2,1,0:T(8,128)(2,1)} %get-tuple-element.14.sr_ref), custom_call_target="tpu_custom_call" | custom-call | flops 6000000000 | bytes 6291456 | tf_op jit(solution)/shard_map/local_levels/pallas_call | solution.py:211
  44.6 0.0 collective-permute-done.3.refs_8_
  44.6 0.0 copy-done
  44.6 0.0 copy-start.8
  44.6 3.8 %collective-permute-start.11 = (bf16[256,2048]{1,0:T(8,128)(2,1)S(1)}, bf16[256,2048]{1,0:T(8,128)(2,1)}, u32[]{:S(2)}, u32[]{:S(2)}) collective-permute-start(bf16[256,2048]{1,0:T(8,128)(2,1)S(1)} %fusion.refs_0_), channel_id=1, source_target_pairs={{0,1},{1,0},{2,3},{3,2},{4,5},{5,4},{6,7},{7,6},{8,9},{9,8},{10,11... | collective-permute-start | bytes 3145736 | tf_op jit(solution)/shard_map/ppermute | solution.py:309
  48.4 0.0 collective-permute-done.4.refs_9_
  48.4 0.0 collective-permute-done.5.refs_10_
  48.4 0.0 copy-done.4
  48.4 0.0 copy-done.5
  48.4 0.0 copy-done.6
  48.4 0.0 copy-start.10
  48.4 0.1 add_convert_fusion
  48.5 7.1 %collective-permute-start.6 = (bf16[2,128,128]{2,1,0:T(8,128)(2,1)S(1)}, bf16[2,128,128]{2,1,0:T(8,128)(2,1)S(1)}, u32[]{:S(2)}, u32[]{:S(2)}) collective-permute-start(bf16[2,128,128]{2,1,0:T(8,128)(2,1)S(1)} %add_convert_fusion), channel_id=1, source_target_pairs={{0,128},{8,136},{16,144},{24,152},{32,160},{40,168},{48,176},{56,1... | collective-permute-start | bytes 196616 | tf_op jit(solution)/shard_map/ppermute | solution.py:326
  55.6 0.5 and_convert_fusion.refs_0_
  56.1 0.0 collective-permute-done.7.refs_1_
  56.1 0.9 slice.8
  57.1 0.0 collective-permute-start.9
  57.1 0.0 collective-permute-done.8.refs_2_
  57.1 1.9 %slice.9 = bf16[128,2048]{1,0:T(8,128)(2,1)} slice(bf16[256,2048]{1,0:T(8,128)(2,1)} %collective-permute-done.8.refs_2_), slice={[128:256], [0:2048]} | slice | bytes 1048576 | tf_op jit(solution)/shard_map/slice | solution.py:315
  58.9 2.7 %collective-permute-start.10 = (bf16[128,2048]{1,0:T(8,128)(2,1)}, bf16[128,2048]{1,0:T(8,128)(2,1)}, u32[]{:S(2)}, u32[]{:S(2)}) collective-permute-start(bf16[128,2048]{1,0:T(8,128)(2,1)} %slice.9), channel_id=1, source_target_pairs={{0,6},{1,7},{2,0},{3,1},{4,2},{5,3},{6,4},{7,5},{8,14},{9,15},{10,... | collective-permute-start | bytes 1572872 | tf_op jit(solution)/shard_map/ppermute | solution.py:306
  61.6 0.9 collective-permute-start.12
  62.5 0.0 collective-permute-done.6.refs_11_
  62.5 0.1 collective-permute-start.13
  62.6 0.0 copy-done.8
  62.6 0.0 copy-done.10
  62.6 0.5 copy-done.12
  63.1 5.8 %attend.1 = bf16[2048,256]{1,0:T(8,128)(2,1)} custom-call(f32[5]{0:T(128)} %and_convert_fusion.refs_0_, bf16[2048,256]{1,0:T(8,128)(2,1)} %get-tuple-element.11.q_ref.refs_1_, f32[256,2048]{1,0:T(8,128)} %local_levels.1.refs_2_, f32[2048,256]{1,0:T(8,128)} %get-tuple-element.15.refs_3_, s32[11,2,2048]{2,1,0:T(2,128)} %refs_4_.1, ...), custom_call_target="tpu_custom_call" | custom-call | flops 3000000000 | bytes 6291456 | tf_op jit(solution)/shard_map/attend/pallas_call | solution.py:255
  68.9 3.5 %all-to-all-start = ((bf16[8,256,256]{2,1,0:T(8,128)(2,1)}), bf16[8,256,256]{2,1,0:T(8,128)(2,1)S(1)}, u32[]{:S(2)}, u32[]{:S(2)}) async-start(bf16[8,256,256]{2,1,0:T(8,128)(2,1)} %bitcast.18), calls=%async_computation | async-start | bytes 2097152 | tf_op jit(solution)/shard_map/all_to_all | solution.py:339
  72.5 0.0 collective-permute-done.9.refs_3_
  72.5 0.5 collective-permute-start.14
  72.9 0.0 collective-permute-done.10.refs_4_
  72.9 1.5 %collective-permute-start.15 = (bf16[128,2048]{1,0:T(8,128)(2,1)}, bf16[128,2048]{1,0:T(8,128)(2,1)}, u32[]{:S(2)}, u32[]{:S(2)}) collective-permute-start(bf16[128,2048]{1,0:T(8,128)(2,1)} %collective-permute-done.10.refs_4_), channel_id=1, source_target_pairs={{0,1},{1,0},{2,3},{3,2},{4,5},{5,4},{6,7},{7,6},{8,9},{9,8},{10,11... | collective-permute-start | bytes 1572872 | tf_op jit(solution)/shard_map/ppermute | solution.py:309
  74.4 0.1 stack.20
  74.5 0.6 pad_add_fusion.at_ref
  75.1 0.0 collective-permute-done.11.refs_5_
  75.1 12.4 %all-to-all-done.a_ref = bf16[8,256,256]{2,1,0:T(8,128)(2,1)S(1)} async-done(((bf16[8,256,256]{2,1,0:T(8,128)(2,1)}), bf16[8,256,256]{2,1,0:T(8,128)(2,1)S(1)}, u32[]{:S(2)}, u32[]{:S(2)}) %all-to-all-start) | async-done | bytes 1048608 | tf_op jit(solution)/shard_map/all_to_all | solution.py:339
  87.5 0.0 collective-permute-done.14.refs_8_
  87.5 0.0 collective-permute-done.15.refs_9_
  87.5 0.0 collective-permute-done.12.refs_6_
  87.6 0.0 collective-permute-done.13.refs_7_
  87.6 0.9 copy-done.1
  88.5 7.3 %project.1 = bf16[256,2048]{1,0:T(8,128)(2,1)} custom-call(s32[10]{0:T(128)} %pad_add_fusion.at_ref, bf16[8,256,256]{2,1,0:T(8,128)(2,1)} %copy-done.1, bf16[256,2048]{1,0:T(8,128)(2,1)} %copy-done, bf16[256,2048]{1,0:T(8,128)(2,1)} %copy-done.2, bf16[256,2048]{1,0:T(8,128)(2,1)} %collective-permute-done.8.refs_2_, ...), custom_call_target="tpu_custom_call" | custom-call | flops 2147483648 | bytes 10485760 | tf_op jit(solution)/shard_map/project/pallas_call | solution.py:288
  (12 shorter events, 0.1 us)
Async XLA Ops:
  0.0 16.5 %copy-start.11 = (s32[2,16]{1,0:T(2,128)S(1)}, s32[2,16]{1,0:T(2,128)}, u32[]{:S(2)}) copy-start(s32[2,16]{1,0:T(2,128)} %param.11) | copy-start | bytes 388
  11.7 5.1 %copy-start.3 = (s32[256,2048]{1,0:T(8,128)S(1)}, s32[256,2048]{1,0:T(8,128)}, u32[]{:S(2)}) copy-start(s32[256,2048]{1,0:T(8,128)} %param.10) | copy-start | bytes 6291460
  11.7 21.2 %collective-permute-start = (bf16[2,128,128]{2,1,0:T(8,128)(2,1)}, bf16[2,128,128]{2,1,0:T(8,128)(2,1)S(1)}, u32[]{:S(2)}, u32[]{:S(2)}) collective-permute-start(bf16[2,128,128]{2,1,0:T(8,128)(2,1)} %get-tuple-element.16), channel_id=1, source_target_pairs={{0,8},{8,0},{16,24},{24,16},{32,40},{40,32},{48,56},{56,48},{64,72... | collective-permute-start | bytes 196616 | tf_op jit(solution)/shard_map/ppermute | solution.py:326
  13.9 19.0 %collective-permute-start.1 = (bf16[2,128,128]{2,1,0:T(8,128)(2,1)}, bf16[2,128,128]{2,1,0:T(8,128)(2,1)S(1)}, u32[]{:S(2)}, u32[]{:S(2)}) collective-permute-start(bf16[2,128,128]{2,1,0:T(8,128)(2,1)} %get-tuple-element.16), channel_id=1, source_target_pairs={{0,16},{8,24},{16,0},{24,8},{32,48},{40,56},{48,32},{56,40},{64,80... | collective-permute-start | bytes 196616 | tf_op jit(solution)/shard_map/ppermute | solution.py:326
  16.5 16.4 %collective-permute-start.2 = (bf16[2,128,128]{2,1,0:T(8,128)(2,1)}, bf16[2,128,128]{2,1,0:T(8,128)(2,1)S(1)}, u32[]{:S(2)}, u32[]{:S(2)}) collective-permute-start(bf16[2,128,128]{2,1,0:T(8,128)(2,1)} %get-tuple-element.16), channel_id=1, source_target_pairs={{0,24},{8,16},{16,8},{24,0},{32,56},{40,48},{48,40},{56,32},{64,88... | collective-permute-start | bytes 196616 | tf_op jit(solution)/shard_map/ppermute | solution.py:326
  19.2 25.4 %copy-start = (bf16[256,2048]{1,0:T(8,128)(2,1)}, bf16[256,2048]{1,0:T(8,128)(2,1)S(1)}, u32[]{:S(2)}) copy-start(bf16[256,2048]{1,0:T(8,128)(2,1)S(1)} %fusion.refs_0_) | copy-start | bytes 3145732
  19.2 36.9 %collective-permute-start.7 = (bf16[256,2048]{1,0:T(8,128)(2,1)S(1)}, bf16[256,2048]{1,0:T(8,128)(2,1)S(1)}, u32[]{:S(2)}, u32[]{:S(2)}) collective-permute-start(bf16[256,2048]{1,0:T(8,128)(2,1)S(1)} %fusion.refs_0_), channel_id=1, source_target_pairs={{0,2},{1,3},{2,4},{3,5},{4,6},{5,7},{6,0},{7,1},{8,10},{9,11},{10,... | collective-permute-start | bytes 3145736 | tf_op jit(solution)/shard_map/ppermute | solution.py:306
  20.5 36.6 %collective-permute-start.8 = (bf16[256,2048]{1,0:T(8,128)(2,1)S(1)}, bf16[256,2048]{1,0:T(8,128)(2,1)}, u32[]{:S(2)}, u32[]{:S(2)}) collective-permute-start(bf16[256,2048]{1,0:T(8,128)(2,1)S(1)} %fusion.refs_0_), channel_id=1, source_target_pairs={{0,6},{1,7},{2,0},{3,1},{4,2},{5,3},{6,4},{7,5},{8,14},{9,15},{10,... | collective-permute-start | bytes 3145736 | tf_op jit(solution)/shard_map/ppermute | solution.py:306
  22.0 11.0 %copy-start.7 = (bf16[2,128,128]{2,1,0:T(8,128)(2,1)S(1)}, bf16[2,128,128]{2,1,0:T(8,128)(2,1)}, u32[]{:S(2)}) copy-start(bf16[2,128,128]{2,1,0:T(8,128)(2,1)} %get-tuple-element.16) | copy-start | bytes 196612
  32.9 15.5 %copy-start.4 = (bf16[2,128,128]{2,1,0:T(8,128)(2,1)}, bf16[2,128,128]{2,1,0:T(8,128)(2,1)S(1)}, u32[]{:S(2)}) copy-start(bf16[2,128,128]{2,1,0:T(8,128)(2,1)S(1)} %collective-permute-done.refs_5_) | copy-start | bytes 196612
  32.9 15.5 %copy-start.5 = (bf16[2,128,128]{2,1,0:T(8,128)(2,1)}, bf16[2,128,128]{2,1,0:T(8,128)(2,1)S(1)}, u32[]{:S(2)}) copy-start(bf16[2,128,128]{2,1,0:T(8,128)(2,1)S(1)} %collective-permute-done.1.refs_6_) | copy-start | bytes 196612
  32.9 15.5 %copy-start.6 = (bf16[2,128,128]{2,1,0:T(8,128)(2,1)}, bf16[2,128,128]{2,1,0:T(8,128)(2,1)S(1)}, u32[]{:S(2)}) copy-start(bf16[2,128,128]{2,1,0:T(8,128)(2,1)S(1)} %collective-permute-done.2.refs_7_) | copy-start | bytes 196612
  33.0 11.6 %collective-permute-start.3 = (bf16[2,128,128]{2,1,0:T(8,128)(2,1)S(1)}, bf16[2,128,128]{2,1,0:T(8,128)(2,1)S(1)}, u32[]{:S(2)}, u32[]{:S(2)}) collective-permute-start(bf16[2,128,128]{2,1,0:T(8,128)(2,1)S(1)} %fusion.1), channel_id=1, source_target_pairs={{0,32},{8,40},{16,48},{24,56},{32,0},{40,8},{48,16},{56,24},{64,96... | collective-permute-start | bytes 196616 | tf_op jit(solution)/shard_map/ppermute | solution.py:326
  34.7 13.7 %collective-permute-start.4 = (bf16[2,128,128]{2,1,0:T(8,128)(2,1)S(1)}, bf16[2,128,128]{2,1,0:T(8,128)(2,1)S(1)}, u32[]{:S(2)}, u32[]{:S(2)}) collective-permute-start(bf16[2,128,128]{2,1,0:T(8,128)(2,1)S(1)} %fusion.1), channel_id=1, source_target_pairs={{0,64},{8,72},{16,80},{24,88},{32,96},{40,104},{48,112},{56,120},{... | collective-permute-start | bytes 196616 | tf_op jit(solution)/shard_map/ppermute | solution.py:326
  37.7 10.7 %collective-permute-start.5 = (bf16[2,128,128]{2,1,0:T(8,128)(2,1)S(1)}, bf16[2,128,128]{2,1,0:T(8,128)(2,1)S(1)}, u32[]{:S(2)}, u32[]{:S(2)}) collective-permute-start(bf16[2,128,128]{2,1,0:T(8,128)(2,1)S(1)} %fusion.1), channel_id=1, source_target_pairs={{0,96},{8,104},{16,112},{24,120},{32,64},{40,72},{48,80},{56,88},{... | collective-permute-start | bytes 196616 | tf_op jit(solution)/shard_map/ppermute | solution.py:326
  44.6 18.0 %copy-start.8 = (bf16[2,128,128]{2,1,0:T(8,128)(2,1)}, bf16[2,128,128]{2,1,0:T(8,128)(2,1)S(1)}, u32[]{:S(2)}) copy-start(bf16[2,128,128]{2,1,0:T(8,128)(2,1)S(1)} %collective-permute-done.3.refs_8_) | copy-start | bytes 196612
  44.6 30.5 %collective-permute-start.11 = (bf16[256,2048]{1,0:T(8,128)(2,1)S(1)}, bf16[256,2048]{1,0:T(8,128)(2,1)}, u32[]{:S(2)}, u32[]{:S(2)}) collective-permute-start(bf16[256,2048]{1,0:T(8,128)(2,1)S(1)} %fusion.refs_0_), channel_id=1, source_target_pairs={{0,1},{1,0},{2,3},{3,2},{4,5},{5,4},{6,7},{7,6},{8,9},{9,8},{10,11... | collective-permute-start | bytes 3145736 | tf_op jit(solution)/shard_map/ppermute | solution.py:309
  48.4 14.2 %copy-start.9 = (bf16[2,128,128]{2,1,0:T(8,128)(2,1)}, bf16[2,128,128]{2,1,0:T(8,128)(2,1)S(1)}, u32[]{:S(2)}) copy-start(bf16[2,128,128]{2,1,0:T(8,128)(2,1)S(1)} %collective-permute-done.4.refs_9_) | copy-start | bytes 196612
  48.4 14.2 %copy-start.10 = (bf16[2,128,128]{2,1,0:T(8,128)(2,1)}, bf16[2,128,128]{2,1,0:T(8,128)(2,1)S(1)}, u32[]{:S(2)}) copy-start(bf16[2,128,128]{2,1,0:T(8,128)(2,1)S(1)} %collective-permute-done.5.refs_10_) | copy-start | bytes 196612
  48.5 14.0 %collective-permute-start.6 = (bf16[2,128,128]{2,1,0:T(8,128)(2,1)S(1)}, bf16[2,128,128]{2,1,0:T(8,128)(2,1)S(1)}, u32[]{:S(2)}, u32[]{:S(2)}) collective-permute-start(bf16[2,128,128]{2,1,0:T(8,128)(2,1)S(1)} %add_convert_fusion), channel_id=1, source_target_pairs={{0,128},{8,136},{16,144},{24,152},{32,160},{40,168},{48,176},{56,1... | collective-permute-start | bytes 196616 | tf_op jit(solution)/shard_map/ppermute | solution.py:326
  56.1 12.8 %copy-start.2 = (bf16[256,2048]{1,0:T(8,128)(2,1)}, bf16[256,2048]{1,0:T(8,128)(2,1)S(1)}, u32[]{:S(2)}) copy-start(bf16[256,2048]{1,0:T(8,128)(2,1)S(1)} %collective-permute-done.7.refs_1_) | copy-start | bytes 3145732
  57.1 15.4 %collective-permute-start.9 = (bf16[128,2048]{1,0:T(8,128)(2,1)}, bf16[128,2048]{1,0:T(8,128)(2,1)}, u32[]{:S(2)}, u32[]{:S(2)}) collective-permute-start(bf16[128,2048]{1,0:T(8,128)(2,1)} %slice.8), channel_id=1, source_target_pairs={{0,2},{1,3},{2,4},{3,5},{4,6},{5,7},{6,0},{7,1},{8,10},{9,11},{10,... | collective-permute-start | bytes 1572872 | tf_op jit(solution)/shard_map/ppermute | solution.py:306
  58.9 14.0 %collective-permute-start.10 = (bf16[128,2048]{1,0:T(8,128)(2,1)}, bf16[128,2048]{1,0:T(8,128)(2,1)}, u32[]{:S(2)}, u32[]{:S(2)}) collective-permute-start(bf16[128,2048]{1,0:T(8,128)(2,1)} %slice.9), channel_id=1, source_target_pairs={{0,6},{1,7},{2,0},{3,1},{4,2},{5,3},{6,4},{7,5},{8,14},{9,15},{10,... | collective-permute-start | bytes 1572872 | tf_op jit(solution)/shard_map/ppermute | solution.py:306
  61.6 25.9 %collective-permute-start.12 = (bf16[256,2048]{1,0:T(8,128)(2,1)S(1)}, bf16[256,2048]{1,0:T(8,128)(2,1)}, u32[]{:S(2)}, u32[]{:S(2)}) collective-permute-start(bf16[256,2048]{1,0:T(8,128)(2,1)S(1)} %collective-permute-done.7.refs_1_), channel_id=1, source_target_pairs={{0,1},{1,0},{2,3},{3,2},{4,5},{5,4},{6,7},{7,6},{8,9},{9,8},{10,11... | collective-permute-start | bytes 3145736 | tf_op jit(solution)/shard_map/ppermute | solution.py:309
  62.5 0.6 copy-start.12
  62.5 25.1 %collective-permute-start.13 = (bf16[256,2048]{1,0:T(8,128)(2,1)}, bf16[256,2048]{1,0:T(8,128)(2,1)}, u32[]{:S(2)}, u32[]{:S(2)}) collective-permute-start(bf16[256,2048]{1,0:T(8,128)(2,1)} %collective-permute-done.8.refs_2_), channel_id=1, source_target_pairs={{0,1},{1,0},{2,3},{3,2},{4,5},{5,4},{6,7},{7,6},{8,9},{9,8},{10,11... | collective-permute-start | bytes 3145736 | tf_op jit(solution)/shard_map/ppermute | solution.py:309
  68.9 18.6 %all-to-all-start = ((bf16[8,256,256]{2,1,0:T(8,128)(2,1)}), bf16[8,256,256]{2,1,0:T(8,128)(2,1)S(1)}, u32[]{:S(2)}, u32[]{:S(2)}) async-start(bf16[8,256,256]{2,1,0:T(8,128)(2,1)} %bitcast.18), calls=%async_computation | async-start | bytes 2097152 | tf_op jit(solution)/shard_map/all_to_all | solution.py:339
  72.5 15.1 %collective-permute-start.14 = (bf16[128,2048]{1,0:T(8,128)(2,1)}, bf16[128,2048]{1,0:T(8,128)(2,1)}, u32[]{:S(2)}, u32[]{:S(2)}) collective-permute-start(bf16[128,2048]{1,0:T(8,128)(2,1)} %collective-permute-done.9.refs_3_), channel_id=1, source_target_pairs={{0,1},{1,0},{2,3},{3,2},{4,5},{5,4},{6,7},{7,6},{8,9},{9,8},{10,11... | collective-permute-start | bytes 1572872 | tf_op jit(solution)/shard_map/ppermute | solution.py:309
  72.9 14.6 %collective-permute-start.15 = (bf16[128,2048]{1,0:T(8,128)(2,1)}, bf16[128,2048]{1,0:T(8,128)(2,1)}, u32[]{:S(2)}, u32[]{:S(2)}) collective-permute-start(bf16[128,2048]{1,0:T(8,128)(2,1)} %collective-permute-done.10.refs_4_), channel_id=1, source_target_pairs={{0,1},{1,0},{2,3},{3,2},{4,5},{5,4},{6,7},{7,6},{8,9},{9,8},{10,11... | collective-permute-start | bytes 1572872 | tf_op jit(solution)/shard_map/ppermute | solution.py:309
  87.5 1.0 %copy-start.1 = (bf16[8,256,256]{2,1,0:T(8,128)(2,1)}, bf16[8,256,256]{2,1,0:T(8,128)(2,1)S(1)}, u32[]{:S(2)}) copy-start(bf16[8,256,256]{2,1,0:T(8,128)(2,1)S(1)} %all-to-all-done.a_ref) | copy-start | bytes 3145732

commit v2 on v1

v2 whole, which is shorter than its diff:
```python
import math

import jax
import jax.numpy as jnp
from jax import lax
from jax.experimental import pallas as pl
from jax.experimental.pallas import tpu as pltpu
from jax.sharding import PartitionSpec as P

D = 2048
HEAD_DIM = 128
STRETCH = 64
BLOCK = 128
TILE = 256
F32 = jnp.float32
BF16 = jnp.bfloat16
MIB = 1024 * 1024
VMEM_LIMIT = 60 * MIB


def cost(flops, size):
    return pl.CostEstimate(flops=int(flops), bytes_accessed=int(size), transcendentals=0)


def full(shape, buffers=2):
    zeros = (0,) * len(shape)
    return pl.BlockSpec(shape, lambda *_: zeros, pipeline_mode=pl.Buffered(buffers))


def dot(a, b):
    return jnp.dot(a, b, preferred_element_type=F32)


def dot_nt(a, b):
    return lax.dot_general(a, b, (((1,), (1,)), ((), ())), preferred_element_type=F32)


def decode_kernel(exponent_ref, codes_ref, out_ref):
    step = pl.program_id(0)
    blocks = codes_ref.shape[1] // BLOCK
    for half in range(2):
        rows = slice(half * BLOCK, (half + 1) * BLOCK)
        for block in range(blocks):
            lanes = slice(block * BLOCK, (block + 1) * BLOCK)
            codes = codes_ref[rows, lanes]
            power = exponent_ref[half, step * blocks + block] + 16
            scale = jnp.left_shift(jnp.int32(1), power).astype(F32) * jnp.float32(2.0 ** (-26))
            size = jnp.left_shift(8 + (codes & 7), (codes >> 3) & 15)
            size = jnp.where(codes >= 128, -size, size).astype(F32)
            out_ref[rows, lanes] = (size * scale).astype(BF16)


def decode_weight(codes, exponents):
    columns = 1024
    return pl.pallas_call(
        decode_kernel,
        grid=(D // columns,),
        in_specs=[
            pl.BlockSpec(memory_space=pltpu.SMEM),
            pl.BlockSpec((2 * BLOCK, columns), lambda i: (0, i)),
        ],
        out_specs=pl.BlockSpec((2 * BLOCK, columns), lambda i: (0, i)),
        out_shape=jax.ShapeDtypeStruct((2 * BLOCK, D), BF16),
        compiler_params=pltpu.CompilerParams(vmem_limit_bytes=VMEM_LIMIT),
        cost_estimate=cost(8e6, 3 * MIB),
        name="decode_weight",
    )(exponents, codes)


CHUNKS = 8
ROWS = 512
PARTS = (1, 2, 0, 3)


def unpack_chunk(chunk, parts, r_buf, w_ref, f_ref):
    size = r_buf.shape[0] // CHUNKS
    slot = chunk % f_ref.shape[0]
    f_ref[slot] = r_buf[pl.ds(chunk * size, size), :].astype(F32)
    rows = size // 8
    for at, part in enumerate(parts):
        for half in range(2):
            piece = f_ref[slot, pl.ds(half * 4 + part, rows, stride=8), :]
            w_ref[pl.ds(chunk * rows, rows), pl.ds(at * 256 + half * 128, 128)] = piece.astype(BF16)


def project_tiles(r_hbm, x_hbm, r_buf, x_buf, w_ref, f_ref, acc_ref, r_sem, x_sem, finish):
    size = r_buf.shape[0] // CHUNKS
    deep = w_ref.shape[0] // CHUNKS
    tiles = x_buf.shape[0] // ROWS

    def chunk_copy(chunk):
        at = pl.ds(chunk * size, size)
        return pltpu.make_async_copy(r_hbm.at[at], r_buf.at[at], r_sem.at[chunk])

    def tile_copy(tile):
        at = pl.ds(tile * ROWS, ROWS)
        return pltpu.make_async_copy(x_hbm.at[at], x_buf.at[at], x_sem.at[tile])

    r_copies = [chunk_copy(chunk) for chunk in range(CHUNKS)]
    x_copies = [tile_copy(tile) for tile in range(tiles)]
    for copy in r_copies[:2] + x_copies[:1] + r_copies[2:] + x_copies[1:]:
        copy.start()
    for chunk in range(2):
        r_copies[chunk].wait()
        unpack_chunk(chunk, PARTS, r_buf, w_ref, f_ref)
    x_copies[0].wait()
    for chunk in range(CHUNKS):
        if chunk + 2 < CHUNKS:
            r_copies[chunk + 2].wait()
        at = pl.ds(chunk * deep, deep)
        term = dot(x_buf[pl.ds(0, ROWS), at], w_ref[at, :])
        if chunk == 0:
            acc_ref[0] = term
        else:
            acc_ref[0] += term
        if chunk + 2 < CHUNKS:
            unpack_chunk(chunk + 2, PARTS, r_buf, w_ref, f_ref)
    for tile in range(1, tiles):
        x_copies[tile].wait()
        acc_ref[tile % 2] = dot(x_buf[pl.ds(tile * ROWS, ROWS), :], w_ref[...])
        finish(tile - 1)
    finish(tiles - 1)


def projection_scratch(rows):
    return [
        pltpu.VMEM((D * 8, 128), BF16),
        pltpu.VMEM((rows, D), BF16),
        pltpu.VMEM((D, 1024), BF16),
        pltpu.VMEM((2, D * 8 // CHUNKS, 128), F32),
        pltpu.VMEM((2, ROWS, 1024), F32),
        pltpu.SemaphoreType.DMA((CHUNKS,)),
        pltpu.SemaphoreType.DMA((rows // ROWS,)),
    ]


def projections_kernel(r_hbm, gain_ref, x_hbm, k_hbm, vt_hbm, q_hbm, gg_hbm, sr_ref, tot_ref, *scratch):
    *shared, k_buf, vt_buf, q_buf, gg_buf, u_ref, out_sem = scratch
    acc_ref = shared[4]
    copies = []

    def finish(tile):
        rows = pl.ds(tile * ROWS, ROWS)
        keys = acc_ref[tile % 2, :, 0:256].astype(BF16)
        k_buf[rows, :] = keys
        vt = acc_ref[tile % 2, :, 256:512].T.astype(BF16)
        vt_buf[:, rows] = vt
        q_buf[rows, :] = acc_ref[tile % 2, :, 512:768].astype(BF16)
        g = acc_ref[tile % 2, :, 768:1024]
        gg_buf[rows, :] = (gain_ref[...] * (g / (1.0 + jnp.exp(-g)))).astype(BF16)
        for place, (source, target) in enumerate(
            (
                (k_buf.at[rows], k_hbm.at[rows]),
                (vt_buf.at[:, rows], vt_hbm.at[:, rows]),
                (q_buf.at[rows], q_hbm.at[rows]),
                (gg_buf.at[rows], gg_hbm.at[rows]),
            )
        ):
            copy = pltpu.make_async_copy(source, target, out_sem.at[tile, place])
            copy.start()
            copies.append(copy)
        for sub in range(ROWS // TILE):
            at = slice(sub * TILE, (sub + 1) * TILE)
            u = dot(vt[:, at], keys[at])
            for head in range(2):
                lanes = slice(head * 128, (head + 1) * 128)
                u_ref[tile * (ROWS // TILE) + sub, head] = u[lanes, lanes]

    project_tiles(r_hbm, x_hbm, *shared, finish)
    u01 = u_ref[0] + u_ref[1]
    u03 = u01 + (u_ref[2] + u_ref[3])
    u45 = u_ref[4] + u_ref[5]
    for at, tile in enumerate((0, 2, 4, 6)):
        sr_ref[at] = u_ref[tile].astype(BF16)
    sr_ref[4] = u01.astype(BF16)
    sr_ref[5] = u45.astype(BF16)
    sr_ref[6] = u03.astype(BF16)
    tot_ref[...] = (u03 + (u45 + (u_ref[6] + u_ref[7]))).astype(BF16)
    for copy in copies:
        copy.wait()


def projections(r, gain, tokens):
    rows = tokens.shape[0]
    anywhere = pl.BlockSpec(memory_space=pl.ANY)
    return pl.pallas_call(
        projections_kernel,
        grid=(1,),
        in_specs=[anywhere, full((1, 256), 1), anywhere],
        out_specs=[anywhere] * 4 + [full((7, 2, 128, 128), 1), full((2, 128, 128), 1)],
        out_shape=[
            jax.ShapeDtypeStruct((rows, 256), BF16),
            jax.ShapeDtypeStruct((256, rows), BF16),
            jax.ShapeDtypeStruct((rows, 256), BF16),
            jax.ShapeDtypeStruct((rows, 256), BF16),
            jax.ShapeDtypeStruct((7, 2, 128, 128), BF16),
            jax.ShapeDtypeStruct((2, 128, 128), BF16),
        ],
        scratch_shapes=projection_scratch(rows)
        + [
            pltpu.VMEM((rows, 256), BF16),
            pltpu.VMEM((256, rows), BF16),
            pltpu.VMEM((rows, 256), BF16),
            pltpu.VMEM((rows, 256), BF16),
            pltpu.VMEM((8, 2, 128, 128), F32),
            pltpu.SemaphoreType.DMA((rows // ROWS, 4)),
        ],
        compiler_params=pltpu.CompilerParams(vmem_limit_bytes=VMEM_LIMIT),
        cost_estimate=cost(2 * rows * D * 1024, 18 * MIB),
        name="projections",
    )(r, gain, tokens)


def level_scale(span):
    return 1.0 / (128.0 * math.sqrt(HEAD_DIM * span))


def local_kernel(start, q_ref, k_ref, vt_ref, codes_ref, sr_ref, *rest):
    out_ref = rest[-1]
    subs = q_ref.shape[0] // TILE
    s = lax.broadcasted_iota(jnp.int32, (TILE, TILE), 0)
    t = lax.broadcasted_iota(jnp.int32, (TILE, TILE), 1)
    gap = (t >> 6) - (s >> 6)
    inside = (gap == 0) & (s <= t)
    odd = (gap == 1) & ((t >> 6) & 1 == 1)
    second = ((t >> 7) - (s >> 7) == 1)
    for sub in range(subs):
        tile = start + sub
        at = slice(sub * TILE, (sub + 1) * TILE)
        flags = [float((tile >> bit) & 1) for bit in range(3)]
        reads = (tile >> 1, 4 + (tile >> 2), 6)
        for head in range(2):
            lanes = slice(head * 128, (head + 1) * 128)

            def row(level, span, head=head, at=at):
                return codes_ref[level, head : head + 1, at].astype(F32) * level_scale(span)

            left = jnp.concatenate(
                [k_ref[at, lanes]] + [sr_ref[r, head] for r, flag in zip(reads, flags) if flag], axis=0
            )
            product = dot_nt(left, q_ref[at, lanes])
            weight = jnp.where(
                inside,
                row(0, STRETCH),
                jnp.where(
                    odd, row(1, STRETCH), jnp.where(second, row(2, 2 * STRETCH), 0.0)
                ),
            )
            masked = (product[:TILE] * weight).astype(BF16)
            total = dot(vt_ref[lanes, at], masked)
            levels = [j for j in range(3) if flags[j]]
            for place, j in enumerate(levels):
                rows = slice(TILE + place * 128, TILE + (place + 1) * 128)
                total += row(3 + j, TILE << j) * product[rows]
            out_ref[lanes, at] = total.astype(BF16)


def local_levels(part, query, keys, vt, codes, sr, *earlier):
    rows = query.shape[0]
    return pl.pallas_call(
        lambda *refs: local_kernel(part * (ROWS // TILE), *refs),
        grid=(1,),
        in_specs=[
            pl.BlockSpec((ROWS, 256), lambda i: (part, 0), pipeline_mode=pl.Buffered(1)),
            pl.BlockSpec((ROWS, 256), lambda i: (part, 0), pipeline_mode=pl.Buffered(1)),
            pl.BlockSpec((256, ROWS), lambda i: (0, part), pipeline_mode=pl.Buffered(1)),
            pl.BlockSpec((11, 2, ROWS), lambda i: (0, 0, part), pipeline_mode=pl.Buffered(1)),
            full(sr.shape, 1),
        ]
        + [pl.BlockSpec(memory_space=pl.ANY)] * len(earlier),
        out_specs=pl.BlockSpec((256, ROWS), lambda i: (0, part), pipeline_mode=pl.Buffered(1)),
        out_shape=jax.ShapeDtypeStruct((256, rows), BF16),
        input_output_aliases={5: 0} if earlier else {},
        compiler_params=pltpu.CompilerParams(vmem_limit_bytes=VMEM_LIMIT),
        cost_estimate=cost(3e9, 2 * MIB),
        name=f"local_levels_{part}",
    )(query, keys, vt, codes, sr, *earlier)


def attend_kernel(rows_here, at_ref, q_ref, m_ref, gg_ref, codes_ref, *refs):
    *read_refs, out_ref, sd_ref = refs
    position = at_ref[0]

    @pl.when(pl.program_id(0) == 0)
    def _():
        for j, read_ref in enumerate(read_refs):
            for head in range(2):
                sd_ref[head, pl.ds(j * 128, 128), :] = read_ref[head]

    for head in range(2):
        lanes = slice(head * 128, (head + 1) * 128)
        product = dot_nt(sd_ref[head], q_ref[:, lanes])
        memory = m_ref[lanes, :].astype(F32)
        for j in range(5):
            scale = ((position >> j) & 1).astype(F32) * level_scale(rows_here << j)
            row = codes_ref[6 + j, head : head + 1, :].astype(F32) * scale
            memory += row * product[j * 128 : (j + 1) * 128]
        mean = jnp.mean(memory * memory, axis=0, keepdims=True)
        normed = memory * lax.rsqrt(mean + 1e-06)
        out_ref[:, lanes] = (normed.T * gg_ref[:, lanes].astype(F32)).astype(BF16)


def attend(position, query, local, gg, codes, reads):
    rows = query.shape[0]
    tile = 512
    return pl.pallas_call(
        lambda *refs: attend_kernel(rows, *refs),
        grid=(rows // tile,),
        in_specs=[
            pl.BlockSpec(memory_space=pltpu.SMEM),
            pl.BlockSpec((tile, 256), lambda i: (i, 0)),
            pl.BlockSpec((256, tile), lambda i: (0, i)),
            pl.BlockSpec((tile, 256), lambda i: (i, 0)),
            pl.BlockSpec((11, 2, tile), lambda i: (0, 0, i)),
        ]
        + [full(read.shape, 1) for read in reads],
        out_specs=pl.BlockSpec((tile, 256), lambda i: (i, 0)),
        out_shape=jax.ShapeDtypeStruct((rows, 256), BF16),
        scratch_shapes=[pltpu.VMEM((2, 640, 128), BF16)],
        compiler_params=pltpu.CompilerParams(vmem_limit_bytes=VMEM_LIMIT),
        cost_estimate=cost(3e9, 6 * MIB),
        name="attend",
    )(position, query, local, gg, codes, *reads)


def project_kernel(at_ref, a_ref, *refs):
    pieces, (out_ref, buf, acc_ref, sem) = refs[:-4], refs[-4:]
    x, core = at_ref[0] >> 1, at_ref[0] & 1
    copies = [pltpu.make_async_copy(piece, buf.at[p], sem.at[p]) for p, piece in enumerate(pieces)]
    for copy in copies:
        copy.start()
    half = len(pieces) // 2
    for p in range(half):
        blocks, weights = [], []
        for flip in range(2):
            copies[p + flip * half].wait()
            blocks.append(a_ref[((x + (0, 3, 1, 2)[p]) & 3) * 2 + (core ^ flip)])
            weights.append(buf[p + flip * half])
        term = dot(jnp.concatenate(blocks, axis=1), jnp.concatenate(weights, axis=0))
        if p == 0:
            acc_ref[...] = term
        elif p < half - 1:
            acc_ref[...] += term
        else:
            out_ref[...] = (acc_ref[...] + term).astype(BF16)


def project(place, attended, pieces):
    rows = attended.shape[1]
    return pl.pallas_call(
        project_kernel,
        grid=(1,),
        in_specs=[pl.BlockSpec(memory_space=pltpu.SMEM), full(attended.shape, 1)]
        + [pl.BlockSpec(memory_space=pl.ANY)] * len(pieces),
        out_specs=full((rows, D), 1),
        out_shape=jax.ShapeDtypeStruct((rows, D), BF16),
        scratch_shapes=[
            pltpu.VMEM((len(pieces), 256, D), BF16),
            pltpu.VMEM((rows, D), F32),
            pltpu.SemaphoreType.DMA((len(pieces),)),
        ],
        compiler_params=pltpu.CompilerParams(vmem_limit_bytes=20 * MIB),
        cost_estimate=cost(2 * 256 * 2048 * 2048, 10 * MIB),
        name="project",
    )(place, attended, *pieces)


def body(tokens, w_proj, gain, level_codes, w_codes, block_exponent):
    place = lax.axis_index("mp").reshape(1)
    position = lax.axis_index("seq").reshape(1)

    def along_x(block, by):
        return lax.ppermute(block, "mp", [(m, (m // 2 + by) % 4 * 2 + m % 2) for m in range(8)])

    def other_core(block):
        return lax.ppermute(block, "mp", [(m, m ^ 1) for m in range(8)])

    def along_seq(block, to, senders=32):
        return lax.ppermute(block.astype(BF16), "seq", [(i, to(i)) for i in range(senders)])

    after = lax.optimization_barrier
    r = w_proj.reshape(D, 4, 2, 128).transpose(0, 2, 1, 3).reshape(D * 8, 128)

    weight = decode_weight(w_codes, block_exponent)
    gain, weight = after((gain, weight))
    from_left, from_right, from_far = along_x(weight, 1), along_x(weight, -1), along_x(weight, 2)
    weight_other = other_core(weight)
    keys, vt, query, gg, sr, state = projections(r, gain.reshape(1, 256), tokens)

    def inside(part, *earlier):
        return local_levels(part, query, keys, vt, level_codes, sr, *earlier)

    local, sums, reads = (), state.astype(F32), []
    for bit in range(4):
        read = along_seq(sums, lambda i: i ^ (1 << bit))
        local = (inside(bit, *local),)
        read, local = after((read, local))
        sums = sums + read.astype(F32)
        reads.append(read)
    reads.append(along_seq(sums, lambda i: 28 - i // 4 * 4 + i % 4, 16))
    attended = attend(position, query, *local, gg, level_codes, reads)
    attended, from_left, from_right, from_far = after((attended, from_left, from_right, from_far))
    attended = lax.all_to_all(attended.reshape(8, 256, 256), "mp", 0, 0, tiled=True)
    pieces = (weight, from_left, from_right, from_far, weight_other)
    pieces += (other_core(from_left), other_core(from_right), other_core(from_far))
    return project(place, attended, pieces)


def solution(mesh):
    placed = (
        P("seq", None),
        P(None, None, "mp"),
        P("mp"),
        P(None, "mp", "seq"),
        P("mp", None),
        P("mp", None),
    )
    return jax.shard_map(
        body, mesh=mesh, in_specs=placed, out_specs=P(("seq", "mp"), None), check_vma=False
    )
```

time: 96.4 us -> 88.8 us (0.921)
  local copies, waits for them, and re-layouts: 4.61 us -> 0.64 us
  other arithmetic: 3.63 us -> 0.14 us
  starting transfers between devices: 32.2 us -> 29.4 us
  waiting for transfers between devices: 12.5 us -> 15.1 us
    convert_element_type x4, other arithmetic: 3.02 us -> 0.14 us  [along_seq(): block.astype(BF16)]
    slice x2 -> x0, local copies, waits for them, and re-layouts: 2.81 us -> none  [the longest x1 1.87 us: body(): far_low = along_x(from_right[128:], -1)]
    all_to_all x1, waiting for transfers between devices: 12.4 us -> 15.1 us  [body(): lax.all_to_all(attended.reshape(8, 256, 256), 'mp', 0, 0, tiled=True)]
    ppermute x7 -> x5, starting transfers between devices: 16.6 us -> 14.7 us  [along_seq(): lax.ppermute(block.astype(BF16), 'seq', [(i, to(i)) for i in range(sender...]
    pallas_call x4 -> x7, Pallas kernels: 36.8 us -> 37.6 us  [the longest x1 16.6 us: projections(): pl.pallas_call(projections_kernel, grid=(1,), in_specs=[anywhere, full((1...]
    ppermute x5 -> x4, starting transfers between devices: 6.65 us -> 6.11 us  [other_core(): return lax.ppermute(block, 'mp', [(m, m ^ 1) for m in range(8)])]
    ppermute x4 -> x3, starting transfers between devices: 5.43 us -> 5.04 us  [along_x(): lax.ppermute(block, 'mp', [(m, (m // 2 + by) % 4 * 2 + m % 2) for m in ra...]
  transfers between devices with their start and end apart: 17 -> 13, of which waited for: 1 -> 1; matrix products, arithmetic and copies ran while one was open for 7% -> 0% of each run, Pallas kernels for 25% -> 39%
where the time goes in v2:
time: 88.8 us; the launch traced here: 88.5 us
  Pallas kernels  42.9 us (48%)
  starting transfers between devices  29.4 us (33%)
  waiting for transfers between devices  15.1 us (17%)
    pallas_call x1, Pallas kernels, projections(): pl.pallas_call(projections_kernel, grid=(1,), in_specs=[anywhere, full((1...  16.6 us
    all_to_all x1, waiting for transfers between devices, body(): lax.all_to_all(attended.reshape(8, 256, 256), 'mp', 0, 0, tiled=True)  15.1 us
    ppermute x5, starting transfers between devices, along_seq(): lax.ppermute(block.astype(BF16), 'seq', [(i, to(i)) for i in range(sender...  14.7 us
    pallas_call x4, Pallas kernels, local_levels(): pl.pallas_call(lambda *refs: local_kernel(part * (ROWS // TILE), *refs),...  12.4 us
    ppermute x4, starting transfers between devices, other_core(): return lax.ppermute(block, 'mp', [(m, m ^ 1) for m in range(8)])  6.11 us
    pallas_call x1, Pallas kernels, project(): pl.pallas_call(project_kernel, grid=(1,), in_specs=[pl.BlockSpec(memory_s...  5.75 us
    pallas_call x1, Pallas kernels, attend(): pl.pallas_call(lambda *refs: attend_kernel(rows, *refs), grid=(rows // ti...  5.32 us
    ppermute x3, starting transfers between devices, along_x(): lax.ppermute(block, 'mp', [(m, (m // 2 + by) % 4 * 2 + m % 2) for m in ra...  5.04 us
  transfers between devices with their start and end apart: 13, of which 1 were waited for; matrix products, arithmetic and copies ran while one was open for 0% of the time, Pallas kernels for 39%

profile of v2, /device:TPU:1, one launch (start us, length us, event | category | flops | bytes accessed | tf_op | source)
XLA Modules:
  0.0 88.5 jit_solution(3681618826547881645)
XLA Ops:
  0.0 2.9 %decode_weight.1.refs_0_ = bf16[256,2048]{1,0:T(8,128)(2,1)} custom-call(s32[2,16]{1,0:T(2,128)} %exponent_ref.1, s32[256,2048]{1,0:T(8,128)} %codes_ref.1), custom_call_target="tpu_custom_call" | custom-call | flops 8000000 | bytes 3145728 | tf_op jit(solution)/shard_map/decode_weight/pallas_call | solution.py:55
  2.9 2.0 %collective-permute-start.5 = (bf16[256,2048]{1,0:T(8,128)(2,1)}, bf16[256,2048]{1,0:T(8,128)(2,1)S(1)}, u32[]{:S(2)}, u32[]{:S(2)}) collective-permute-start(bf16[256,2048]{1,0:T(8,128)(2,1)} %decode_weight.1.refs_0_), channel_id=1, source_target_pairs={{0,2},{1,3},{2,4},{3,5},{4,6},{5,7},{6,0},{7,1},{8,10},{9,11},{10,... | collective-permute-start | bytes 3145736 | tf_op jit(solution)/shard_map/ppermute | solution.py:373
  4.9 1.3 %collective-permute-start.6 = (bf16[256,2048]{1,0:T(8,128)(2,1)}, bf16[256,2048]{1,0:T(8,128)(2,1)}, u32[]{:S(2)}, u32[]{:S(2)}) collective-permute-start(bf16[256,2048]{1,0:T(8,128)(2,1)} %decode_weight.1.refs_0_), channel_id=1, source_target_pairs={{0,6},{1,7},{2,0},{3,1},{4,2},{5,3},{6,4},{7,5},{8,14},{9,15},{10,... | collective-permute-start | bytes 3145736 | tf_op jit(solution)/shard_map/ppermute | solution.py:373
  6.2 1.7 %collective-permute-start.7 = (bf16[256,2048]{1,0:T(8,128)(2,1)}, bf16[256,2048]{1,0:T(8,128)(2,1)}, u32[]{:S(2)}, u32[]{:S(2)}) collective-permute-start(bf16[256,2048]{1,0:T(8,128)(2,1)} %decode_weight.1.refs_0_), channel_id=1, source_target_pairs={{0,4},{1,5},{2,6},{3,7},{4,0},{5,1},{6,2},{7,3},{8,12},{9,13},{10,... | collective-permute-start | bytes 3145736 | tf_op jit(solution)/shard_map/ppermute | solution.py:373
  7.9 16.6 %projections.1 = (bf16[2048,256]{1,0:T(8,128)(2,1)}, bf16[256,2048]{1,0:T(8,128)(2,1)}, bf16[2048,256]{1,0:T(8,128)(2,1)}, bf16[2048,256]{1,0:T(8,128)(2,1)}, bf...) custom-call(bf16[16384,128]{1,0:T(8,128)(2,1)} %bitcast.10, f32[1,256]{1,0:T(1,128)} %bitcast.11, ...), custom_call_target="tpu_custom_call" | custom-call | flops 8589934592 | bytes 18874368 | tf_op jit(solution)/shard_map/projections/pallas_call | solution.py:186
  24.5 1.6 %collective-permute-start = (bf16[2,128,128]{2,1,0:T(8,128)(2,1)}, bf16[2,128,128]{2,1,0:T(8,128)(2,1)S(1)}, u32[]{:S(2)}, u32[]{:S(2)}) collective-permute-start(bf16[2,128,128]{2,1,0:T(8,128)(2,1)} %get-tuple-element.27), channel_id=1, source_target_pairs={{0,8},{8,0},{16,24},{24,16},{32,40},{40,32},{48,56},{56,48},{64,72... | collective-permute-start | bytes 196616 | tf_op jit(solution)/shard_map/ppermute | solution.py:379
  26.1 0.0 copy-start.2
  26.1 3.1 %local_levels_0.1.refs_5_ = bf16[256,2048]{1,0:T(8,128)(2,1)} custom-call(bf16[2048,256]{1,0:T(8,128)(2,1)} %get-tuple-element.26.refs_0_.refs_1_, bf16[2048,256]{1,0:T(8,128)(2,1)} %get-tuple-element.28.refs_1_, bf16[256,2048]{1,0:T(8,128)(2,1)} %get-tuple-element.29.refs_2_, s32[11,2,2048]{2,1,0:T(2,128)} %refs_4_.1, ...), custom_call_target="tpu_custom_call" | custom-call | flops 3000000000 | bytes 2097152 | tf_op jit(solution)/shard_map/local_levels_0/pallas_call | solution.py:260
  29.2 0.0 collective-permute-done.refs_5_
  29.2 0.0 copy-done.2
  29.2 0.0 copy-start.1
  29.3 2.7 %collective-permute-start.1 = (bf16[2,128,128]{2,1,0:T(8,128)(2,1)S(1)}, bf16[2,128,128]{2,1,0:T(8,128)(2,1)S(1)}, u32[]{:S(2)}, u32[]{:S(2)}) collective-permute-start(bf16[2,128,128]{2,1,0:T(8,128)(2,1)S(1)} %fusion), channel_id=1, source_target_pairs={{0,16},{8,24},{16,0},{24,8},{32,48},{40,56},{48,32},{56,40},{64,80... | collective-permute-start | bytes 196616 | tf_op jit(solution)/shard_map/ppermute | solution.py:379
  32.0 3.1 %local_levels_1.1.refs_5_ = bf16[256,2048]{1,0:T(8,128)(2,1)} custom-call(bf16[2048,256]{1,0:T(8,128)(2,1)} %get-tuple-element.26.refs_0_.refs_1_, bf16[2048,256]{1,0:T(8,128)(2,1)} %get-tuple-element.28.refs_1_, bf16[256,2048]{1,0:T(8,128)(2,1)} %get-tuple-element.29.refs_2_, s32[11,2,2048]{2,1,0:T(2,128)} %refs_4_.1, ...), custom_call_target="tpu_custom_call", output_to_operand_aliasing={{}: (5, {})} | custom-call | flops 3000000000 | bytes 2097152 | tf_op jit(solution)/shard_map/local_levels_1/pallas_call | solution.py:260
  35.0 0.0 collective-permute-done.1.refs_6_
  35.0 0.0 copy-start.3
  35.1 1.7 %collective-permute-start.2 = (bf16[2,128,128]{2,1,0:T(8,128)(2,1)S(1)}, bf16[2,128,128]{2,1,0:T(8,128)(2,1)S(1)}, u32[]{:S(2)}, u32[]{:S(2)}) collective-permute-start(bf16[2,128,128]{2,1,0:T(8,128)(2,1)S(1)} %fusion.2), channel_id=1, source_target_pairs={{0,32},{8,40},{16,48},{24,56},{32,0},{40,8},{48,16},{56,24},{64,96... | collective-permute-start | bytes 196616 | tf_op jit(solution)/shard_map/ppermute | solution.py:379
  36.8 3.1 %local_levels_2.1.refs_5_ = bf16[256,2048]{1,0:T(8,128)(2,1)} custom-call(bf16[2048,256]{1,0:T(8,128)(2,1)} %get-tuple-element.26.refs_0_.refs_1_, bf16[2048,256]{1,0:T(8,128)(2,1)} %get-tuple-element.28.refs_1_, bf16[256,2048]{1,0:T(8,128)(2,1)} %get-tuple-element.29.refs_2_, s32[11,2,2048]{2,1,0:T(2,128)} %refs_4_.1, ...), custom_call_target="tpu_custom_call", output_to_operand_aliasing={{}: (5, {})} | custom-call | flops 3000000000 | bytes 2097152 | tf_op jit(solution)/shard_map/local_levels_2/pallas_call | solution.py:260
  39.9 0.0 collective-permute-done.2.refs_7_
  39.9 0.0 copy-start.4
  39.9 0.0 copy-start
  39.9 3.1 %collective-permute-start.3 = (bf16[2,128,128]{2,1,0:T(8,128)(2,1)S(1)}, bf16[2,128,128]{2,1,0:T(8,128)(2,1)S(1)}, u32[]{:S(2)}, u32[]{:S(2)}) collective-permute-start(bf16[2,128,128]{2,1,0:T(8,128)(2,1)S(1)} %fusion.1), channel_id=1, source_target_pairs={{0,64},{8,72},{16,80},{24,88},{32,96},{40,104},{48,112},{56,120},{... | collective-permute-start | bytes 196616 | tf_op jit(solution)/shard_map/ppermute | solution.py:379
  43.0 3.1 %local_levels_3.1.refs_2_ = bf16[256,2048]{1,0:T(8,128)(2,1)} custom-call(bf16[2048,256]{1,0:T(8,128)(2,1)} %get-tuple-element.26.refs_0_.refs_1_, bf16[2048,256]{1,0:T(8,128)(2,1)} %get-tuple-element.28.refs_1_, bf16[256,2048]{1,0:T(8,128)(2,1)} %get-tuple-element.29.refs_2_, s32[11,2,2048]{2,1,0:T(2,128)} %refs_4_.1, ...), custom_call_target="tpu_custom_call", output_to_operand_aliasing={{}: (5, {})} | custom-call | flops 3000000000 | bytes 2097152 | tf_op jit(solution)/shard_map/local_levels_3/pallas_call | solution.py:260
  46.1 0.0 collective-permute-done.3.refs_8_
  46.1 0.0 copy-done.1
  46.1 0.0 copy-done.3
  46.1 0.0 copy-done.4
  46.1 0.0 copy-start.5
  46.1 0.1 add_convert_fusion
  46.2 5.6 %collective-permute-start.4 = (bf16[2,128,128]{2,1,0:T(8,128)(2,1)S(1)}, bf16[2,128,128]{2,1,0:T(8,128)(2,1)S(1)}, u32[]{:S(2)}, u32[]{:S(2)}) collective-permute-start(bf16[2,128,128]{2,1,0:T(8,128)(2,1)S(1)} %add_convert_fusion), channel_id=1, source_target_pairs={{0,224},{8,232},{16,240},{24,248},{32,192},{40,200},{48,208},{56,2... | collective-permute-start | bytes 196616 | tf_op jit(solution)/shard_map/ppermute | solution.py:379
  51.8 0.0 copy-done
  51.8 3.7 %collective-permute-start.8 = (bf16[256,2048]{1,0:T(8,128)(2,1)S(1)}, bf16[256,2048]{1,0:T(8,128)(2,1)}, u32[]{:S(2)}, u32[]{:S(2)}) collective-permute-start(bf16[256,2048]{1,0:T(8,128)(2,1)S(1)} %copy-done), channel_id=1, source_target_pairs={{0,1},{1,0},{2,3},{3,2},{4,5},{5,4},{6,7},{7,6},{8,9},{9,8},{10,11... | collective-permute-start | bytes 3145736 | tf_op jit(solution)/shard_map/ppermute | solution.py:376
  55.5 0.0 collective-permute-done.4.refs_9_
  55.5 0.0 copy-start.6
  55.5 0.0 copy-done.5
  55.5 0.6 copy-done.6
  56.1 5.3 %attend.1 = bf16[2048,256]{1,0:T(8,128)(2,1)} custom-call(s32[1]{0:T(128)} %bitcast.1.refs_0_, bf16[2048,256]{1,0:T(8,128)(2,1)} %get-tuple-element.26.refs_0_.refs_1_, bf16[256,2048]{1,0:T(8,128)(2,1)} %local_levels_3.1.refs_2_, bf16[2048,256]{1,0:T(8,128)(2,1)} %get-tuple-element.38.refs_3_, s32[11,2,2048]{2,1,0:T(2,128)} %refs_4_.1, ...), custom_call_target="tpu_custom_call" | custom-call | flops 3000000000 | bytes 6291456 | tf_op jit(solution)/shard_map/attend/pallas_call | solution.py:306
  61.4 0.0 collective-permute-done.5.refs_1_
  61.5 0.0 collective-permute-done.6.refs_2_
  61.5 0.0 collective-permute-done.7.refs_3_
  61.5 1.9 %collective-permute-start.10 = (bf16[256,2048]{1,0:T(8,128)(2,1)}, bf16[256,2048]{1,0:T(8,128)(2,1)}, u32[]{:S(2)}, u32[]{:S(2)}) collective-permute-start(bf16[256,2048]{1,0:T(8,128)(2,1)} %collective-permute-done.6.refs_2_), channel_id=1, source_target_pairs={{0,1},{1,0},{2,3},{3,2},{4,5},{5,4},{6,7},{7,6},{8,9},{9,8},{10,11... | collective-permute-start | bytes 3145736 | tf_op jit(solution)/shard_map/ppermute | solution.py:376
  63.3 0.1 collective-permute-start.11
  63.5 0.4 collective-permute-start.9
  63.9 3.6 %all-to-all-start = ((bf16[8,256,256]{2,1,0:T(8,128)(2,1)}), bf16[8,256,256]{2,1,0:T(8,128)(2,1)S(1)}, u32[]{:S(2)}, u32[]{:S(2)}) async-start(bf16[8,256,256]{2,1,0:T(8,128)(2,1)} %bitcast.9), calls=%async_computation | async-start | bytes 2097152 | tf_op jit(solution)/shard_map/all_to_all | solution.py:403
  67.4 0.0 collective-permute-done.8.refs_4_
  67.4 15.1 %all-to-all-done.a_ref = bf16[8,256,256]{2,1,0:T(8,128)(2,1)S(1)} async-done(((bf16[8,256,256]{2,1,0:T(8,128)(2,1)}), bf16[8,256,256]{2,1,0:T(8,128)(2,1)S(1)}, u32[]{:S(2)}, u32[]{:S(2)}) %all-to-all-start) | async-done | bytes 1048608 | tf_op jit(solution)/shard_map/all_to_all | solution.py:403
  82.5 0.0 collective-permute-done.10.refs_6_
  82.5 0.0 collective-permute-done.11.refs_7_
  82.5 0.0 collective-permute-done.9.refs_5_
  82.6 5.7 %project.1 = bf16[256,2048]{1,0:T(8,128)(2,1)} custom-call(s32[1]{0:T(128)} %bitcast.at_ref, bf16[8,256,256]{2,1,0:T(8,128)(2,1)S(1)} %all-to-all-done.a_ref, bf16[256,2048]{1,0:T(8,128)(2,1)S(1)} %copy-done, bf16[256,2048]{1,0:T(8,128)(2,1)S(1)} %collective-permute-done.5.refs_1_, bf16[256,2048]{1,0:T(8,128)(2,1)} %collective-permute-done.6.refs_2_, ...), custom_call_target="tpu_custom_call" | custom-call | flops 2147483648 | bytes 10485760 | tf_op jit(solution)/shard_map/project/pallas_call | solution.py:350
  (3 shorter events, 0.1 us)
Async XLA Ops:
  2.9 58.6 %collective-permute-start.5 = (bf16[256,2048]{1,0:T(8,128)(2,1)}, bf16[256,2048]{1,0:T(8,128)(2,1)S(1)}, u32[]{:S(2)}, u32[]{:S(2)}) collective-permute-start(bf16[256,2048]{1,0:T(8,128)(2,1)} %decode_weight.1.refs_0_), channel_id=1, source_target_pairs={{0,2},{1,3},{2,4},{3,5},{4,6},{5,7},{6,0},{7,1},{8,10},{9,11},{10,... | collective-permute-start | bytes 3145736 | tf_op jit(solution)/shard_map/ppermute | solution.py:373
  4.9 56.6 %collective-permute-start.6 = (bf16[256,2048]{1,0:T(8,128)(2,1)}, bf16[256,2048]{1,0:T(8,128)(2,1)}, u32[]{:S(2)}, u32[]{:S(2)}) collective-permute-start(bf16[256,2048]{1,0:T(8,128)(2,1)} %decode_weight.1.refs_0_), channel_id=1, source_target_pairs={{0,6},{1,7},{2,0},{3,1},{4,2},{5,3},{6,4},{7,5},{8,14},{9,15},{10,... | collective-permute-start | bytes 3145736 | tf_op jit(solution)/shard_map/ppermute | solution.py:373
  6.2 55.3 %collective-permute-start.7 = (bf16[256,2048]{1,0:T(8,128)(2,1)}, bf16[256,2048]{1,0:T(8,128)(2,1)}, u32[]{:S(2)}, u32[]{:S(2)}) collective-permute-start(bf16[256,2048]{1,0:T(8,128)(2,1)} %decode_weight.1.refs_0_), channel_id=1, source_target_pairs={{0,4},{1,5},{2,6},{3,7},{4,0},{5,1},{6,2},{7,3},{8,12},{9,13},{10,... | collective-permute-start | bytes 3145736 | tf_op jit(solution)/shard_map/ppermute | solution.py:373
  24.5 4.7 %collective-permute-start = (bf16[2,128,128]{2,1,0:T(8,128)(2,1)}, bf16[2,128,128]{2,1,0:T(8,128)(2,1)S(1)}, u32[]{:S(2)}, u32[]{:S(2)}) collective-permute-start(bf16[2,128,128]{2,1,0:T(8,128)(2,1)} %get-tuple-element.27), channel_id=1, source_target_pairs={{0,8},{8,0},{16,24},{24,16},{32,40},{40,32},{48,56},{56,48},{64,72... | collective-permute-start | bytes 196616 | tf_op jit(solution)/shard_map/ppermute | solution.py:379
  26.1 3.1 %copy-start.2 = (bf16[2,128,128]{2,1,0:T(8,128)(2,1)S(1)}, bf16[2,128,128]{2,1,0:T(8,128)(2,1)}, u32[]{:S(2)}) copy-start(bf16[2,128,128]{2,1,0:T(8,128)(2,1)} %get-tuple-element.27) | copy-start | bytes 196612
  29.2 16.9 %copy-start.1 = (bf16[2,128,128]{2,1,0:T(8,128)(2,1)}, bf16[2,128,128]{2,1,0:T(8,128)(2,1)S(1)}, u32[]{:S(2)}) copy-start(bf16[2,128,128]{2,1,0:T(8,128)(2,1)S(1)} %collective-permute-done.refs_5_) | copy-start | bytes 196612
  29.3 5.8 %collective-permute-start.1 = (bf16[2,128,128]{2,1,0:T(8,128)(2,1)S(1)}, bf16[2,128,128]{2,1,0:T(8,128)(2,1)S(1)}, u32[]{:S(2)}, u32[]{:S(2)}) collective-permute-start(bf16[2,128,128]{2,1,0:T(8,128)(2,1)S(1)} %fusion), channel_id=1, source_target_pairs={{0,16},{8,24},{16,0},{24,8},{32,48},{40,56},{48,32},{56,40},{64,80... | collective-permute-start | bytes 196616 | tf_op jit(solution)/shard_map/ppermute | solution.py:379
  35.0 11.1 %copy-start.3 = (bf16[2,128,128]{2,1,0:T(8,128)(2,1)}, bf16[2,128,128]{2,1,0:T(8,128)(2,1)S(1)}, u32[]{:S(2)}) copy-start(bf16[2,128,128]{2,1,0:T(8,128)(2,1)S(1)} %collective-permute-done.1.refs_6_) | copy-start | bytes 196612
  35.1 4.8 %collective-permute-start.2 = (bf16[2,128,128]{2,1,0:T(8,128)(2,1)S(1)}, bf16[2,128,128]{2,1,0:T(8,128)(2,1)S(1)}, u32[]{:S(2)}, u32[]{:S(2)}) collective-permute-start(bf16[2,128,128]{2,1,0:T(8,128)(2,1)S(1)} %fusion.2), channel_id=1, source_target_pairs={{0,32},{8,40},{16,48},{24,56},{32,0},{40,8},{48,16},{56,24},{64,96... | collective-permute-start | bytes 196616 | tf_op jit(solution)/shard_map/ppermute | solution.py:379
  39.9 6.3 %copy-start.4 = (bf16[2,128,128]{2,1,0:T(8,128)(2,1)}, bf16[2,128,128]{2,1,0:T(8,128)(2,1)S(1)}, u32[]{:S(2)}) copy-start(bf16[2,128,128]{2,1,0:T(8,128)(2,1)S(1)} %collective-permute-done.2.refs_7_) | copy-start | bytes 196612
  39.9 11.9 %copy-start = (bf16[256,2048]{1,0:T(8,128)(2,1)S(1)}, bf16[256,2048]{1,0:T(8,128)(2,1)}, u32[]{:S(2)}) copy-start(bf16[256,2048]{1,0:T(8,128)(2,1)} %decode_weight.1.refs_0_) | copy-start | bytes 3145732
  39.9 6.2 %collective-permute-start.3 = (bf16[2,128,128]{2,1,0:T(8,128)(2,1)S(1)}, bf16[2,128,128]{2,1,0:T(8,128)(2,1)S(1)}, u32[]{:S(2)}, u32[]{:S(2)}) collective-permute-start(bf16[2,128,128]{2,1,0:T(8,128)(2,1)S(1)} %fusion.1), channel_id=1, source_target_pairs={{0,64},{8,72},{16,80},{24,88},{32,96},{40,104},{48,112},{56,120},{... | collective-permute-start | bytes 196616 | tf_op jit(solution)/shard_map/ppermute | solution.py:379
  46.1 9.4 %copy-start.5 = (bf16[2,128,128]{2,1,0:T(8,128)(2,1)}, bf16[2,128,128]{2,1,0:T(8,128)(2,1)S(1)}, u32[]{:S(2)}) copy-start(bf16[2,128,128]{2,1,0:T(8,128)(2,1)S(1)} %collective-permute-done.3.refs_8_) | copy-start | bytes 196612
  46.2 9.3 %collective-permute-start.4 = (bf16[2,128,128]{2,1,0:T(8,128)(2,1)S(1)}, bf16[2,128,128]{2,1,0:T(8,128)(2,1)S(1)}, u32[]{:S(2)}, u32[]{:S(2)}) collective-permute-start(bf16[2,128,128]{2,1,0:T(8,128)(2,1)S(1)} %add_convert_fusion), channel_id=1, source_target_pairs={{0,224},{8,232},{16,240},{24,248},{32,192},{40,200},{48,208},{56,2... | collective-permute-start | bytes 196616 | tf_op jit(solution)/shard_map/ppermute | solution.py:379
  51.8 15.6 %collective-permute-start.8 = (bf16[256,2048]{1,0:T(8,128)(2,1)S(1)}, bf16[256,2048]{1,0:T(8,128)(2,1)}, u32[]{:S(2)}, u32[]{:S(2)}) collective-permute-start(bf16[256,2048]{1,0:T(8,128)(2,1)S(1)} %copy-done), channel_id=1, source_target_pairs={{0,1},{1,0},{2,3},{3,2},{4,5},{5,4},{6,7},{7,6},{8,9},{9,8},{10,11... | collective-permute-start | bytes 3145736 | tf_op jit(solution)/shard_map/ppermute | solution.py:376
  55.5 0.6 copy-start.6
  61.5 21.1 %collective-permute-start.10 = (bf16[256,2048]{1,0:T(8,128)(2,1)}, bf16[256,2048]{1,0:T(8,128)(2,1)}, u32[]{:S(2)}, u32[]{:S(2)}) collective-permute-start(bf16[256,2048]{1,0:T(8,128)(2,1)} %collective-permute-done.6.refs_2_), channel_id=1, source_target_pairs={{0,1},{1,0},{2,3},{3,2},{4,5},{5,4},{6,7},{7,6},{8,9},{9,8},{10,11... | collective-permute-start | bytes 3145736 | tf_op jit(solution)/shard_map/ppermute | solution.py:376
  63.3 19.2 %collective-permute-start.11 = (bf16[256,2048]{1,0:T(8,128)(2,1)}, bf16[256,2048]{1,0:T(8,128)(2,1)}, u32[]{:S(2)}, u32[]{:S(2)}) collective-permute-start(bf16[256,2048]{1,0:T(8,128)(2,1)} %collective-permute-done.7.refs_3_), channel_id=1, source_target_pairs={{0,1},{1,0},{2,3},{3,2},{4,5},{5,4},{6,7},{7,6},{8,9},{9,8},{10,11... | collective-permute-start | bytes 3145736 | tf_op jit(solution)/shard_map/ppermute | solution.py:376
  63.5 19.1 %collective-permute-start.9 = (bf16[256,2048]{1,0:T(8,128)(2,1)S(1)}, bf16[256,2048]{1,0:T(8,128)(2,1)}, u32[]{:S(2)}, u32[]{:S(2)}) collective-permute-start(bf16[256,2048]{1,0:T(8,128)(2,1)S(1)} %collective-permute-done.5.refs_1_), channel_id=1, source_target_pairs={{0,1},{1,0},{2,3},{3,2},{4,5},{5,4},{6,7},{7,6},{8,9},{9,8},{10,11... | collective-permute-start | bytes 3145736 | tf_op jit(solution)/shard_map/ppermute | solution.py:376
  63.9 18.7 %all-to-all-start = ((bf16[8,256,256]{2,1,0:T(8,128)(2,1)}), bf16[8,256,256]{2,1,0:T(8,128)(2,1)S(1)}, u32[]{:S(2)}, u32[]{:S(2)}) async-start(bf16[8,256,256]{2,1,0:T(8,128)(2,1)} %bitcast.9), calls=%async_computation | async-start | bytes 2097152 | tf_op jit(solution)/shard_map/all_to_all | solution.py:403

commit v3 on v2

--- a/solution.py
+++ b/solution.py
@@ -104,17 +104,18 @@
         r_copies[chunk].wait()
         unpack_chunk(chunk, PARTS, r_buf, w_ref, f_ref)
     x_copies[0].wait()
-    for chunk in range(CHUNKS):
-        if chunk + 2 < CHUNKS:
-            r_copies[chunk + 2].wait()
-        at = pl.ds(chunk * deep, deep)
+    for chunk in range(0, CHUNKS, 2):
+        later = range(chunk + 2, min(chunk + 4, CHUNKS))
+        for ahead in later:
+            r_copies[ahead].wait()
+        at = pl.ds(chunk * deep, 2 * deep)
         term = dot(x_buf[pl.ds(0, ROWS), at], w_ref[at, :])
         if chunk == 0:
             acc_ref[0] = term
         else:
             acc_ref[0] += term
-        if chunk + 2 < CHUNKS:
-            unpack_chunk(chunk + 2, PARTS, r_buf, w_ref, f_ref)
+        for ahead in later:
+            unpack_chunk(ahead, PARTS, r_buf, w_ref, f_ref)
     for tile in range(1, tiles):
         x_copies[tile].wait()
         acc_ref[tile % 2] = dot(x_buf[pl.ds(tile * ROWS, ROWS), :], w_ref[...])
@@ -302,7 +303,7 @@
 
 def attend(position, query, local, gg, codes, reads):
     rows = query.shape[0]
-    tile = 512
+    tile = 1024
     return pl.pallas_call(
         lambda *refs: attend_kernel(rows, *refs),
         grid=(rows // tile,),
@@ -384,7 +385,6 @@
     weight = decode_weight(w_codes, block_exponent)
     gain, weight = after((gain, weight))
     from_left, from_right, from_far = along_x(weight, 1), along_x(weight, -1), along_x(weight, 2)
-    weight_other = other_core(weight)
     keys, vt, query, gg, sr, state = projections(r, gain.reshape(1, 256), tokens)
 
     def inside(part, *earlier):
@@ -399,11 +399,9 @@
         reads.append(read)
     reads.append(along_seq(sums, lambda i: 28 - i // 4 * 4 + i % 4, 16))
     attended = attend(position, query, *local, gg, level_codes, reads)
-    attended, from_left, from_right, from_far = after((attended, from_left, from_right, from_far))
+    attended, *pieces = after((attended, weight, from_left, from_right, from_far))
     attended = lax.all_to_all(attended.reshape(8, 256, 256), "mp", 0, 0, tiled=True)
-    pieces = (weight, from_left, from_right, from_far, weight_other)
-    pieces += (other_core(from_left), other_core(from_right), other_core(from_far))
-    return project(place, attended, pieces)
+    return project(place, attended, pieces + [other_core(piece) for piece in pieces])
 
 
 def solution(mesh):

time: 88.8 us -> 88.2 us (level)
  waiting for transfers between devices: 15.1 us -> 16.5 us
  Pallas kernels: 42.9 us -> 41.9 us
  starting transfers between devices: 29.4 us -> 28.5 us
    ppermute x5, waiting for transfers between devices: 0.01 us -> 1.32 us  [along_seq(): lax.ppermute(block.astype(BF16), 'seq', [(i, to(i)) for i in range(sender...]
    ppermute x4, starting transfers between devices: 6.11 us -> 4.91 us  [other_core(): return lax.ppermute(block, 'mp', [(m, m ^ 1) for m in range(8)])]
  transfers between devices with their start and end apart: 13 -> 13, of which waited for: 1 -> 2; matrix products, arithmetic and copies ran while one was open for 0% -> 0% of each run, Pallas kernels for 39% -> 38%
where the time goes in v3:
time: 88.2 us; the launch traced here: 87.9 us
  Pallas kernels  41.9 us (48%)
  starting transfers between devices  28.5 us (32%)
  waiting for transfers between devices  16.5 us (19%)
    pallas_call x1, Pallas kernels, projections(): pl.pallas_call(projections_kernel, grid=(1,), in_specs=[anywhere, full((1...  16.3 us
    all_to_all x1, waiting for transfers between devices, body(): lax.all_to_all(attended.reshape(8, 256, 256), 'mp', 0, 0, tiled=True)  15.1 us
    ppermute x5, starting transfers between devices, along_seq(): lax.ppermute(block.astype(BF16), 'seq', [(i, to(i)) for i in range(sender...  14.7 us
    pallas_call x4, Pallas kernels, local_levels(): pl.pallas_call(lambda *refs: local_kernel(part * (ROWS // TILE), *refs),...  12.4 us
    pallas_call x1, Pallas kernels, project(): pl.pallas_call(project_kernel, grid=(1,), in_specs=[pl.BlockSpec(memory_s...  5.75 us
    ppermute x3, starting transfers between devices, along_x(): lax.ppermute(block, 'mp', [(m, (m // 2 + by) % 4 * 2 + m % 2) for m in ra...  5.04 us
    ppermute x4, starting transfers between devices, other_core(): return lax.ppermute(block, 'mp', [(m, m ^ 1) for m in range(8)])  4.91 us
    pallas_call x1, Pallas kernels, attend(): pl.pallas_call(lambda *refs: attend_kernel(rows, *refs), grid=(rows // ti...  4.6 us
  transfers between devices with their start and end apart: 13, of which 2 were waited for; matrix products, arithmetic and copies ran while one was open for 0% of the time, Pallas kernels for 38%

profile of v3, /device:TPU:1, one launch (start us, length us, event | category | flops | bytes accessed | tf_op | source)
XLA Modules:
  0.0 87.9 jit_solution(11209170844428738929)
XLA Ops:
  0.0 2.9 %decode_weight.1.refs_0_ = bf16[256,2048]{1,0:T(8,128)(2,1)} custom-call(s32[2,16]{1,0:T(2,128)} %exponent_ref.1, s32[256,2048]{1,0:T(8,128)} %codes_ref.1), custom_call_target="tpu_custom_call" | custom-call | flops 8000000 | bytes 3145728 | tf_op jit(solution)/shard_map/decode_weight/pallas_call | solution.py:55
  2.9 2.0 %collective-permute-start.5 = (bf16[256,2048]{1,0:T(8,128)(2,1)}, bf16[256,2048]{1,0:T(8,128)(2,1)S(1)}, u32[]{:S(2)}, u32[]{:S(2)}) collective-permute-start(bf16[256,2048]{1,0:T(8,128)(2,1)} %decode_weight.1.refs_0_), channel_id=1, source_target_pairs={{0,2},{1,3},{2,4},{3,5},{4,6},{5,7},{6,0},{7,1},{8,10},{9,11},{10,... | collective-permute-start | bytes 3145736 | tf_op jit(solution)/shard_map/ppermute | solution.py:374
  4.9 1.3 %collective-permute-start.6 = (bf16[256,2048]{1,0:T(8,128)(2,1)}, bf16[256,2048]{1,0:T(8,128)(2,1)}, u32[]{:S(2)}, u32[]{:S(2)}) collective-permute-start(bf16[256,2048]{1,0:T(8,128)(2,1)} %decode_weight.1.refs_0_), channel_id=1, source_target_pairs={{0,6},{1,7},{2,0},{3,1},{4,2},{5,3},{6,4},{7,5},{8,14},{9,15},{10,... | collective-permute-start | bytes 3145736 | tf_op jit(solution)/shard_map/ppermute | solution.py:374
  6.2 1.7 %collective-permute-start.7 = (bf16[256,2048]{1,0:T(8,128)(2,1)}, bf16[256,2048]{1,0:T(8,128)(2,1)}, u32[]{:S(2)}, u32[]{:S(2)}) collective-permute-start(bf16[256,2048]{1,0:T(8,128)(2,1)} %decode_weight.1.refs_0_), channel_id=1, source_target_pairs={{0,4},{1,5},{2,6},{3,7},{4,0},{5,1},{6,2},{7,3},{8,12},{9,13},{10,... | collective-permute-start | bytes 3145736 | tf_op jit(solution)/shard_map/ppermute | solution.py:374
  7.9 16.3 %projections.1 = (bf16[2048,256]{1,0:T(8,128)(2,1)}, bf16[256,2048]{1,0:T(8,128)(2,1)}, bf16[2048,256]{1,0:T(8,128)(2,1)}, bf16[2048,256]{1,0:T(8,128)(2,1)}, bf...) custom-call(bf16[16384,128]{1,0:T(8,128)(2,1)} %bitcast.10, f32[1,256]{1,0:T(1,128)} %bitcast.11, ...), custom_call_target="tpu_custom_call" | custom-call | flops 8589934592 | bytes 18874368 | tf_op jit(solution)/shard_map/projections/pallas_call | solution.py:187
  24.2 1.6 %collective-permute-start = (bf16[2,128,128]{2,1,0:T(8,128)(2,1)}, bf16[2,128,128]{2,1,0:T(8,128)(2,1)S(1)}, u32[]{:S(2)}, u32[]{:S(2)}) collective-permute-start(bf16[2,128,128]{2,1,0:T(8,128)(2,1)} %get-tuple-element.28), channel_id=1, source_target_pairs={{0,8},{8,0},{16,24},{24,16},{32,40},{40,32},{48,56},{56,48},{64,72... | collective-permute-start | bytes 196616 | tf_op jit(solution)/shard_map/ppermute | solution.py:380
  25.8 0.0 copy-start.2
  25.8 3.1 %local_levels_0.1.refs_5_ = bf16[256,2048]{1,0:T(8,128)(2,1)} custom-call(bf16[2048,256]{1,0:T(8,128)(2,1)} %get-tuple-element.27.refs_0_.refs_1_, bf16[2048,256]{1,0:T(8,128)(2,1)} %get-tuple-element.29.refs_1_, bf16[256,2048]{1,0:T(8,128)(2,1)} %get-tuple-element.30.refs_2_, s32[11,2,2048]{2,1,0:T(2,128)} %refs_4_.1, ...), custom_call_target="tpu_custom_call" | custom-call | flops 3000000000 | bytes 2097152 | tf_op jit(solution)/shard_map/local_levels_0/pallas_call | solution.py:261
  28.9 0.0 collective-permute-done.refs_5_
  28.9 0.0 copy-done.2
  28.9 0.0 copy-start.1
  28.9 2.7 %collective-permute-start.1 = (bf16[2,128,128]{2,1,0:T(8,128)(2,1)S(1)}, bf16[2,128,128]{2,1,0:T(8,128)(2,1)S(1)}, u32[]{:S(2)}, u32[]{:S(2)}) collective-permute-start(bf16[2,128,128]{2,1,0:T(8,128)(2,1)S(1)} %fusion), channel_id=1, source_target_pairs={{0,16},{8,24},{16,0},{24,8},{32,48},{40,56},{48,32},{56,40},{64,80... | collective-permute-start | bytes 196616 | tf_op jit(solution)/shard_map/ppermute | solution.py:380
  31.6 3.1 %local_levels_1.1.refs_5_ = bf16[256,2048]{1,0:T(8,128)(2,1)} custom-call(bf16[2048,256]{1,0:T(8,128)(2,1)} %get-tuple-element.27.refs_0_.refs_1_, bf16[2048,256]{1,0:T(8,128)(2,1)} %get-tuple-element.29.refs_1_, bf16[256,2048]{1,0:T(8,128)(2,1)} %get-tuple-element.30.refs_2_, s32[11,2,2048]{2,1,0:T(2,128)} %refs_4_.1, ...), custom_call_target="tpu_custom_call", output_to_operand_aliasing={{}: (5, {})} | custom-call | flops 3000000000 | bytes 2097152 | tf_op jit(solution)/shard_map/local_levels_1/pallas_call | solution.py:261
  34.7 0.0 collective-permute-done.1.refs_6_
  34.7 0.0 copy-start.3
  34.8 1.7 %collective-permute-start.2 = (bf16[2,128,128]{2,1,0:T(8,128)(2,1)S(1)}, bf16[2,128,128]{2,1,0:T(8,128)(2,1)S(1)}, u32[]{:S(2)}, u32[]{:S(2)}) collective-permute-start(bf16[2,128,128]{2,1,0:T(8,128)(2,1)S(1)} %fusion.2), channel_id=1, source_target_pairs={{0,32},{8,40},{16,48},{24,56},{32,0},{40,8},{48,16},{56,24},{64,96... | collective-permute-start | bytes 196616 | tf_op jit(solution)/shard_map/ppermute | solution.py:380
  36.5 3.1 %local_levels_2.1.refs_5_ = bf16[256,2048]{1,0:T(8,128)(2,1)} custom-call(bf16[2048,256]{1,0:T(8,128)(2,1)} %get-tuple-element.27.refs_0_.refs_1_, bf16[2048,256]{1,0:T(8,128)(2,1)} %get-tuple-element.29.refs_1_, bf16[256,2048]{1,0:T(8,128)(2,1)} %get-tuple-element.30.refs_2_, s32[11,2,2048]{2,1,0:T(2,128)} %refs_4_.1, ...), custom_call_target="tpu_custom_call", output_to_operand_aliasing={{}: (5, {})} | custom-call | flops 3000000000 | bytes 2097152 | tf_op jit(solution)/shard_map/local_levels_2/pallas_call | solution.py:261
  39.6 0.0 collective-permute-done.2.refs_7_
  39.6 0.0 copy-start.4
  39.6 3.1 %collective-permute-start.3 = (bf16[2,128,128]{2,1,0:T(8,128)(2,1)S(1)}, bf16[2,128,128]{2,1,0:T(8,128)(2,1)S(1)}, u32[]{:S(2)}, u32[]{:S(2)}) collective-permute-start(bf16[2,128,128]{2,1,0:T(8,128)(2,1)S(1)} %fusion.1), channel_id=1, source_target_pairs={{0,64},{8,72},{16,80},{24,88},{32,96},{40,104},{48,112},{56,120},{... | collective-permute-start | bytes 196616 | tf_op jit(solution)/shard_map/ppermute | solution.py:380
  42.7 3.1 %local_levels_3.1.refs_2_ = bf16[256,2048]{1,0:T(8,128)(2,1)} custom-call(bf16[2048,256]{1,0:T(8,128)(2,1)} %get-tuple-element.27.refs_0_.refs_1_, bf16[2048,256]{1,0:T(8,128)(2,1)} %get-tuple-element.29.refs_1_, bf16[256,2048]{1,0:T(8,128)(2,1)} %get-tuple-element.30.refs_2_, s32[11,2,2048]{2,1,0:T(2,128)} %refs_4_.1, ...), custom_call_target="tpu_custom_call", output_to_operand_aliasing={{}: (5, {})} | custom-call | flops 3000000000 | bytes 2097152 | tf_op jit(solution)/shard_map/local_levels_3/pallas_call | solution.py:261
  45.8 0.0 collective-permute-done.3.refs_8_
  45.8 0.0 copy-done.1
  45.8 0.0 copy-done.3
  45.8 0.0 copy-done.4
  45.8 0.0 copy-start.5
  45.8 0.1 add_convert_fusion
  45.9 5.6 %collective-permute-start.4 = (bf16[2,128,128]{2,1,0:T(8,128)(2,1)S(1)}, bf16[2,128,128]{2,1,0:T(8,128)(2,1)S(1)}, u32[]{:S(2)}, u32[]{:S(2)}) collective-permute-start(bf16[2,128,128]{2,1,0:T(8,128)(2,1)S(1)} %add_convert_fusion), channel_id=1, source_target_pairs={{0,224},{8,232},{16,240},{24,248},{32,192},{40,200},{48,208},{56,2... | collective-permute-start | bytes 196616 | tf_op jit(solution)/shard_map/ppermute | solution.py:380
  51.5 1.3 %collective-permute-done.4.refs_9_ = bf16[2,128,128]{2,1,0:T(8,128)(2,1)S(1)} collective-permute-done((bf16[2,128,128]{2,1,0:T(8,128)(2,1)S(1)}, bf16[2,128,128]{2,1,0:T(8,128)(2,1)S(1)}, u32[]{:S(2)}, u32[]{:S(2)}) %collective-permute-start.4) | collective-permute-done | bytes 65568 | tf_op jit(solution)/shard_map/ppermute | solution.py:380
  52.8 0.0 copy-start.6
  52.8 0.0 copy-done.5
  52.8 0.6 copy-done.6
  53.4 0.0 copy-start
  53.4 4.6 %attend.1 = bf16[2048,256]{1,0:T(8,128)(2,1)} custom-call(s32[1]{0:T(128)} %bitcast.1.refs_0_, bf16[2048,256]{1,0:T(8,128)(2,1)} %get-tuple-element.27.refs_0_.refs_1_, bf16[256,2048]{1,0:T(8,128)(2,1)} %local_levels_3.1.refs_2_, bf16[2048,256]{1,0:T(8,128)(2,1)} %get-tuple-element.39.refs_3_, s32[11,2,2048]{2,1,0:T(2,128)} %refs_4_.1, ...), custom_call_target="tpu_custom_call" | custom-call | flops 3000000000 | bytes 6291456 | tf_op jit(solution)/shard_map/attend/pallas_call | solution.py:307
  58.0 0.0 collective-permute-done.5.refs_1_
  58.0 0.0 collective-permute-done.6.refs_2_
  58.0 0.0 collective-permute-done.7.refs_3_
  58.0 0.0 copy-done
  58.0 4.3 %collective-permute-start.8 = (bf16[256,2048]{1,0:T(8,128)(2,1)S(1)}, bf16[256,2048]{1,0:T(8,128)(2,1)}, u32[]{:S(2)}, u32[]{:S(2)}) collective-permute-start(bf16[256,2048]{1,0:T(8,128)(2,1)S(1)} %copy-done), channel_id=1, source_target_pairs={{0,1},{1,0},{2,3},{3,2},{4,5},{5,4},{6,7},{7,6},{8,9},{9,8},{10,11... | collective-permute-start | bytes 3145736 | tf_op jit(solution)/shard_map/ppermute | solution.py:377
  62.3 0.1 collective-permute-start.9
  62.4 0.4 collective-permute-start.10
  62.8 0.1 collective-permute-start.11
  62.9 3.9 %all-to-all-start = ((bf16[8,256,256]{2,1,0:T(8,128)(2,1)}), bf16[8,256,256]{2,1,0:T(8,128)(2,1)S(1)}, u32[]{:S(2)}, u32[]{:S(2)}) async-start(bf16[8,256,256]{2,1,0:T(8,128)(2,1)} %bitcast.9), calls=%async_computation | async-start | bytes 2097152 | tf_op jit(solution)/shard_map/all_to_all | solution.py:403
  66.8 15.1 %all-to-all-done.a_ref = bf16[8,256,256]{2,1,0:T(8,128)(2,1)S(1)} async-done(((bf16[8,256,256]{2,1,0:T(8,128)(2,1)}), bf16[8,256,256]{2,1,0:T(8,128)(2,1)S(1)}, u32[]{:S(2)}, u32[]{:S(2)}) %all-to-all-start) | async-done | bytes 1048608 | tf_op jit(solution)/shard_map/all_to_all | solution.py:403
  81.9 0.0 collective-permute-done.8.refs_4_
  81.9 0.0 collective-permute-done.9.refs_5_
  81.9 0.0 collective-permute-done.10.refs_6_
  81.9 0.0 collective-permute-done.11.refs_7_
  81.9 5.7 %project.1 = bf16[256,2048]{1,0:T(8,128)(2,1)} custom-call(s32[1]{0:T(128)} %bitcast.at_ref, bf16[8,256,256]{2,1,0:T(8,128)(2,1)S(1)} %all-to-all-done.a_ref, bf16[256,2048]{1,0:T(8,128)(2,1)S(1)} %copy-done, bf16[256,2048]{1,0:T(8,128)(2,1)S(1)} %collective-permute-done.5.refs_1_, bf16[256,2048]{1,0:T(8,128)(2,1)} %collective-permute-done.6.refs_2_, ...), custom_call_target="tpu_custom_call" | custom-call | flops 2147483648 | bytes 10485760 | tf_op jit(solution)/shard_map/project/pallas_call | solution.py:351
  (3 shorter events, 0.1 us)
Async XLA Ops:
  2.9 55.1 %collective-permute-start.5 = (bf16[256,2048]{1,0:T(8,128)(2,1)}, bf16[256,2048]{1,0:T(8,128)(2,1)S(1)}, u32[]{:S(2)}, u32[]{:S(2)}) collective-permute-start(bf16[256,2048]{1,0:T(8,128)(2,1)} %decode_weight.1.refs_0_), channel_id=1, source_target_pairs={{0,2},{1,3},{2,4},{3,5},{4,6},{5,7},{6,0},{7,1},{8,10},{9,11},{10,... | collective-permute-start | bytes 3145736 | tf_op jit(solution)/shard_map/ppermute | solution.py:374
  4.9 53.1 %collective-permute-start.6 = (bf16[256,2048]{1,0:T(8,128)(2,1)}, bf16[256,2048]{1,0:T(8,128)(2,1)}, u32[]{:S(2)}, u32[]{:S(2)}) collective-permute-start(bf16[256,2048]{1,0:T(8,128)(2,1)} %decode_weight.1.refs_0_), channel_id=1, source_target_pairs={{0,6},{1,7},{2,0},{3,1},{4,2},{5,3},{6,4},{7,5},{8,14},{9,15},{10,... | collective-permute-start | bytes 3145736 | tf_op jit(solution)/shard_map/ppermute | solution.py:374
  6.2 51.8 %collective-permute-start.7 = (bf16[256,2048]{1,0:T(8,128)(2,1)}, bf16[256,2048]{1,0:T(8,128)(2,1)}, u32[]{:S(2)}, u32[]{:S(2)}) collective-permute-start(bf16[256,2048]{1,0:T(8,128)(2,1)} %decode_weight.1.refs_0_), channel_id=1, source_target_pairs={{0,4},{1,5},{2,6},{3,7},{4,0},{5,1},{6,2},{7,3},{8,12},{9,13},{10,... | collective-permute-start | bytes 3145736 | tf_op jit(solution)/shard_map/ppermute | solution.py:374
  24.2 4.7 %collective-permute-start = (bf16[2,128,128]{2,1,0:T(8,128)(2,1)}, bf16[2,128,128]{2,1,0:T(8,128)(2,1)S(1)}, u32[]{:S(2)}, u32[]{:S(2)}) collective-permute-start(bf16[2,128,128]{2,1,0:T(8,128)(2,1)} %get-tuple-element.28), channel_id=1, source_target_pairs={{0,8},{8,0},{16,24},{24,16},{32,40},{40,32},{48,56},{56,48},{64,72... | collective-permute-start | bytes 196616 | tf_op jit(solution)/shard_map/ppermute | solution.py:380
  25.8 3.1 %copy-start.2 = (bf16[2,128,128]{2,1,0:T(8,128)(2,1)S(1)}, bf16[2,128,128]{2,1,0:T(8,128)(2,1)}, u32[]{:S(2)}) copy-start(bf16[2,128,128]{2,1,0:T(8,128)(2,1)} %get-tuple-element.28) | copy-start | bytes 196612
  28.9 16.9 %copy-start.1 = (bf16[2,128,128]{2,1,0:T(8,128)(2,1)}, bf16[2,128,128]{2,1,0:T(8,128)(2,1)S(1)}, u32[]{:S(2)}) copy-start(bf16[2,128,128]{2,1,0:T(8,128)(2,1)S(1)} %collective-permute-done.refs_5_) | copy-start | bytes 196612
  28.9 5.8 %collective-permute-start.1 = (bf16[2,128,128]{2,1,0:T(8,128)(2,1)S(1)}, bf16[2,128,128]{2,1,0:T(8,128)(2,1)S(1)}, u32[]{:S(2)}, u32[]{:S(2)}) collective-permute-start(bf16[2,128,128]{2,1,0:T(8,128)(2,1)S(1)} %fusion), channel_id=1, source_target_pairs={{0,16},{8,24},{16,0},{24,8},{32,48},{40,56},{48,32},{56,40},{64,80... | collective-permute-start | bytes 196616 | tf_op jit(solution)/shard_map/ppermute | solution.py:380
  34.7 11.1 %copy-start.3 = (bf16[2,128,128]{2,1,0:T(8,128)(2,1)}, bf16[2,128,128]{2,1,0:T(8,128)(2,1)S(1)}, u32[]{:S(2)}) copy-start(bf16[2,128,128]{2,1,0:T(8,128)(2,1)S(1)} %collective-permute-done.1.refs_6_) | copy-start | bytes 196612
  34.8 4.8 %collective-permute-start.2 = (bf16[2,128,128]{2,1,0:T(8,128)(2,1)S(1)}, bf16[2,128,128]{2,1,0:T(8,128)(2,1)S(1)}, u32[]{:S(2)}, u32[]{:S(2)}) collective-permute-start(bf16[2,128,128]{2,1,0:T(8,128)(2,1)S(1)} %fusion.2), channel_id=1, source_target_pairs={{0,32},{8,40},{16,48},{24,56},{32,0},{40,8},{48,16},{56,24},{64,96... | collective-permute-start | bytes 196616 | tf_op jit(solution)/shard_map/ppermute | solution.py:380
  39.6 6.2 %copy-start.4 = (bf16[2,128,128]{2,1,0:T(8,128)(2,1)}, bf16[2,128,128]{2,1,0:T(8,128)(2,1)S(1)}, u32[]{:S(2)}) copy-start(bf16[2,128,128]{2,1,0:T(8,128)(2,1)S(1)} %collective-permute-done.2.refs_7_) | copy-start | bytes 196612
  39.6 6.2 %collective-permute-start.3 = (bf16[2,128,128]{2,1,0:T(8,128)(2,1)S(1)}, bf16[2,128,128]{2,1,0:T(8,128)(2,1)S(1)}, u32[]{:S(2)}, u32[]{:S(2)}) collective-permute-start(bf16[2,128,128]{2,1,0:T(8,128)(2,1)S(1)} %fusion.1), channel_id=1, source_target_pairs={{0,64},{8,72},{16,80},{24,88},{32,96},{40,104},{48,112},{56,120},{... | collective-permute-start | bytes 196616 | tf_op jit(solution)/shard_map/ppermute | solution.py:380
  45.8 7.0 %copy-start.5 = (bf16[2,128,128]{2,1,0:T(8,128)(2,1)}, bf16[2,128,128]{2,1,0:T(8,128)(2,1)S(1)}, u32[]{:S(2)}) copy-start(bf16[2,128,128]{2,1,0:T(8,128)(2,1)S(1)} %collective-permute-done.3.refs_8_) | copy-start | bytes 196612
  45.9 6.9 %collective-permute-start.4 = (bf16[2,128,128]{2,1,0:T(8,128)(2,1)S(1)}, bf16[2,128,128]{2,1,0:T(8,128)(2,1)S(1)}, u32[]{:S(2)}, u32[]{:S(2)}) collective-permute-start(bf16[2,128,128]{2,1,0:T(8,128)(2,1)S(1)} %add_convert_fusion), channel_id=1, source_target_pairs={{0,224},{8,232},{16,240},{24,248},{32,192},{40,200},{48,208},{56,2... | collective-permute-start | bytes 196616 | tf_op jit(solution)/shard_map/ppermute | solution.py:380
  52.8 0.6 copy-start.6
  53.4 4.6 %copy-start = (bf16[256,2048]{1,0:T(8,128)(2,1)S(1)}, bf16[256,2048]{1,0:T(8,128)(2,1)}, u32[]{:S(2)}) copy-start(bf16[256,2048]{1,0:T(8,128)(2,1)} %decode_weight.1.refs_0_) | copy-start | bytes 3145732
  58.0 23.9 %collective-permute-start.8 = (bf16[256,2048]{1,0:T(8,128)(2,1)S(1)}, bf16[256,2048]{1,0:T(8,128)(2,1)}, u32[]{:S(2)}, u32[]{:S(2)}) collective-permute-start(bf16[256,2048]{1,0:T(8,128)(2,1)S(1)} %copy-done), channel_id=1, source_target_pairs={{0,1},{1,0},{2,3},{3,2},{4,5},{5,4},{6,7},{7,6},{8,9},{9,8},{10,11... | collective-permute-start | bytes 3145736 | tf_op jit(solution)/shard_map/ppermute | solution.py:377
  62.3 19.6 %collective-permute-start.9 = (bf16[256,2048]{1,0:T(8,128)(2,1)S(1)}, bf16[256,2048]{1,0:T(8,128)(2,1)}, u32[]{:S(2)}, u32[]{:S(2)}) collective-permute-start(bf16[256,2048]{1,0:T(8,128)(2,1)S(1)} %collective-permute-done.5.refs_1_), channel_id=1, source_target_pairs={{0,1},{1,0},{2,3},{3,2},{4,5},{5,4},{6,7},{7,6},{8,9},{9,8},{10,11... | collective-permute-start | bytes 3145736 | tf_op jit(solution)/shard_map/ppermute | solution.py:377
  62.4 19.5 %collective-permute-start.10 = (bf16[256,2048]{1,0:T(8,128)(2,1)}, bf16[256,2048]{1,0:T(8,128)(2,1)}, u32[]{:S(2)}, u32[]{:S(2)}) collective-permute-start(bf16[256,2048]{1,0:T(8,128)(2,1)} %collective-permute-done.6.refs_2_), channel_id=1, source_target_pairs={{0,1},{1,0},{2,3},{3,2},{4,5},{5,4},{6,7},{7,6},{8,9},{9,8},{10,11... | collective-permute-start | bytes 3145736 | tf_op jit(solution)/shard_map/ppermute | solution.py:377
  62.8 19.1 %collective-permute-start.11 = (bf16[256,2048]{1,0:T(8,128)(2,1)}, bf16[256,2048]{1,0:T(8,128)(2,1)}, u32[]{:S(2)}, u32[]{:S(2)}) collective-permute-start(bf16[256,2048]{1,0:T(8,128)(2,1)} %collective-permute-done.7.refs_3_), channel_id=1, source_target_pairs={{0,1},{1,0},{2,3},{3,2},{4,5},{5,4},{6,7},{7,6},{8,9},{9,8},{10,11... | collective-permute-start | bytes 3145736 | tf_op jit(solution)/shard_map/ppermute | solution.py:377
  62.9 19.0 %all-to-all-start = ((bf16[8,256,256]{2,1,0:T(8,128)(2,1)}), bf16[8,256,256]{2,1,0:T(8,128)(2,1)S(1)}, u32[]{:S(2)}, u32[]{:S(2)}) async-start(bf16[8,256,256]{2,1,0:T(8,128)(2,1)} %bitcast.9), calls=%async_computation | async-start | bytes 2097152 | tf_op jit(solution)/shard_map/all_to_all | solution.py:403

commit v4 on v3

--- a/solution.py
+++ b/solution.py
@@ -328,9 +328,10 @@
     pieces, (out_ref, buf, acc_ref, sem) = refs[:-4], refs[-4:]
     x, core = at_ref[0] >> 1, at_ref[0] & 1
     copies = [pltpu.make_async_copy(piece, buf.at[p], sem.at[p]) for p, piece in enumerate(pieces)]
-    for copy in copies:
-        copy.start()
     half = len(pieces) // 2
+    for p in range(half):
+        copies[p].start()
+        copies[p + half].start()
     for p in range(half):
         blocks, weights = [], []
         for flip in range(2):

time: 88.2 us -> 87.5 us (level)
  no operation moved by 1% of the time
where the time goes in v4:
time: 87.5 us; the launch traced here: 87.1 us
  Pallas kernels  41.2 us (47%)
  starting transfers between devices  28.5 us (33%)
  waiting for transfers between devices  16.5 us (19%)
    pallas_call x1, Pallas kernels, projections(): pl.pallas_call(projections_kernel, grid=(1,), in_specs=[anywhere, full((1...  16.3 us
    all_to_all x1, waiting for transfers between devices, body(): lax.all_to_all(attended.reshape(8, 256, 256), 'mp', 0, 0, tiled=True)  15.1 us
    ppermute x5, starting transfers between devices, along_seq(): lax.ppermute(block.astype(BF16), 'seq', [(i, to(i)) for i in range(sender...  14.7 us
    pallas_call x4, Pallas kernels, local_levels(): pl.pallas_call(lambda *refs: local_kernel(part * (ROWS // TILE), *refs),...  12.4 us
    pallas_call x1, Pallas kernels, project(): pl.pallas_call(project_kernel, grid=(1,), in_specs=[pl.BlockSpec(memory_s...  5.04 us
    ppermute x3, starting transfers between devices, along_x(): lax.ppermute(block, 'mp', [(m, (m // 2 + by) % 4 * 2 + m % 2) for m in ra...  5.04 us
    ppermute x4, starting transfers between devices, other_core(): return lax.ppermute(block, 'mp', [(m, m ^ 1) for m in range(8)])  4.91 us
    pallas_call x1, Pallas kernels, attend(): pl.pallas_call(lambda *refs: attend_kernel(rows, *refs), grid=(rows // ti...  4.6 us
  transfers between devices with their start and end apart: 13, of which 2 were waited for; matrix products, arithmetic and copies ran while one was open for 0% of the time, Pallas kernels for 38%

profile of v4, /device:TPU:1, one launch (start us, length us, event | category | flops | bytes accessed | tf_op | source)
XLA Modules:
  0.0 87.1 jit_solution(8135994283229934429)
XLA Ops:
  0.0 2.9 %decode_weight.1.refs_0_ = bf16[256,2048]{1,0:T(8,128)(2,1)} custom-call(s32[2,16]{1,0:T(2,128)} %exponent_ref.1, s32[256,2048]{1,0:T(8,128)} %codes_ref.1), custom_call_target="tpu_custom_call" | custom-call | flops 8000000 | bytes 3145728 | tf_op jit(solution)/shard_map/decode_weight/pallas_call | solution.py:55
  2.9 2.0 %collective-permute-start.5 = (bf16[256,2048]{1,0:T(8,128)(2,1)}, bf16[256,2048]{1,0:T(8,128)(2,1)S(1)}, u32[]{:S(2)}, u32[]{:S(2)}) collective-permute-start(bf16[256,2048]{1,0:T(8,128)(2,1)} %decode_weight.1.refs_0_), channel_id=1, source_target_pairs={{0,2},{1,3},{2,4},{3,5},{4,6},{5,7},{6,0},{7,1},{8,10},{9,11},{10,... | collective-permute-start | bytes 3145736 | tf_op jit(solution)/shard_map/ppermute | solution.py:375
  4.9 1.3 %collective-permute-start.6 = (bf16[256,2048]{1,0:T(8,128)(2,1)}, bf16[256,2048]{1,0:T(8,128)(2,1)}, u32[]{:S(2)}, u32[]{:S(2)}) collective-permute-start(bf16[256,2048]{1,0:T(8,128)(2,1)} %decode_weight.1.refs_0_), channel_id=1, source_target_pairs={{0,6},{1,7},{2,0},{3,1},{4,2},{5,3},{6,4},{7,5},{8,14},{9,15},{10,... | collective-permute-start | bytes 3145736 | tf_op jit(solution)/shard_map/ppermute | solution.py:375
  6.2 1.7 %collective-permute-start.7 = (bf16[256,2048]{1,0:T(8,128)(2,1)}, bf16[256,2048]{1,0:T(8,128)(2,1)}, u32[]{:S(2)}, u32[]{:S(2)}) collective-permute-start(bf16[256,2048]{1,0:T(8,128)(2,1)} %decode_weight.1.refs_0_), channel_id=1, source_target_pairs={{0,4},{1,5},{2,6},{3,7},{4,0},{5,1},{6,2},{7,3},{8,12},{9,13},{10,... | collective-permute-start | bytes 3145736 | tf_op jit(solution)/shard_map/ppermute | solution.py:375
  7.9 16.3 %projections.1 = (bf16[2048,256]{1,0:T(8,128)(2,1)}, bf16[256,2048]{1,0:T(8,128)(2,1)}, bf16[2048,256]{1,0:T(8,128)(2,1)}, bf16[2048,256]{1,0:T(8,128)(2,1)}, bf...) custom-call(bf16[16384,128]{1,0:T(8,128)(2,1)} %bitcast.10, f32[1,256]{1,0:T(1,128)} %bitcast.11, ...), custom_call_target="tpu_custom_call" | custom-call | flops 8589934592 | bytes 18874368 | tf_op jit(solution)/shard_map/projections/pallas_call | solution.py:187
  24.2 1.6 %collective-permute-start = (bf16[2,128,128]{2,1,0:T(8,128)(2,1)}, bf16[2,128,128]{2,1,0:T(8,128)(2,1)S(1)}, u32[]{:S(2)}, u32[]{:S(2)}) collective-permute-start(bf16[2,128,128]{2,1,0:T(8,128)(2,1)} %get-tuple-element.28), channel_id=1, source_target_pairs={{0,8},{8,0},{16,24},{24,16},{32,40},{40,32},{48,56},{56,48},{64,72... | collective-permute-start | bytes 196616 | tf_op jit(solution)/shard_map/ppermute | solution.py:381
  25.8 0.0 copy-start.2
  25.8 3.1 %local_levels_0.1.refs_5_ = bf16[256,2048]{1,0:T(8,128)(2,1)} custom-call(bf16[2048,256]{1,0:T(8,128)(2,1)} %get-tuple-element.27.refs_0_.refs_1_, bf16[2048,256]{1,0:T(8,128)(2,1)} %get-tuple-element.29.refs_1_, bf16[256,2048]{1,0:T(8,128)(2,1)} %get-tuple-element.30.refs_2_, s32[11,2,2048]{2,1,0:T(2,128)} %refs_4_.1, ...), custom_call_target="tpu_custom_call" | custom-call | flops 3000000000 | bytes 2097152 | tf_op jit(solution)/shard_map/local_levels_0/pallas_call | solution.py:261
  28.9 0.0 collective-permute-done.refs_5_
  28.9 0.0 copy-done.2
  28.9 0.0 copy-start.1
  28.9 2.7 %collective-permute-start.1 = (bf16[2,128,128]{2,1,0:T(8,128)(2,1)S(1)}, bf16[2,128,128]{2,1,0:T(8,128)(2,1)S(1)}, u32[]{:S(2)}, u32[]{:S(2)}) collective-permute-start(bf16[2,128,128]{2,1,0:T(8,128)(2,1)S(1)} %fusion), channel_id=1, source_target_pairs={{0,16},{8,24},{16,0},{24,8},{32,48},{40,56},{48,32},{56,40},{64,80... | collective-permute-start | bytes 196616 | tf_op jit(solution)/shard_map/ppermute | solution.py:381
  31.6 3.1 %local_levels_1.1.refs_5_ = bf16[256,2048]{1,0:T(8,128)(2,1)} custom-call(bf16[2048,256]{1,0:T(8,128)(2,1)} %get-tuple-element.27.refs_0_.refs_1_, bf16[2048,256]{1,0:T(8,128)(2,1)} %get-tuple-element.29.refs_1_, bf16[256,2048]{1,0:T(8,128)(2,1)} %get-tuple-element.30.refs_2_, s32[11,2,2048]{2,1,0:T(2,128)} %refs_4_.1, ...), custom_call_target="tpu_custom_call", output_to_operand_aliasing={{}: (5, {})} | custom-call | flops 3000000000 | bytes 2097152 | tf_op jit(solution)/shard_map/local_levels_1/pallas_call | solution.py:261
  34.7 0.0 collective-permute-done.1.refs_6_
  34.7 0.0 copy-start.3
  34.8 1.7 %collective-permute-start.2 = (bf16[2,128,128]{2,1,0:T(8,128)(2,1)S(1)}, bf16[2,128,128]{2,1,0:T(8,128)(2,1)S(1)}, u32[]{:S(2)}, u32[]{:S(2)}) collective-permute-start(bf16[2,128,128]{2,1,0:T(8,128)(2,1)S(1)} %fusion.2), channel_id=1, source_target_pairs={{0,32},{8,40},{16,48},{24,56},{32,0},{40,8},{48,16},{56,24},{64,96... | collective-permute-start | bytes 196616 | tf_op jit(solution)/shard_map/ppermute | solution.py:381
  36.5 3.1 %local_levels_2.1.refs_5_ = bf16[256,2048]{1,0:T(8,128)(2,1)} custom-call(bf16[2048,256]{1,0:T(8,128)(2,1)} %get-tuple-element.27.refs_0_.refs_1_, bf16[2048,256]{1,0:T(8,128)(2,1)} %get-tuple-element.29.refs_1_, bf16[256,2048]{1,0:T(8,128)(2,1)} %get-tuple-element.30.refs_2_, s32[11,2,2048]{2,1,0:T(2,128)} %refs_4_.1, ...), custom_call_target="tpu_custom_call", output_to_operand_aliasing={{}: (5, {})} | custom-call | flops 3000000000 | bytes 2097152 | tf_op jit(solution)/shard_map/local_levels_2/pallas_call | solution.py:261
  39.6 0.0 collective-permute-done.2.refs_7_
  39.6 0.0 copy-start.4
  39.6 3.1 %collective-permute-start.3 = (bf16[2,128,128]{2,1,0:T(8,128)(2,1)S(1)}, bf16[2,128,128]{2,1,0:T(8,128)(2,1)S(1)}, u32[]{:S(2)}, u32[]{:S(2)}) collective-permute-start(bf16[2,128,128]{2,1,0:T(8,128)(2,1)S(1)} %fusion.1), channel_id=1, source_target_pairs={{0,64},{8,72},{16,80},{24,88},{32,96},{40,104},{48,112},{56,120},{... | collective-permute-start | bytes 196616 | tf_op jit(solution)/shard_map/ppermute | solution.py:381
  42.7 3.1 %local_levels_3.1.refs_2_ = bf16[256,2048]{1,0:T(8,128)(2,1)} custom-call(bf16[2048,256]{1,0:T(8,128)(2,1)} %get-tuple-element.27.refs_0_.refs_1_, bf16[2048,256]{1,0:T(8,128)(2,1)} %get-tuple-element.29.refs_1_, bf16[256,2048]{1,0:T(8,128)(2,1)} %get-tuple-element.30.refs_2_, s32[11,2,2048]{2,1,0:T(2,128)} %refs_4_.1, ...), custom_call_target="tpu_custom_call", output_to_operand_aliasing={{}: (5, {})} | custom-call | flops 3000000000 | bytes 2097152 | tf_op jit(solution)/shard_map/local_levels_3/pallas_call | solution.py:261
  45.8 0.0 collective-permute-done.3.refs_8_
  45.8 0.0 copy-done.1
  45.8 0.0 copy-done.3
  45.8 0.0 copy-done.4
  45.8 0.0 copy-start.5
  45.8 0.1 add_convert_fusion
  45.9 5.6 %collective-permute-start.4 = (bf16[2,128,128]{2,1,0:T(8,128)(2,1)S(1)}, bf16[2,128,128]{2,1,0:T(8,128)(2,1)S(1)}, u32[]{:S(2)}, u32[]{:S(2)}) collective-permute-start(bf16[2,128,128]{2,1,0:T(8,128)(2,1)S(1)} %add_convert_fusion), channel_id=1, source_target_pairs={{0,224},{8,232},{16,240},{24,248},{32,192},{40,200},{48,208},{56,2... | collective-permute-start | bytes 196616 | tf_op jit(solution)/shard_map/ppermute | solution.py:381
  51.5 1.3 %collective-permute-done.4.refs_9_ = bf16[2,128,128]{2,1,0:T(8,128)(2,1)S(1)} collective-permute-done((bf16[2,128,128]{2,1,0:T(8,128)(2,1)S(1)}, bf16[2,128,128]{2,1,0:T(8,128)(2,1)S(1)}, u32[]{:S(2)}, u32[]{:S(2)}) %collective-permute-start.4) | collective-permute-done | bytes 65568 | tf_op jit(solution)/shard_map/ppermute | solution.py:381
  52.8 0.0 copy-start.6
  52.8 0.0 copy-done.5
  52.8 0.6 copy-done.6
  53.4 0.0 copy-start
  53.4 4.6 %attend.1 = bf16[2048,256]{1,0:T(8,128)(2,1)} custom-call(s32[1]{0:T(128)} %bitcast.1.refs_0_, bf16[2048,256]{1,0:T(8,128)(2,1)} %get-tuple-element.27.refs_0_.refs_1_, bf16[256,2048]{1,0:T(8,128)(2,1)} %local_levels_3.1.refs_2_, bf16[2048,256]{1,0:T(8,128)(2,1)} %get-tuple-element.39.refs_3_, s32[11,2,2048]{2,1,0:T(2,128)} %refs_4_.1, ...), custom_call_target="tpu_custom_call" | custom-call | flops 3000000000 | bytes 6291456 | tf_op jit(solution)/shard_map/attend/pallas_call | solution.py:307
  58.0 0.0 collective-permute-done.5.refs_1_
  58.0 0.0 collective-permute-done.6.refs_2_
  58.0 0.0 collective-permute-done.7.refs_3_
  58.0 0.0 copy-done
  58.0 4.3 %collective-permute-start.8 = (bf16[256,2048]{1,0:T(8,128)(2,1)S(1)}, bf16[256,2048]{1,0:T(8,128)(2,1)}, u32[]{:S(2)}, u32[]{:S(2)}) collective-permute-start(bf16[256,2048]{1,0:T(8,128)(2,1)S(1)} %copy-done), channel_id=1, source_target_pairs={{0,1},{1,0},{2,3},{3,2},{4,5},{5,4},{6,7},{7,6},{8,9},{9,8},{10,11... | collective-permute-start | bytes 3145736 | tf_op jit(solution)/shard_map/ppermute | solution.py:378
  62.3 0.1 collective-permute-start.9
  62.4 0.4 collective-permute-start.10
  62.8 0.1 collective-permute-start.11
  62.9 3.9 %all-to-all-start = ((bf16[8,256,256]{2,1,0:T(8,128)(2,1)}), bf16[8,256,256]{2,1,0:T(8,128)(2,1)S(1)}, u32[]{:S(2)}, u32[]{:S(2)}) async-start(bf16[8,256,256]{2,1,0:T(8,128)(2,1)} %bitcast.9), calls=%async_computation | async-start | bytes 2097152 | tf_op jit(solution)/shard_map/all_to_all | solution.py:404
  66.8 15.1 %all-to-all-done.a_ref = bf16[8,256,256]{2,1,0:T(8,128)(2,1)S(1)} async-done(((bf16[8,256,256]{2,1,0:T(8,128)(2,1)}), bf16[8,256,256]{2,1,0:T(8,128)(2,1)S(1)}, u32[]{:S(2)}, u32[]{:S(2)}) %all-to-all-start) | async-done | bytes 1048608 | tf_op jit(solution)/shard_map/all_to_all | solution.py:404
  81.9 0.0 collective-permute-done.8.refs_4_
  81.9 0.0 collective-permute-done.9.refs_5_
  81.9 0.0 collective-permute-done.10.refs_6_
  81.9 0.0 collective-permute-done.11.refs_7_
  81.9 5.0 %project.1 = bf16[256,2048]{1,0:T(8,128)(2,1)} custom-call(s32[1]{0:T(128)} %bitcast.at_ref, bf16[8,256,256]{2,1,0:T(8,128)(2,1)S(1)} %all-to-all-done.a_ref, bf16[256,2048]{1,0:T(8,128)(2,1)S(1)} %copy-done, bf16[256,2048]{1,0:T(8,128)(2,1)S(1)} %collective-permute-done.5.refs_1_, bf16[256,2048]{1,0:T(8,128)(2,1)} %collective-permute-done.6.refs_2_, ...), custom_call_target="tpu_custom_call" | custom-call | flops 2147483648 | bytes 10485760 | tf_op jit(solution)/shard_map/project/pallas_call | solution.py:352
  (3 shorter events, 0.1 us)
Async XLA Ops:
  2.9 55.1 %collective-permute-start.5 = (bf16[256,2048]{1,0:T(8,128)(2,1)}, bf16[256,2048]{1,0:T(8,128)(2,1)S(1)}, u32[]{:S(2)}, u32[]{:S(2)}) collective-permute-start(bf16[256,2048]{1,0:T(8,128)(2,1)} %decode_weight.1.refs_0_), channel_id=1, source_target_pairs={{0,2},{1,3},{2,4},{3,5},{4,6},{5,7},{6,0},{7,1},{8,10},{9,11},{10,... | collective-permute-start | bytes 3145736 | tf_op jit(solution)/shard_map/ppermute | solution.py:375
  4.9 53.1 %collective-permute-start.6 = (bf16[256,2048]{1,0:T(8,128)(2,1)}, bf16[256,2048]{1,0:T(8,128)(2,1)}, u32[]{:S(2)}, u32[]{:S(2)}) collective-permute-start(bf16[256,2048]{1,0:T(8,128)(2,1)} %decode_weight.1.refs_0_), channel_id=1, source_target_pairs={{0,6},{1,7},{2,0},{3,1},{4,2},{5,3},{6,4},{7,5},{8,14},{9,15},{10,... | collective-permute-start | bytes 3145736 | tf_op jit(solution)/shard_map/ppermute | solution.py:375
  6.2 51.8 %collective-permute-start.7 = (bf16[256,2048]{1,0:T(8,128)(2,1)}, bf16[256,2048]{1,0:T(8,128)(2,1)}, u32[]{:S(2)}, u32[]{:S(2)}) collective-permute-start(bf16[256,2048]{1,0:T(8,128)(2,1)} %decode_weight.1.refs_0_), channel_id=1, source_target_pairs={{0,4},{1,5},{2,6},{3,7},{4,0},{5,1},{6,2},{7,3},{8,12},{9,13},{10,... | collective-permute-start | bytes 3145736 | tf_op jit(solution)/shard_map/ppermute | solution.py:375
  24.2 4.7 %collective-permute-start = (bf16[2,128,128]{2,1,0:T(8,128)(2,1)}, bf16[2,128,128]{2,1,0:T(8,128)(2,1)S(1)}, u32[]{:S(2)}, u32[]{:S(2)}) collective-permute-start(bf16[2,128,128]{2,1,0:T(8,128)(2,1)} %get-tuple-element.28), channel_id=1, source_target_pairs={{0,8},{8,0},{16,24},{24,16},{32,40},{40,32},{48,56},{56,48},{64,72... | collective-permute-start | bytes 196616 | tf_op jit(solution)/shard_map/ppermute | solution.py:381
  25.8 3.1 %copy-start.2 = (bf16[2,128,128]{2,1,0:T(8,128)(2,1)S(1)}, bf16[2,128,128]{2,1,0:T(8,128)(2,1)}, u32[]{:S(2)}) copy-start(bf16[2,128,128]{2,1,0:T(8,128)(2,1)} %get-tuple-element.28) | copy-start | bytes 196612
  28.9 16.9 %copy-start.1 = (bf16[2,128,128]{2,1,0:T(8,128)(2,1)}, bf16[2,128,128]{2,1,0:T(8,128)(2,1)S(1)}, u32[]{:S(2)}) copy-start(bf16[2,128,128]{2,1,0:T(8,128)(2,1)S(1)} %collective-permute-done.refs_5_) | copy-start | bytes 196612
  28.9 5.8 %collective-permute-start.1 = (bf16[2,128,128]{2,1,0:T(8,128)(2,1)S(1)}, bf16[2,128,128]{2,1,0:T(8,128)(2,1)S(1)}, u32[]{:S(2)}, u32[]{:S(2)}) collective-permute-start(bf16[2,128,128]{2,1,0:T(8,128)(2,1)S(1)} %fusion), channel_id=1, source_target_pairs={{0,16},{8,24},{16,0},{24,8},{32,48},{40,56},{48,32},{56,40},{64,80... | collective-permute-start | bytes 196616 | tf_op jit(solution)/shard_map/ppermute | solution.py:381
  34.7 11.1 %copy-start.3 = (bf16[2,128,128]{2,1,0:T(8,128)(2,1)}, bf16[2,128,128]{2,1,0:T(8,128)(2,1)S(1)}, u32[]{:S(2)}) copy-start(bf16[2,128,128]{2,1,0:T(8,128)(2,1)S(1)} %collective-permute-done.1.refs_6_) | copy-start | bytes 196612
  34.8 4.8 %collective-permute-start.2 = (bf16[2,128,128]{2,1,0:T(8,128)(2,1)S(1)}, bf16[2,128,128]{2,1,0:T(8,128)(2,1)S(1)}, u32[]{:S(2)}, u32[]{:S(2)}) collective-permute-start(bf16[2,128,128]{2,1,0:T(8,128)(2,1)S(1)} %fusion.2), channel_id=1, source_target_pairs={{0,32},{8,40},{16,48},{24,56},{32,0},{40,8},{48,16},{56,24},{64,96... | collective-permute-start | bytes 196616 | tf_op jit(solution)/shard_map/ppermute | solution.py:381
  39.6 6.2 %copy-start.4 = (bf16[2,128,128]{2,1,0:T(8,128)(2,1)}, bf16[2,128,128]{2,1,0:T(8,128)(2,1)S(1)}, u32[]{:S(2)}) copy-start(bf16[2,128,128]{2,1,0:T(8,128)(2,1)S(1)} %collective-permute-done.2.refs_7_) | copy-start | bytes 196612
  39.6 6.2 %collective-permute-start.3 = (bf16[2,128,128]{2,1,0:T(8,128)(2,1)S(1)}, bf16[2,128,128]{2,1,0:T(8,128)(2,1)S(1)}, u32[]{:S(2)}, u32[]{:S(2)}) collective-permute-start(bf16[2,128,128]{2,1,0:T(8,128)(2,1)S(1)} %fusion.1), channel_id=1, source_target_pairs={{0,64},{8,72},{16,80},{24,88},{32,96},{40,104},{48,112},{56,120},{... | collective-permute-start | bytes 196616 | tf_op jit(solution)/shard_map/ppermute | solution.py:381
  45.8 7.0 %copy-start.5 = (bf16[2,128,128]{2,1,0:T(8,128)(2,1)}, bf16[2,128,128]{2,1,0:T(8,128)(2,1)S(1)}, u32[]{:S(2)}) copy-start(bf16[2,128,128]{2,1,0:T(8,128)(2,1)S(1)} %collective-permute-done.3.refs_8_) | copy-start | bytes 196612
  45.9 6.9 %collective-permute-start.4 = (bf16[2,128,128]{2,1,0:T(8,128)(2,1)S(1)}, bf16[2,128,128]{2,1,0:T(8,128)(2,1)S(1)}, u32[]{:S(2)}, u32[]{:S(2)}) collective-permute-start(bf16[2,128,128]{2,1,0:T(8,128)(2,1)S(1)} %add_convert_fusion), channel_id=1, source_target_pairs={{0,224},{8,232},{16,240},{24,248},{32,192},{40,200},{48,208},{56,2... | collective-permute-start | bytes 196616 | tf_op jit(solution)/shard_map/ppermute | solution.py:381
  52.8 0.6 copy-start.6
  53.4 4.6 %copy-start = (bf16[256,2048]{1,0:T(8,128)(2,1)S(1)}, bf16[256,2048]{1,0:T(8,128)(2,1)}, u32[]{:S(2)}) copy-start(bf16[256,2048]{1,0:T(8,128)(2,1)} %decode_weight.1.refs_0_) | copy-start | bytes 3145732
  58.0 23.9 %collective-permute-start.8 = (bf16[256,2048]{1,0:T(8,128)(2,1)S(1)}, bf16[256,2048]{1,0:T(8,128)(2,1)}, u32[]{:S(2)}, u32[]{:S(2)}) collective-permute-start(bf16[256,2048]{1,0:T(8,128)(2,1)S(1)} %copy-done), channel_id=1, source_target_pairs={{0,1},{1,0},{2,3},{3,2},{4,5},{5,4},{6,7},{7,6},{8,9},{9,8},{10,11... | collective-permute-start | bytes 3145736 | tf_op jit(solution)/shard_map/ppermute | solution.py:378
  62.3 19.6 %collective-permute-start.9 = (bf16[256,2048]{1,0:T(8,128)(2,1)S(1)}, bf16[256,2048]{1,0:T(8,128)(2,1)}, u32[]{:S(2)}, u32[]{:S(2)}) collective-permute-start(bf16[256,2048]{1,0:T(8,128)(2,1)S(1)} %collective-permute-done.5.refs_1_), channel_id=1, source_target_pairs={{0,1},{1,0},{2,3},{3,2},{4,5},{5,4},{6,7},{7,6},{8,9},{9,8},{10,11... | collective-permute-start | bytes 3145736 | tf_op jit(solution)/shard_map/ppermute | solution.py:378
  62.4 19.5 %collective-permute-start.10 = (bf16[256,2048]{1,0:T(8,128)(2,1)}, bf16[256,2048]{1,0:T(8,128)(2,1)}, u32[]{:S(2)}, u32[]{:S(2)}) collective-permute-start(bf16[256,2048]{1,0:T(8,128)(2,1)} %collective-permute-done.6.refs_2_), channel_id=1, source_target_pairs={{0,1},{1,0},{2,3},{3,2},{4,5},{5,4},{6,7},{7,6},{8,9},{9,8},{10,11... | collective-permute-start | bytes 3145736 | tf_op jit(solution)/shard_map/ppermute | solution.py:378
  62.8 19.1 %collective-permute-start.11 = (bf16[256,2048]{1,0:T(8,128)(2,1)}, bf16[256,2048]{1,0:T(8,128)(2,1)}, u32[]{:S(2)}, u32[]{:S(2)}) collective-permute-start(bf16[256,2048]{1,0:T(8,128)(2,1)} %collective-permute-done.7.refs_3_), channel_id=1, source_target_pairs={{0,1},{1,0},{2,3},{3,2},{4,5},{5,4},{6,7},{7,6},{8,9},{9,8},{10,11... | collective-permute-start | bytes 3145736 | tf_op jit(solution)/shard_map/ppermute | solution.py:378
  62.9 19.0 %all-to-all-start = ((bf16[8,256,256]{2,1,0:T(8,128)(2,1)}), bf16[8,256,256]{2,1,0:T(8,128)(2,1)S(1)}, u32[]{:S(2)}, u32[]{:S(2)}) async-start(bf16[8,256,256]{2,1,0:T(8,128)(2,1)} %bitcast.9), calls=%async_computation | async-start | bytes 2097152 | tf_op jit(solution)/shard_map/all_to_all | solution.py:404

commit v5 on v4

--- a/solution.py
+++ b/solution.py
@@ -36,31 +36,24 @@
 
 
 def decode_kernel(exponent_ref, codes_ref, out_ref):
-    step = pl.program_id(0)
-    blocks = codes_ref.shape[1] // BLOCK
-    for half in range(2):
-        rows = slice(half * BLOCK, (half + 1) * BLOCK)
-        for block in range(blocks):
-            lanes = slice(block * BLOCK, (block + 1) * BLOCK)
-            codes = codes_ref[rows, lanes]
-            power = exponent_ref[half, step * blocks + block] + 16
-            scale = jnp.left_shift(jnp.int32(1), power).astype(F32) * jnp.float32(2.0 ** (-26))
-            size = jnp.left_shift(8 + (codes & 7), (codes >> 3) & 15)
-            size = jnp.where(codes >= 128, -size, size).astype(F32)
-            out_ref[rows, lanes] = (size * scale).astype(BF16)
+    for block in range(codes_ref.shape[1] // BLOCK):
+        lanes = slice(block * BLOCK, (block + 1) * BLOCK)
+        codes = codes_ref[:, lanes]
+        power = exponent_ref[pl.program_id(0), block] + 16
+        scale = jnp.left_shift(jnp.int32(1), power).astype(F32) * jnp.float32(2.0 ** (-26))
+        size = jnp.left_shift(8 + (codes & 7), (codes >> 3) & 15)
+        size = jnp.where(codes >= 128, -size, size).astype(F32)
+        out_ref[:, lanes] = (size * scale).astype(BF16)
 
 
 def decode_weight(codes, exponents):
-    columns = 1024
+    rows = pl.BlockSpec((BLOCK, D), lambda i: (i, 0))
     return pl.pallas_call(
         decode_kernel,
-        grid=(D // columns,),
-        in_specs=[
-            pl.BlockSpec(memory_space=pltpu.SMEM),
-            pl.BlockSpec((2 * BLOCK, columns), lambda i: (0, i)),
-        ],
-        out_specs=pl.BlockSpec((2 * BLOCK, columns), lambda i: (0, i)),
-        out_shape=jax.ShapeDtypeStruct((2 * BLOCK, D), BF16),
+        grid=(codes.shape[0] // BLOCK,),
+        in_specs=[pl.BlockSpec(memory_space=pltpu.SMEM), rows],
+        out_specs=rows,
+        out_shape=jax.ShapeDtypeStruct(codes.shape, BF16),
         compiler_params=pltpu.CompilerParams(vmem_limit_bytes=VMEM_LIMIT),
         cost_estimate=cost(8e6, 3 * MIB),
         name="decode_weight",
@@ -216,8 +209,8 @@
     return 1.0 / (128.0 * math.sqrt(HEAD_DIM * span))
 
 
-def local_kernel(start, q_ref, k_ref, vt_ref, codes_ref, sr_ref, *rest):
-    out_ref = rest[-1]
+def local_kernel(start, picks, q_ref, k_ref, vt_ref, codes_ref, *rest):
+    states, out_ref = dict(zip(picks, rest)), rest[-1]
     subs = q_ref.shape[0] // TILE
     s = lax.broadcasted_iota(jnp.int32, (TILE, TILE), 0)
     t = lax.broadcasted_iota(jnp.int32, (TILE, TILE), 1)
@@ -237,7 +230,7 @@
                 return codes_ref[level, head : head + 1, at].astype(F32) * level_scale(span)
 
             left = jnp.concatenate(
-                [k_ref[at, lanes]] + [sr_ref[r, head] for r, flag in zip(reads, flags) if flag], axis=0
+                [k_ref[at, lanes]] + [states[r][0, head] for r, flag in zip(reads, flags) if flag], axis=0
             )
             product = dot_nt(left, q_ref[at, lanes])
             weight = jnp.where(
@@ -258,24 +251,28 @@
 
 def local_levels(part, query, keys, vt, codes, sr, *earlier):
     rows = query.shape[0]
+    picks = [part] + [4 + part // 2] * (part % 2) + [6] * (part // 2)
     return pl.pallas_call(
-        lambda *refs: local_kernel(part * (ROWS // TILE), *refs),
+        lambda *refs: local_kernel(part * (ROWS // TILE), picks, *refs),
         grid=(1,),
         in_specs=[
             pl.BlockSpec((ROWS, 256), lambda i: (part, 0), pipeline_mode=pl.Buffered(1)),
             pl.BlockSpec((ROWS, 256), lambda i: (part, 0), pipeline_mode=pl.Buffered(1)),
             pl.BlockSpec((256, ROWS), lambda i: (0, part), pipeline_mode=pl.Buffered(1)),
             pl.BlockSpec((11, 2, ROWS), lambda i: (0, 0, part), pipeline_mode=pl.Buffered(1)),
-            full(sr.shape, 1),
+        ]
+        + [
+            pl.BlockSpec((1, 2, 128, 128), lambda i, pick=pick: (pick, 0, 0, 0), pipeline_mode=pl.Buffered(1))
+            for pick in picks
         ]
         + [pl.BlockSpec(memory_space=pl.ANY)] * len(earlier),
         out_specs=pl.BlockSpec((256, ROWS), lambda i: (0, part), pipeline_mode=pl.Buffered(1)),
         out_shape=jax.ShapeDtypeStruct((256, rows), BF16),
-        input_output_aliases={5: 0} if earlier else {},
+        input_output_aliases={4 + len(picks): 0} if earlier else {},
         compiler_params=pltpu.CompilerParams(vmem_limit_bytes=VMEM_LIMIT),
         cost_estimate=cost(3e9, 2 * MIB),
         name=f"local_levels_{part}",
-    )(query, keys, vt, codes, sr, *earlier)
+    )(query, keys, vt, codes, *[sr] * len(picks), *earlier)
 
 
 def attend_kernel(rows_here, at_ref, q_ref, m_ref, gg_ref, codes_ref, *refs):

time: 87.5 us -> 87.2 us (level)
  no operation moved by 1% of the time
where the time goes in v5:
time: 87.2 us; the launch traced here: 86.9 us
  Pallas kernels  40.6 us (47%)
  starting transfers between devices  28.9 us (33%)
  waiting for transfers between devices  16.5 us (19%)
    pallas_call x1, Pallas kernels, projections(): pl.pallas_call(projections_kernel, grid=(1,), in_specs=[anywhere, full((1...  16.3 us
    all_to_all x1, waiting for transfers between devices, body(): lax.all_to_all(attended.reshape(8, 256, 256), 'mp', 0, 0, tiled=True)  15.1 us
    ppermute x5, starting transfers between devices, along_seq(): lax.ppermute(block.astype(BF16), 'seq', [(i, to(i)) for i in range(sender...  14.8 us
    pallas_call x4, Pallas kernels, local_levels(): pl.pallas_call(lambda *refs: local_kernel(part * (ROWS // TILE), picks, *...  11.8 us
    ppermute x4, starting transfers between devices, other_core(): return lax.ppermute(block, 'mp', [(m, m ^ 1) for m in range(8)])  5.19 us
    pallas_call x1, Pallas kernels, project(): pl.pallas_call(project_kernel, grid=(1,), in_specs=[pl.BlockSpec(memory_s...  5.04 us
    ppermute x3, starting transfers between devices, along_x(): lax.ppermute(block, 'mp', [(m, (m // 2 + by) % 4 * 2 + m % 2) for m in ra...  5.04 us
    pallas_call x1, Pallas kernels, attend(): pl.pallas_call(lambda *refs: attend_kernel(rows, *refs), grid=(rows // ti...  4.6 us
  transfers between devices with their start and end apart: 13, of which 2 were waited for; matrix products, arithmetic and copies ran while one was open for 0% of the time, Pallas kernels for 38%

profile of v5, /device:TPU:1, one launch (start us, length us, event | category | flops | bytes accessed | tf_op | source)
XLA Modules:
  0.0 86.9 jit_solution(10732905656931414097)
XLA Ops:
  0.0 2.8 %decode_weight.1.refs_0_ = bf16[256,2048]{1,0:T(8,128)(2,1)} custom-call(s32[2,16]{1,0:T(2,128)} %exponent_ref.1, s32[256,2048]{1,0:T(8,128)} %codes_ref.1), custom_call_target="tpu_custom_call" | custom-call | flops 8000000 | bytes 3145728 | tf_op jit(solution)/shard_map/decode_weight/pallas_call | solution.py:51
  2.8 2.0 %collective-permute-start.5 = (bf16[256,2048]{1,0:T(8,128)(2,1)}, bf16[256,2048]{1,0:T(8,128)(2,1)S(1)}, u32[]{:S(2)}, u32[]{:S(2)}) collective-permute-start(bf16[256,2048]{1,0:T(8,128)(2,1)} %decode_weight.1.refs_0_), channel_id=1, source_target_pairs={{0,2},{1,3},{2,4},{3,5},{4,6},{5,7},{6,0},{7,1},{8,10},{9,11},{10,... | collective-permute-start | bytes 3145736 | tf_op jit(solution)/shard_map/ppermute | solution.py:372
  4.9 1.3 %collective-permute-start.6 = (bf16[256,2048]{1,0:T(8,128)(2,1)}, bf16[256,2048]{1,0:T(8,128)(2,1)}, u32[]{:S(2)}, u32[]{:S(2)}) collective-permute-start(bf16[256,2048]{1,0:T(8,128)(2,1)} %decode_weight.1.refs_0_), channel_id=1, source_target_pairs={{0,6},{1,7},{2,0},{3,1},{4,2},{5,3},{6,4},{7,5},{8,14},{9,15},{10,... | collective-permute-start | bytes 3145736 | tf_op jit(solution)/shard_map/ppermute | solution.py:372
  6.1 1.7 %collective-permute-start.7 = (bf16[256,2048]{1,0:T(8,128)(2,1)}, bf16[256,2048]{1,0:T(8,128)(2,1)}, u32[]{:S(2)}, u32[]{:S(2)}) collective-permute-start(bf16[256,2048]{1,0:T(8,128)(2,1)} %decode_weight.1.refs_0_), channel_id=1, source_target_pairs={{0,4},{1,5},{2,6},{3,7},{4,0},{5,1},{6,2},{7,3},{8,12},{9,13},{10,... | collective-permute-start | bytes 3145736 | tf_op jit(solution)/shard_map/ppermute | solution.py:372
  7.9 16.3 %projections.1 = (bf16[2048,256]{1,0:T(8,128)(2,1)}, bf16[256,2048]{1,0:T(8,128)(2,1)}, bf16[2048,256]{1,0:T(8,128)(2,1)}, bf16[2048,256]{1,0:T(8,128)(2,1)}, bf...) custom-call(bf16[16384,128]{1,0:T(8,128)(2,1)} %bitcast.10, f32[1,256]{1,0:T(1,128)} %bitcast.11, ...), custom_call_target="tpu_custom_call" | custom-call | flops 8589934592 | bytes 18874368 | tf_op jit(solution)/shard_map/projections/pallas_call | solution.py:180
  24.2 1.6 %collective-permute-start = (bf16[2,128,128]{2,1,0:T(8,128)(2,1)}, bf16[2,128,128]{2,1,0:T(8,128)(2,1)S(1)}, u32[]{:S(2)}, u32[]{:S(2)}) collective-permute-start(bf16[2,128,128]{2,1,0:T(8,128)(2,1)} %get-tuple-element.28), channel_id=1, source_target_pairs={{0,8},{8,0},{16,24},{24,16},{32,40},{40,32},{48,56},{56,48},{64,72... | collective-permute-start | bytes 196616 | tf_op jit(solution)/shard_map/ppermute | solution.py:378
  25.7 0.0 copy-start.2
  25.7 3.0 %local_levels_0.1.refs_6_ = bf16[256,2048]{1,0:T(8,128)(2,1)} custom-call(bf16[2048,256]{1,0:T(8,128)(2,1)} %get-tuple-element.27.refs_0_.refs_1_, bf16[2048,256]{1,0:T(8,128)(2,1)} %get-tuple-element.29.refs_1_, bf16[256,2048]{1,0:T(8,128)(2,1)} %get-tuple-element.30.refs_2_, s32[11,2,2048]{2,1,0:T(2,128)} %refs_4_.1, ...), custom_call_target="tpu_custom_call" | custom-call | flops 3000000000 | bytes 2097152 | tf_op jit(solution)/shard_map/local_levels_0/pallas_call | solution.py:255
  28.7 0.0 collective-permute-done.refs_5_
  28.7 0.0 copy-done.2
  28.7 0.0 copy-start.1
  28.7 2.7 %collective-permute-start.1 = (bf16[2,128,128]{2,1,0:T(8,128)(2,1)S(1)}, bf16[2,128,128]{2,1,0:T(8,128)(2,1)S(1)}, u32[]{:S(2)}, u32[]{:S(2)}) collective-permute-start(bf16[2,128,128]{2,1,0:T(8,128)(2,1)S(1)} %fusion), channel_id=1, source_target_pairs={{0,16},{8,24},{16,0},{24,8},{32,48},{40,56},{48,32},{56,40},{64,80... | collective-permute-start | bytes 196616 | tf_op jit(solution)/shard_map/ppermute | solution.py:378
  31.5 2.9 %local_levels_1.1.refs_6_ = bf16[256,2048]{1,0:T(8,128)(2,1)} custom-call(bf16[2048,256]{1,0:T(8,128)(2,1)} %get-tuple-element.27.refs_0_.refs_1_, bf16[2048,256]{1,0:T(8,128)(2,1)} %get-tuple-element.29.refs_1_, bf16[256,2048]{1,0:T(8,128)(2,1)} %get-tuple-element.30.refs_2_, s32[11,2,2048]{2,1,0:T(2,128)} %refs_4_.1, ...), custom_call_target="tpu_custom_call", output_to_operand_aliasing={{}: (6, {})} | custom-call | flops 3000000000 | bytes 2097152 | tf_op jit(solution)/shard_map/local_levels_1/pallas_call | solution.py:255
  34.4 0.0 collective-permute-done.1.refs_6_
  34.4 0.0 copy-start.3
  34.4 1.7 %collective-permute-start.2 = (bf16[2,128,128]{2,1,0:T(8,128)(2,1)S(1)}, bf16[2,128,128]{2,1,0:T(8,128)(2,1)S(1)}, u32[]{:S(2)}, u32[]{:S(2)}) collective-permute-start(bf16[2,128,128]{2,1,0:T(8,128)(2,1)S(1)} %fusion.2), channel_id=1, source_target_pairs={{0,32},{8,40},{16,48},{24,56},{32,0},{40,8},{48,16},{56,24},{64,96... | collective-permute-start | bytes 196616 | tf_op jit(solution)/shard_map/ppermute | solution.py:378
  36.1 2.9 %local_levels_2.1.refs_7_ = bf16[256,2048]{1,0:T(8,128)(2,1)} custom-call(bf16[2048,256]{1,0:T(8,128)(2,1)} %get-tuple-element.27.refs_0_.refs_1_, bf16[2048,256]{1,0:T(8,128)(2,1)} %get-tuple-element.29.refs_1_, bf16[256,2048]{1,0:T(8,128)(2,1)} %get-tuple-element.30.refs_2_, s32[11,2,2048]{2,1,0:T(2,128)} %refs_4_.1, ...), custom_call_target="tpu_custom_call", output_to_operand_aliasing={{}: (6, {})} | custom-call | flops 3000000000 | bytes 2097152 | tf_op jit(solution)/shard_map/local_levels_2/pallas_call | solution.py:255
  39.1 0.0 collective-permute-done.2.refs_7_
  39.1 0.0 copy-start.4
  39.1 3.1 %collective-permute-start.3 = (bf16[2,128,128]{2,1,0:T(8,128)(2,1)S(1)}, bf16[2,128,128]{2,1,0:T(8,128)(2,1)S(1)}, u32[]{:S(2)}, u32[]{:S(2)}) collective-permute-start(bf16[2,128,128]{2,1,0:T(8,128)(2,1)S(1)} %fusion.1), channel_id=1, source_target_pairs={{0,64},{8,72},{16,80},{24,88},{32,96},{40,104},{48,112},{56,120},{... | collective-permute-start | bytes 196616 | tf_op jit(solution)/shard_map/ppermute | solution.py:378
  42.2 3.0 %local_levels_3.1.refs_2_ = bf16[256,2048]{1,0:T(8,128)(2,1)} custom-call(bf16[2048,256]{1,0:T(8,128)(2,1)} %get-tuple-element.27.refs_0_.refs_1_, bf16[2048,256]{1,0:T(8,128)(2,1)} %get-tuple-element.29.refs_1_, bf16[256,2048]{1,0:T(8,128)(2,1)} %get-tuple-element.30.refs_2_, s32[11,2,2048]{2,1,0:T(2,128)} %refs_4_.1, ...), custom_call_target="tpu_custom_call", output_to_operand_aliasing={{}: (7, {})} | custom-call | flops 3000000000 | bytes 2097152 | tf_op jit(solution)/shard_map/local_levels_3/pallas_call | solution.py:255
  45.2 0.0 collective-permute-done.3.refs_8_
  45.2 0.0 copy-done.1
  45.2 0.0 copy-done.3
  45.2 0.0 copy-done.4
  45.2 0.0 copy-start.5
  45.2 0.1 add_convert_fusion
  45.3 5.7 %collective-permute-start.4 = (bf16[2,128,128]{2,1,0:T(8,128)(2,1)S(1)}, bf16[2,128,128]{2,1,0:T(8,128)(2,1)S(1)}, u32[]{:S(2)}, u32[]{:S(2)}) collective-permute-start(bf16[2,128,128]{2,1,0:T(8,128)(2,1)S(1)} %add_convert_fusion), channel_id=1, source_target_pairs={{0,224},{8,232},{16,240},{24,248},{32,192},{40,200},{48,208},{56,2... | collective-permute-start | bytes 196616 | tf_op jit(solution)/shard_map/ppermute | solution.py:378
  51.0 1.3 %collective-permute-done.4.refs_9_ = bf16[2,128,128]{2,1,0:T(8,128)(2,1)S(1)} collective-permute-done((bf16[2,128,128]{2,1,0:T(8,128)(2,1)S(1)}, bf16[2,128,128]{2,1,0:T(8,128)(2,1)S(1)}, u32[]{:S(2)}, u32[]{:S(2)}) %collective-permute-start.4) | collective-permute-done | bytes 65568 | tf_op jit(solution)/shard_map/ppermute | solution.py:378
  52.3 0.0 copy-start.6
  52.3 0.0 copy-done.5
  52.3 0.6 copy-done.6
  52.9 0.0 copy-start
  52.9 4.6 %attend.1 = bf16[2048,256]{1,0:T(8,128)(2,1)} custom-call(s32[1]{0:T(128)} %bitcast.1.refs_0_, bf16[2048,256]{1,0:T(8,128)(2,1)} %get-tuple-element.27.refs_0_.refs_1_, bf16[256,2048]{1,0:T(8,128)(2,1)} %local_levels_3.1.refs_2_, bf16[2048,256]{1,0:T(8,128)(2,1)} %get-tuple-element.39.refs_3_, s32[11,2,2048]{2,1,0:T(2,128)} %refs_4_.1, ...), custom_call_target="tpu_custom_call" | custom-call | flops 3000000000 | bytes 6291456 | tf_op jit(solution)/shard_map/attend/pallas_call | solution.py:304
  57.5 0.0 collective-permute-done.5.refs_1_
  57.5 0.0 collective-permute-done.6.refs_2_
  57.5 0.0 collective-permute-done.7.refs_3_
  57.5 0.0 copy-done
  57.5 4.6 %collective-permute-start.8 = (bf16[256,2048]{1,0:T(8,128)(2,1)S(1)}, bf16[256,2048]{1,0:T(8,128)(2,1)}, u32[]{:S(2)}, u32[]{:S(2)}) collective-permute-start(bf16[256,2048]{1,0:T(8,128)(2,1)S(1)} %copy-done), channel_id=1, source_target_pairs={{0,1},{1,0},{2,3},{3,2},{4,5},{5,4},{6,7},{7,6},{8,9},{9,8},{10,11... | collective-permute-start | bytes 3145736 | tf_op jit(solution)/shard_map/ppermute | solution.py:375
  62.1 0.1 collective-permute-start.9
  62.2 0.4 collective-permute-start.10
  62.6 0.1 collective-permute-start.11
  62.7 3.9 %all-to-all-start = ((bf16[8,256,256]{2,1,0:T(8,128)(2,1)}), bf16[8,256,256]{2,1,0:T(8,128)(2,1)S(1)}, u32[]{:S(2)}, u32[]{:S(2)}) async-start(bf16[8,256,256]{2,1,0:T(8,128)(2,1)} %bitcast.9), calls=%async_computation | async-start | bytes 2097152 | tf_op jit(solution)/shard_map/all_to_all | solution.py:401
  66.6 15.1 %all-to-all-done.a_ref = bf16[8,256,256]{2,1,0:T(8,128)(2,1)S(1)} async-done(((bf16[8,256,256]{2,1,0:T(8,128)(2,1)}), bf16[8,256,256]{2,1,0:T(8,128)(2,1)S(1)}, u32[]{:S(2)}, u32[]{:S(2)}) %all-to-all-start) | async-done | bytes 1048608 | tf_op jit(solution)/shard_map/all_to_all | solution.py:401
  81.7 0.0 collective-permute-done.8.refs_4_
  81.7 0.0 collective-permute-done.9.refs_5_
  81.7 0.0 collective-permute-done.10.refs_6_
  81.7 0.0 collective-permute-done.11.refs_7_
  81.7 5.0 %project.1 = bf16[256,2048]{1,0:T(8,128)(2,1)} custom-call(s32[1]{0:T(128)} %bitcast.at_ref, bf16[8,256,256]{2,1,0:T(8,128)(2,1)S(1)} %all-to-all-done.a_ref, bf16[256,2048]{1,0:T(8,128)(2,1)S(1)} %copy-done, bf16[256,2048]{1,0:T(8,128)(2,1)S(1)} %collective-permute-done.5.refs_1_, bf16[256,2048]{1,0:T(8,128)(2,1)} %collective-permute-done.6.refs_2_, ...), custom_call_target="tpu_custom_call" | custom-call | flops 2147483648 | bytes 10485760 | tf_op jit(solution)/shard_map/project/pallas_call | solution.py:349
  (3 shorter events, 0.1 us)
Async XLA Ops:
  2.8 54.7 %collective-permute-start.5 = (bf16[256,2048]{1,0:T(8,128)(2,1)}, bf16[256,2048]{1,0:T(8,128)(2,1)S(1)}, u32[]{:S(2)}, u32[]{:S(2)}) collective-permute-start(bf16[256,2048]{1,0:T(8,128)(2,1)} %decode_weight.1.refs_0_), channel_id=1, source_target_pairs={{0,2},{1,3},{2,4},{3,5},{4,6},{5,7},{6,0},{7,1},{8,10},{9,11},{10,... | collective-permute-start | bytes 3145736 | tf_op jit(solution)/shard_map/ppermute | solution.py:372
  4.9 52.7 %collective-permute-start.6 = (bf16[256,2048]{1,0:T(8,128)(2,1)}, bf16[256,2048]{1,0:T(8,128)(2,1)}, u32[]{:S(2)}, u32[]{:S(2)}) collective-permute-start(bf16[256,2048]{1,0:T(8,128)(2,1)} %decode_weight.1.refs_0_), channel_id=1, source_target_pairs={{0,6},{1,7},{2,0},{3,1},{4,2},{5,3},{6,4},{7,5},{8,14},{9,15},{10,... | collective-permute-start | bytes 3145736 | tf_op jit(solution)/shard_map/ppermute | solution.py:372
  6.1 51.4 %collective-permute-start.7 = (bf16[256,2048]{1,0:T(8,128)(2,1)}, bf16[256,2048]{1,0:T(8,128)(2,1)}, u32[]{:S(2)}, u32[]{:S(2)}) collective-permute-start(bf16[256,2048]{1,0:T(8,128)(2,1)} %decode_weight.1.refs_0_), channel_id=1, source_target_pairs={{0,4},{1,5},{2,6},{3,7},{4,0},{5,1},{6,2},{7,3},{8,12},{9,13},{10,... | collective-permute-start | bytes 3145736 | tf_op jit(solution)/shard_map/ppermute | solution.py:372
  24.2 4.5 %collective-permute-start = (bf16[2,128,128]{2,1,0:T(8,128)(2,1)}, bf16[2,128,128]{2,1,0:T(8,128)(2,1)S(1)}, u32[]{:S(2)}, u32[]{:S(2)}) collective-permute-start(bf16[2,128,128]{2,1,0:T(8,128)(2,1)} %get-tuple-element.28), channel_id=1, source_target_pairs={{0,8},{8,0},{16,24},{24,16},{32,40},{40,32},{48,56},{56,48},{64,72... | collective-permute-start | bytes 196616 | tf_op jit(solution)/shard_map/ppermute | solution.py:378
  25.7 3.0 %copy-start.2 = (bf16[2,128,128]{2,1,0:T(8,128)(2,1)S(1)}, bf16[2,128,128]{2,1,0:T(8,128)(2,1)}, u32[]{:S(2)}) copy-start(bf16[2,128,128]{2,1,0:T(8,128)(2,1)} %get-tuple-element.28) | copy-start | bytes 196612
  28.7 16.5 %copy-start.1 = (bf16[2,128,128]{2,1,0:T(8,128)(2,1)}, bf16[2,128,128]{2,1,0:T(8,128)(2,1)S(1)}, u32[]{:S(2)}) copy-start(bf16[2,128,128]{2,1,0:T(8,128)(2,1)S(1)} %collective-permute-done.refs_5_) | copy-start | bytes 196612
  28.7 5.6 %collective-permute-start.1 = (bf16[2,128,128]{2,1,0:T(8,128)(2,1)S(1)}, bf16[2,128,128]{2,1,0:T(8,128)(2,1)S(1)}, u32[]{:S(2)}, u32[]{:S(2)}) collective-permute-start(bf16[2,128,128]{2,1,0:T(8,128)(2,1)S(1)} %fusion), channel_id=1, source_target_pairs={{0,16},{8,24},{16,0},{24,8},{32,48},{40,56},{48,32},{56,40},{64,80... | collective-permute-start | bytes 196616 | tf_op jit(solution)/shard_map/ppermute | solution.py:378
  34.4 10.8 %copy-start.3 = (bf16[2,128,128]{2,1,0:T(8,128)(2,1)}, bf16[2,128,128]{2,1,0:T(8,128)(2,1)S(1)}, u32[]{:S(2)}) copy-start(bf16[2,128,128]{2,1,0:T(8,128)(2,1)S(1)} %collective-permute-done.1.refs_6_) | copy-start | bytes 196612
  34.4 4.7 %collective-permute-start.2 = (bf16[2,128,128]{2,1,0:T(8,128)(2,1)S(1)}, bf16[2,128,128]{2,1,0:T(8,128)(2,1)S(1)}, u32[]{:S(2)}, u32[]{:S(2)}) collective-permute-start(bf16[2,128,128]{2,1,0:T(8,128)(2,1)S(1)} %fusion.2), channel_id=1, source_target_pairs={{0,32},{8,40},{16,48},{24,56},{32,0},{40,8},{48,16},{56,24},{64,96... | collective-permute-start | bytes 196616 | tf_op jit(solution)/shard_map/ppermute | solution.py:378
  39.1 6.1 %copy-start.4 = (bf16[2,128,128]{2,1,0:T(8,128)(2,1)}, bf16[2,128,128]{2,1,0:T(8,128)(2,1)S(1)}, u32[]{:S(2)}) copy-start(bf16[2,128,128]{2,1,0:T(8,128)(2,1)S(1)} %collective-permute-done.2.refs_7_) | copy-start | bytes 196612
  39.1 6.1 %collective-permute-start.3 = (bf16[2,128,128]{2,1,0:T(8,128)(2,1)S(1)}, bf16[2,128,128]{2,1,0:T(8,128)(2,1)S(1)}, u32[]{:S(2)}, u32[]{:S(2)}) collective-permute-start(bf16[2,128,128]{2,1,0:T(8,128)(2,1)S(1)} %fusion.1), channel_id=1, source_target_pairs={{0,64},{8,72},{16,80},{24,88},{32,96},{40,104},{48,112},{56,120},{... | collective-permute-start | bytes 196616 | tf_op jit(solution)/shard_map/ppermute | solution.py:378
  45.2 7.1 %copy-start.5 = (bf16[2,128,128]{2,1,0:T(8,128)(2,1)}, bf16[2,128,128]{2,1,0:T(8,128)(2,1)S(1)}, u32[]{:S(2)}) copy-start(bf16[2,128,128]{2,1,0:T(8,128)(2,1)S(1)} %collective-permute-done.3.refs_8_) | copy-start | bytes 196612
  45.3 7.0 %collective-permute-start.4 = (bf16[2,128,128]{2,1,0:T(8,128)(2,1)S(1)}, bf16[2,128,128]{2,1,0:T(8,128)(2,1)S(1)}, u32[]{:S(2)}, u32[]{:S(2)}) collective-permute-start(bf16[2,128,128]{2,1,0:T(8,128)(2,1)S(1)} %add_convert_fusion), channel_id=1, source_target_pairs={{0,224},{8,232},{16,240},{24,248},{32,192},{40,200},{48,208},{56,2... | collective-permute-start | bytes 196616 | tf_op jit(solution)/shard_map/ppermute | solution.py:378
  52.3 0.6 copy-start.6
  52.9 4.6 %copy-start = (bf16[256,2048]{1,0:T(8,128)(2,1)S(1)}, bf16[256,2048]{1,0:T(8,128)(2,1)}, u32[]{:S(2)}) copy-start(bf16[256,2048]{1,0:T(8,128)(2,1)} %decode_weight.1.refs_0_) | copy-start | bytes 3145732
  57.5 24.2 %collective-permute-start.8 = (bf16[256,2048]{1,0:T(8,128)(2,1)S(1)}, bf16[256,2048]{1,0:T(8,128)(2,1)}, u32[]{:S(2)}, u32[]{:S(2)}) collective-permute-start(bf16[256,2048]{1,0:T(8,128)(2,1)S(1)} %copy-done), channel_id=1, source_target_pairs={{0,1},{1,0},{2,3},{3,2},{4,5},{5,4},{6,7},{7,6},{8,9},{9,8},{10,11... | collective-permute-start | bytes 3145736 | tf_op jit(solution)/shard_map/ppermute | solution.py:375
  62.1 19.6 %collective-permute-start.9 = (bf16[256,2048]{1,0:T(8,128)(2,1)S(1)}, bf16[256,2048]{1,0:T(8,128)(2,1)}, u32[]{:S(2)}, u32[]{:S(2)}) collective-permute-start(bf16[256,2048]{1,0:T(8,128)(2,1)S(1)} %collective-permute-done.5.refs_1_), channel_id=1, source_target_pairs={{0,1},{1,0},{2,3},{3,2},{4,5},{5,4},{6,7},{7,6},{8,9},{9,8},{10,11... | collective-permute-start | bytes 3145736 | tf_op jit(solution)/shard_map/ppermute | solution.py:375
  62.2 19.5 %collective-permute-start.10 = (bf16[256,2048]{1,0:T(8,128)(2,1)}, bf16[256,2048]{1,0:T(8,128)(2,1)}, u32[]{:S(2)}, u32[]{:S(2)}) collective-permute-start(bf16[256,2048]{1,0:T(8,128)(2,1)} %collective-permute-done.6.refs_2_), channel_id=1, source_target_pairs={{0,1},{1,0},{2,3},{3,2},{4,5},{5,4},{6,7},{7,6},{8,9},{9,8},{10,11... | collective-permute-start | bytes 3145736 | tf_op jit(solution)/shard_map/ppermute | solution.py:375
  62.6 19.1 %collective-permute-start.11 = (bf16[256,2048]{1,0:T(8,128)(2,1)}, bf16[256,2048]{1,0:T(8,128)(2,1)}, u32[]{:S(2)}, u32[]{:S(2)}) collective-permute-start(bf16[256,2048]{1,0:T(8,128)(2,1)} %collective-permute-done.7.refs_3_), channel_id=1, source_target_pairs={{0,1},{1,0},{2,3},{3,2},{4,5},{5,4},{6,7},{7,6},{8,9},{9,8},{10,11... | collective-permute-start | bytes 3145736 | tf_op jit(solution)/shard_map/ppermute | solution.py:375
  62.7 19.0 %all-to-all-start = ((bf16[8,256,256]{2,1,0:T(8,128)(2,1)}), bf16[8,256,256]{2,1,0:T(8,128)(2,1)S(1)}, u32[]{:S(2)}, u32[]{:S(2)}) async-start(bf16[8,256,256]{2,1,0:T(8,128)(2,1)} %bitcast.9), calls=%async_computation | async-start | bytes 2097152 | tf_op jit(solution)/shard_map/all_to_all | solution.py:401

commit v6 on v5

--- a/solution.py
+++ b/solution.py
@@ -259,7 +259,7 @@
             pl.BlockSpec((ROWS, 256), lambda i: (part, 0), pipeline_mode=pl.Buffered(1)),
             pl.BlockSpec((ROWS, 256), lambda i: (part, 0), pipeline_mode=pl.Buffered(1)),
             pl.BlockSpec((256, ROWS), lambda i: (0, part), pipeline_mode=pl.Buffered(1)),
-            pl.BlockSpec((11, 2, ROWS), lambda i: (0, 0, part), pipeline_mode=pl.Buffered(1)),
+            pl.BlockSpec((6, 2, ROWS), lambda i: (0, 0, part), pipeline_mode=pl.Buffered(1)),
         ]
         + [
             pl.BlockSpec((1, 2, 128, 128), lambda i, pick=pick: (pick, 0, 0, 0), pipeline_mode=pl.Buffered(1))

time: 87.2 us -> 87.2 us (level)
  no operation moved by 1% of the time
where the time goes in v6:
time: 87.2 us; the launch traced here: 86.9 us
  Pallas kernels  40.5 us (46%)
  starting transfers between devices  28.9 us (33%)
  waiting for transfers between devices  16.5 us (19%)
    pallas_call x1, Pallas kernels, projections(): pl.pallas_call(projections_kernel, grid=(1,), in_specs=[anywhere, full((1...  16.3 us
    all_to_all x1, waiting for transfers between devices, body(): lax.all_to_all(attended.reshape(8, 256, 256), 'mp', 0, 0, tiled=True)  15.1 us
    ppermute x5, starting transfers between devices, along_seq(): lax.ppermute(block.astype(BF16), 'seq', [(i, to(i)) for i in range(sender...  14.8 us
    pallas_call x4, Pallas kernels, local_levels(): pl.pallas_call(lambda *refs: local_kernel(part * (ROWS // TILE), picks, *...  11.8 us
    ppermute x4, starting transfers between devices, other_core(): return lax.ppermute(block, 'mp', [(m, m ^ 1) for m in range(8)])  5.21 us
    pallas_call x1, Pallas kernels, project(): pl.pallas_call(project_kernel, grid=(1,), in_specs=[pl.BlockSpec(memory_s...  5.04 us
    ppermute x3, starting transfers between devices, along_x(): lax.ppermute(block, 'mp', [(m, (m // 2 + by) % 4 * 2 + m % 2) for m in ra...  5.04 us
    pallas_call x1, Pallas kernels, attend(): pl.pallas_call(lambda *refs: attend_kernel(rows, *refs), grid=(rows // ti...  4.59 us
  transfers between devices with their start and end apart: 13, of which 2 were waited for; matrix products, arithmetic and copies ran while one was open for 0% of the time, Pallas kernels for 38%

profile of v6, /device:TPU:1, one launch (start us, length us, event | category | flops | bytes accessed | tf_op | source)
XLA Modules:
  0.0 86.9 jit_solution(13824796375288202281)
XLA Ops:
  0.0 2.8 %decode_weight.1.refs_0_ = bf16[256,2048]{1,0:T(8,128)(2,1)} custom-call(s32[2,16]{1,0:T(2,128)} %exponent_ref.1, s32[256,2048]{1,0:T(8,128)} %codes_ref.1), custom_call_target="tpu_custom_call" | custom-call | flops 8000000 | bytes 3145728 | tf_op jit(solution)/shard_map/decode_weight/pallas_call | solution.py:51
  2.8 2.0 %collective-permute-start.5 = (bf16[256,2048]{1,0:T(8,128)(2,1)}, bf16[256,2048]{1,0:T(8,128)(2,1)S(1)}, u32[]{:S(2)}, u32[]{:S(2)}) collective-permute-start(bf16[256,2048]{1,0:T(8,128)(2,1)} %decode_weight.1.refs_0_), channel_id=1, source_target_pairs={{0,2},{1,3},{2,4},{3,5},{4,6},{5,7},{6,0},{7,1},{8,10},{9,11},{10,... | collective-permute-start | bytes 3145736 | tf_op jit(solution)/shard_map/ppermute | solution.py:372
  4.9 1.3 %collective-permute-start.6 = (bf16[256,2048]{1,0:T(8,128)(2,1)}, bf16[256,2048]{1,0:T(8,128)(2,1)}, u32[]{:S(2)}, u32[]{:S(2)}) collective-permute-start(bf16[256,2048]{1,0:T(8,128)(2,1)} %decode_weight.1.refs_0_), channel_id=1, source_target_pairs={{0,6},{1,7},{2,0},{3,1},{4,2},{5,3},{6,4},{7,5},{8,14},{9,15},{10,... | collective-permute-start | bytes 3145736 | tf_op jit(solution)/shard_map/ppermute | solution.py:372
  6.1 1.7 %collective-permute-start.7 = (bf16[256,2048]{1,0:T(8,128)(2,1)}, bf16[256,2048]{1,0:T(8,128)(2,1)}, u32[]{:S(2)}, u32[]{:S(2)}) collective-permute-start(bf16[256,2048]{1,0:T(8,128)(2,1)} %decode_weight.1.refs_0_), channel_id=1, source_target_pairs={{0,4},{1,5},{2,6},{3,7},{4,0},{5,1},{6,2},{7,3},{8,12},{9,13},{10,... | collective-permute-start | bytes 3145736 | tf_op jit(solution)/shard_map/ppermute | solution.py:372
  7.9 16.3 %projections.1 = (bf16[2048,256]{1,0:T(8,128)(2,1)}, bf16[256,2048]{1,0:T(8,128)(2,1)}, bf16[2048,256]{1,0:T(8,128)(2,1)}, bf16[2048,256]{1,0:T(8,128)(2,1)}, bf...) custom-call(bf16[16384,128]{1,0:T(8,128)(2,1)} %bitcast.10, f32[1,256]{1,0:T(1,128)} %bitcast.11, ...), custom_call_target="tpu_custom_call" | custom-call | flops 8589934592 | bytes 18874368 | tf_op jit(solution)/shard_map/projections/pallas_call | solution.py:180
  24.2 1.6 %collective-permute-start = (bf16[2,128,128]{2,1,0:T(8,128)(2,1)}, bf16[2,128,128]{2,1,0:T(8,128)(2,1)S(1)}, u32[]{:S(2)}, u32[]{:S(2)}) collective-permute-start(bf16[2,128,128]{2,1,0:T(8,128)(2,1)} %get-tuple-element.28), channel_id=1, source_target_pairs={{0,8},{8,0},{16,24},{24,16},{32,40},{40,32},{48,56},{56,48},{64,72... | collective-permute-start | bytes 196616 | tf_op jit(solution)/shard_map/ppermute | solution.py:378
  25.7 0.0 copy-start.2
  25.7 3.0 %local_levels_0.1.refs_6_ = bf16[256,2048]{1,0:T(8,128)(2,1)} custom-call(bf16[2048,256]{1,0:T(8,128)(2,1)} %get-tuple-element.27.refs_0_.refs_1_, bf16[2048,256]{1,0:T(8,128)(2,1)} %get-tuple-element.29.refs_1_, bf16[256,2048]{1,0:T(8,128)(2,1)} %get-tuple-element.30.refs_2_, s32[11,2,2048]{2,1,0:T(2,128)} %refs_4_.1, ...), custom_call_target="tpu_custom_call" | custom-call | flops 3000000000 | bytes 2097152 | tf_op jit(solution)/shard_map/local_levels_0/pallas_call | solution.py:255
  28.7 0.0 collective-permute-done.refs_5_
  28.7 0.0 copy-done.2
  28.7 0.0 copy-start.1
  28.7 2.7 %collective-permute-start.1 = (bf16[2,128,128]{2,1,0:T(8,128)(2,1)S(1)}, bf16[2,128,128]{2,1,0:T(8,128)(2,1)S(1)}, u32[]{:S(2)}, u32[]{:S(2)}) collective-permute-start(bf16[2,128,128]{2,1,0:T(8,128)(2,1)S(1)} %fusion), channel_id=1, source_target_pairs={{0,16},{8,24},{16,0},{24,8},{32,48},{40,56},{48,32},{56,40},{64,80... | collective-permute-start | bytes 196616 | tf_op jit(solution)/shard_map/ppermute | solution.py:378
  31.5 2.9 %local_levels_1.1.refs_6_ = bf16[256,2048]{1,0:T(8,128)(2,1)} custom-call(bf16[2048,256]{1,0:T(8,128)(2,1)} %get-tuple-element.27.refs_0_.refs_1_, bf16[2048,256]{1,0:T(8,128)(2,1)} %get-tuple-element.29.refs_1_, bf16[256,2048]{1,0:T(8,128)(2,1)} %get-tuple-element.30.refs_2_, s32[11,2,2048]{2,1,0:T(2,128)} %refs_4_.1, ...), custom_call_target="tpu_custom_call", output_to_operand_aliasing={{}: (6, {})} | custom-call | flops 3000000000 | bytes 2097152 | tf_op jit(solution)/shard_map/local_levels_1/pallas_call | solution.py:255
  34.4 0.0 collective-permute-done.1.refs_6_
  34.4 0.0 copy-start.3
  34.4 1.7 %collective-permute-start.2 = (bf16[2,128,128]{2,1,0:T(8,128)(2,1)S(1)}, bf16[2,128,128]{2,1,0:T(8,128)(2,1)S(1)}, u32[]{:S(2)}, u32[]{:S(2)}) collective-permute-start(bf16[2,128,128]{2,1,0:T(8,128)(2,1)S(1)} %fusion.2), channel_id=1, source_target_pairs={{0,32},{8,40},{16,48},{24,56},{32,0},{40,8},{48,16},{56,24},{64,96... | collective-permute-start | bytes 196616 | tf_op jit(solution)/shard_map/ppermute | solution.py:378
  36.1 2.9 %local_levels_2.1.refs_7_ = bf16[256,2048]{1,0:T(8,128)(2,1)} custom-call(bf16[2048,256]{1,0:T(8,128)(2,1)} %get-tuple-element.27.refs_0_.refs_1_, bf16[2048,256]{1,0:T(8,128)(2,1)} %get-tuple-element.29.refs_1_, bf16[256,2048]{1,0:T(8,128)(2,1)} %get-tuple-element.30.refs_2_, s32[11,2,2048]{2,1,0:T(2,128)} %refs_4_.1, ...), custom_call_target="tpu_custom_call", output_to_operand_aliasing={{}: (6, {})} | custom-call | flops 3000000000 | bytes 2097152 | tf_op jit(solution)/shard_map/local_levels_2/pallas_call | solution.py:255
  39.0 0.0 collective-permute-done.2.refs_7_
  39.0 0.0 copy-start.4
  39.1 3.1 %collective-permute-start.3 = (bf16[2,128,128]{2,1,0:T(8,128)(2,1)S(1)}, bf16[2,128,128]{2,1,0:T(8,128)(2,1)S(1)}, u32[]{:S(2)}, u32[]{:S(2)}) collective-permute-start(bf16[2,128,128]{2,1,0:T(8,128)(2,1)S(1)} %fusion.1), channel_id=1, source_target_pairs={{0,64},{8,72},{16,80},{24,88},{32,96},{40,104},{48,112},{56,120},{... | collective-permute-start | bytes 196616 | tf_op jit(solution)/shard_map/ppermute | solution.py:378
  42.2 3.0 %local_levels_3.1.refs_2_ = bf16[256,2048]{1,0:T(8,128)(2,1)} custom-call(bf16[2048,256]{1,0:T(8,128)(2,1)} %get-tuple-element.27.refs_0_.refs_1_, bf16[2048,256]{1,0:T(8,128)(2,1)} %get-tuple-element.29.refs_1_, bf16[256,2048]{1,0:T(8,128)(2,1)} %get-tuple-element.30.refs_2_, s32[11,2,2048]{2,1,0:T(2,128)} %refs_4_.1, ...), custom_call_target="tpu_custom_call", output_to_operand_aliasing={{}: (7, {})} | custom-call | flops 3000000000 | bytes 2097152 | tf_op jit(solution)/shard_map/local_levels_3/pallas_call | solution.py:255
  45.1 0.0 collective-permute-done.3.refs_8_
  45.1 0.0 copy-done.1
  45.1 0.0 copy-done.3
  45.1 0.0 copy-done.4
  45.2 0.0 copy-start.5
  45.2 0.1 add_convert_fusion
  45.2 5.7 %collective-permute-start.4 = (bf16[2,128,128]{2,1,0:T(8,128)(2,1)S(1)}, bf16[2,128,128]{2,1,0:T(8,128)(2,1)S(1)}, u32[]{:S(2)}, u32[]{:S(2)}) collective-permute-start(bf16[2,128,128]{2,1,0:T(8,128)(2,1)S(1)} %add_convert_fusion), channel_id=1, source_target_pairs={{0,224},{8,232},{16,240},{24,248},{32,192},{40,200},{48,208},{56,2... | collective-permute-start | bytes 196616 | tf_op jit(solution)/shard_map/ppermute | solution.py:378
  51.0 1.3 %collective-permute-done.4.refs_9_ = bf16[2,128,128]{2,1,0:T(8,128)(2,1)S(1)} collective-permute-done((bf16[2,128,128]{2,1,0:T(8,128)(2,1)S(1)}, bf16[2,128,128]{2,1,0:T(8,128)(2,1)S(1)}, u32[]{:S(2)}, u32[]{:S(2)}) %collective-permute-start.4) | collective-permute-done | bytes 65568 | tf_op jit(solution)/shard_map/ppermute | solution.py:378
  52.3 0.0 copy-start.6
  52.3 0.0 copy-done.5
  52.3 0.6 copy-done.6
  52.9 0.0 copy-start
  52.9 4.6 %attend.1 = bf16[2048,256]{1,0:T(8,128)(2,1)} custom-call(s32[1]{0:T(128)} %bitcast.1.refs_0_, bf16[2048,256]{1,0:T(8,128)(2,1)} %get-tuple-element.27.refs_0_.refs_1_, bf16[256,2048]{1,0:T(8,128)(2,1)} %local_levels_3.1.refs_2_, bf16[2048,256]{1,0:T(8,128)(2,1)} %get-tuple-element.39.refs_3_, s32[11,2,2048]{2,1,0:T(2,128)} %refs_4_.1, ...), custom_call_target="tpu_custom_call" | custom-call | flops 3000000000 | bytes 6291456 | tf_op jit(solution)/shard_map/attend/pallas_call | solution.py:304
  57.5 0.0 collective-permute-done.5.refs_1_
  57.5 0.0 collective-permute-done.6.refs_2_
  57.5 0.0 collective-permute-done.7.refs_3_
  57.5 0.0 copy-done
  57.5 4.6 %collective-permute-start.8 = (bf16[256,2048]{1,0:T(8,128)(2,1)S(1)}, bf16[256,2048]{1,0:T(8,128)(2,1)}, u32[]{:S(2)}, u32[]{:S(2)}) collective-permute-start(bf16[256,2048]{1,0:T(8,128)(2,1)S(1)} %copy-done), channel_id=1, source_target_pairs={{0,1},{1,0},{2,3},{3,2},{4,5},{5,4},{6,7},{7,6},{8,9},{9,8},{10,11... | collective-permute-start | bytes 3145736 | tf_op jit(solution)/shard_map/ppermute | solution.py:375
  62.1 0.1 collective-permute-start.9
  62.2 0.4 collective-permute-start.10
  62.6 0.1 collective-permute-start.11
  62.7 3.9 %all-to-all-start = ((bf16[8,256,256]{2,1,0:T(8,128)(2,1)}), bf16[8,256,256]{2,1,0:T(8,128)(2,1)S(1)}, u32[]{:S(2)}, u32[]{:S(2)}) async-start(bf16[8,256,256]{2,1,0:T(8,128)(2,1)} %bitcast.9), calls=%async_computation | async-start | bytes 2097152 | tf_op jit(solution)/shard_map/all_to_all | solution.py:401
  66.6 15.1 %all-to-all-done.a_ref = bf16[8,256,256]{2,1,0:T(8,128)(2,1)S(1)} async-done(((bf16[8,256,256]{2,1,0:T(8,128)(2,1)}), bf16[8,256,256]{2,1,0:T(8,128)(2,1)S(1)}, u32[]{:S(2)}, u32[]{:S(2)}) %all-to-all-start) | async-done | bytes 1048608 | tf_op jit(solution)/shard_map/all_to_all | solution.py:401
  81.7 0.0 collective-permute-done.8.refs_4_
  81.7 0.0 collective-permute-done.9.refs_5_
  81.7 0.0 collective-permute-done.10.refs_6_
  81.7 0.0 collective-permute-done.11.refs_7_
  81.7 5.0 %project.1 = bf16[256,2048]{1,0:T(8,128)(2,1)} custom-call(s32[1]{0:T(128)} %bitcast.at_ref, bf16[8,256,256]{2,1,0:T(8,128)(2,1)S(1)} %all-to-all-done.a_ref, bf16[256,2048]{1,0:T(8,128)(2,1)S(1)} %copy-done, bf16[256,2048]{1,0:T(8,128)(2,1)S(1)} %collective-permute-done.5.refs_1_, bf16[256,2048]{1,0:T(8,128)(2,1)} %collective-permute-done.6.refs_2_, ...), custom_call_target="tpu_custom_call" | custom-call | flops 2147483648 | bytes 10485760 | tf_op jit(solution)/shard_map/project/pallas_call | solution.py:349
  (3 shorter events, 0.1 us)
Async XLA Ops:
  2.8 54.7 %collective-permute-start.5 = (bf16[256,2048]{1,0:T(8,128)(2,1)}, bf16[256,2048]{1,0:T(8,128)(2,1)S(1)}, u32[]{:S(2)}, u32[]{:S(2)}) collective-permute-start(bf16[256,2048]{1,0:T(8,128)(2,1)} %decode_weight.1.refs_0_), channel_id=1, source_target_pairs={{0,2},{1,3},{2,4},{3,5},{4,6},{5,7},{6,0},{7,1},{8,10},{9,11},{10,... | collective-permute-start | bytes 3145736 | tf_op jit(solution)/shard_map/ppermute | solution.py:372
  4.9 52.6 %collective-permute-start.6 = (bf16[256,2048]{1,0:T(8,128)(2,1)}, bf16[256,2048]{1,0:T(8,128)(2,1)}, u32[]{:S(2)}, u32[]{:S(2)}) collective-permute-start(bf16[256,2048]{1,0:T(8,128)(2,1)} %decode_weight.1.refs_0_), channel_id=1, source_target_pairs={{0,6},{1,7},{2,0},{3,1},{4,2},{5,3},{6,4},{7,5},{8,14},{9,15},{10,... | collective-permute-start | bytes 3145736 | tf_op jit(solution)/shard_map/ppermute | solution.py:372
  6.1 51.4 %collective-permute-start.7 = (bf16[256,2048]{1,0:T(8,128)(2,1)}, bf16[256,2048]{1,0:T(8,128)(2,1)}, u32[]{:S(2)}, u32[]{:S(2)}) collective-permute-start(bf16[256,2048]{1,0:T(8,128)(2,1)} %decode_weight.1.refs_0_), channel_id=1, source_target_pairs={{0,4},{1,5},{2,6},{3,7},{4,0},{5,1},{6,2},{7,3},{8,12},{9,13},{10,... | collective-permute-start | bytes 3145736 | tf_op jit(solution)/shard_map/ppermute | solution.py:372
  24.2 4.5 %collective-permute-start = (bf16[2,128,128]{2,1,0:T(8,128)(2,1)}, bf16[2,128,128]{2,1,0:T(8,128)(2,1)S(1)}, u32[]{:S(2)}, u32[]{:S(2)}) collective-permute-start(bf16[2,128,128]{2,1,0:T(8,128)(2,1)} %get-tuple-element.28), channel_id=1, source_target_pairs={{0,8},{8,0},{16,24},{24,16},{32,40},{40,32},{48,56},{56,48},{64,72... | collective-permute-start | bytes 196616 | tf_op jit(solution)/shard_map/ppermute | solution.py:378
  25.7 3.0 %copy-start.2 = (bf16[2,128,128]{2,1,0:T(8,128)(2,1)S(1)}, bf16[2,128,128]{2,1,0:T(8,128)(2,1)}, u32[]{:S(2)}) copy-start(bf16[2,128,128]{2,1,0:T(8,128)(2,1)} %get-tuple-element.28) | copy-start | bytes 196612
  28.7 16.4 %copy-start.1 = (bf16[2,128,128]{2,1,0:T(8,128)(2,1)}, bf16[2,128,128]{2,1,0:T(8,128)(2,1)S(1)}, u32[]{:S(2)}) copy-start(bf16[2,128,128]{2,1,0:T(8,128)(2,1)S(1)} %collective-permute-done.refs_5_) | copy-start | bytes 196612
  28.7 5.6 %collective-permute-start.1 = (bf16[2,128,128]{2,1,0:T(8,128)(2,1)S(1)}, bf16[2,128,128]{2,1,0:T(8,128)(2,1)S(1)}, u32[]{:S(2)}, u32[]{:S(2)}) collective-permute-start(bf16[2,128,128]{2,1,0:T(8,128)(2,1)S(1)} %fusion), channel_id=1, source_target_pairs={{0,16},{8,24},{16,0},{24,8},{32,48},{40,56},{48,32},{56,40},{64,80... | collective-permute-start | bytes 196616 | tf_op jit(solution)/shard_map/ppermute | solution.py:378
  34.4 10.8 %copy-start.3 = (bf16[2,128,128]{2,1,0:T(8,128)(2,1)}, bf16[2,128,128]{2,1,0:T(8,128)(2,1)S(1)}, u32[]{:S(2)}) copy-start(bf16[2,128,128]{2,1,0:T(8,128)(2,1)S(1)} %collective-permute-done.1.refs_6_) | copy-start | bytes 196612
  34.4 4.6 %collective-permute-start.2 = (bf16[2,128,128]{2,1,0:T(8,128)(2,1)S(1)}, bf16[2,128,128]{2,1,0:T(8,128)(2,1)S(1)}, u32[]{:S(2)}, u32[]{:S(2)}) collective-permute-start(bf16[2,128,128]{2,1,0:T(8,128)(2,1)S(1)} %fusion.2), channel_id=1, source_target_pairs={{0,32},{8,40},{16,48},{24,56},{32,0},{40,8},{48,16},{56,24},{64,96... | collective-permute-start | bytes 196616 | tf_op jit(solution)/shard_map/ppermute | solution.py:378
  39.0 6.1 %copy-start.4 = (bf16[2,128,128]{2,1,0:T(8,128)(2,1)}, bf16[2,128,128]{2,1,0:T(8,128)(2,1)S(1)}, u32[]{:S(2)}) copy-start(bf16[2,128,128]{2,1,0:T(8,128)(2,1)S(1)} %collective-permute-done.2.refs_7_) | copy-start | bytes 196612
  39.1 6.0 %collective-permute-start.3 = (bf16[2,128,128]{2,1,0:T(8,128)(2,1)S(1)}, bf16[2,128,128]{2,1,0:T(8,128)(2,1)S(1)}, u32[]{:S(2)}, u32[]{:S(2)}) collective-permute-start(bf16[2,128,128]{2,1,0:T(8,128)(2,1)S(1)} %fusion.1), channel_id=1, source_target_pairs={{0,64},{8,72},{16,80},{24,88},{32,96},{40,104},{48,112},{56,120},{... | collective-permute-start | bytes 196616 | tf_op jit(solution)/shard_map/ppermute | solution.py:378
  45.2 7.1 %copy-start.5 = (bf16[2,128,128]{2,1,0:T(8,128)(2,1)}, bf16[2,128,128]{2,1,0:T(8,128)(2,1)S(1)}, u32[]{:S(2)}) copy-start(bf16[2,128,128]{2,1,0:T(8,128)(2,1)S(1)} %collective-permute-done.3.refs_8_) | copy-start | bytes 196612
  45.2 7.0 %collective-permute-start.4 = (bf16[2,128,128]{2,1,0:T(8,128)(2,1)S(1)}, bf16[2,128,128]{2,1,0:T(8,128)(2,1)S(1)}, u32[]{:S(2)}, u32[]{:S(2)}) collective-permute-start(bf16[2,128,128]{2,1,0:T(8,128)(2,1)S(1)} %add_convert_fusion), channel_id=1, source_target_pairs={{0,224},{8,232},{16,240},{24,248},{32,192},{40,200},{48,208},{56,2... | collective-permute-start | bytes 196616 | tf_op jit(solution)/shard_map/ppermute | solution.py:378
  52.3 0.6 copy-start.6
  52.9 4.6 %copy-start = (bf16[256,2048]{1,0:T(8,128)(2,1)S(1)}, bf16[256,2048]{1,0:T(8,128)(2,1)}, u32[]{:S(2)}) copy-start(bf16[256,2048]{1,0:T(8,128)(2,1)} %decode_weight.1.refs_0_) | copy-start | bytes 3145732
  57.5 24.2 %collective-permute-start.8 = (bf16[256,2048]{1,0:T(8,128)(2,1)S(1)}, bf16[256,2048]{1,0:T(8,128)(2,1)}, u32[]{:S(2)}, u32[]{:S(2)}) collective-permute-start(bf16[256,2048]{1,0:T(8,128)(2,1)S(1)} %copy-done), channel_id=1, source_target_pairs={{0,1},{1,0},{2,3},{3,2},{4,5},{5,4},{6,7},{7,6},{8,9},{9,8},{10,11... | collective-permute-start | bytes 3145736 | tf_op jit(solution)/shard_map/ppermute | solution.py:375
  62.1 19.6 %collective-permute-start.9 = (bf16[256,2048]{1,0:T(8,128)(2,1)S(1)}, bf16[256,2048]{1,0:T(8,128)(2,1)}, u32[]{:S(2)}, u32[]{:S(2)}) collective-permute-start(bf16[256,2048]{1,0:T(8,128)(2,1)S(1)} %collective-permute-done.5.refs_1_), channel_id=1, source_target_pairs={{0,1},{1,0},{2,3},{3,2},{4,5},{5,4},{6,7},{7,6},{8,9},{9,8},{10,11... | collective-permute-start | bytes 3145736 | tf_op jit(solution)/shard_map/ppermute | solution.py:375
  62.2 19.5 %collective-permute-start.10 = (bf16[256,2048]{1,0:T(8,128)(2,1)}, bf16[256,2048]{1,0:T(8,128)(2,1)}, u32[]{:S(2)}, u32[]{:S(2)}) collective-permute-start(bf16[256,2048]{1,0:T(8,128)(2,1)} %collective-permute-done.6.refs_2_), channel_id=1, source_target_pairs={{0,1},{1,0},{2,3},{3,2},{4,5},{5,4},{6,7},{7,6},{8,9},{9,8},{10,11... | collective-permute-start | bytes 3145736 | tf_op jit(solution)/shard_map/ppermute | solution.py:375
  62.6 19.1 %collective-permute-start.11 = (bf16[256,2048]{1,0:T(8,128)(2,1)}, bf16[256,2048]{1,0:T(8,128)(2,1)}, u32[]{:S(2)}, u32[]{:S(2)}) collective-permute-start(bf16[256,2048]{1,0:T(8,128)(2,1)} %collective-permute-done.7.refs_3_), channel_id=1, source_target_pairs={{0,1},{1,0},{2,3},{3,2},{4,5},{5,4},{6,7},{7,6},{8,9},{9,8},{10,11... | collective-permute-start | bytes 3145736 | tf_op jit(solution)/shard_map/ppermute | solution.py:375
  62.7 19.0 %all-to-all-start = ((bf16[8,256,256]{2,1,0:T(8,128)(2,1)}), bf16[8,256,256]{2,1,0:T(8,128)(2,1)S(1)}, u32[]{:S(2)}, u32[]{:S(2)}) async-start(bf16[8,256,256]{2,1,0:T(8,128)(2,1)} %bitcast.9), calls=%async_computation | async-start | bytes 2097152 | tf_op jit(solution)/shard_map/all_to_all | solution.py:401

commit v7 on v5

--- a/solution.py
+++ b/solution.py
@@ -91,7 +91,7 @@
 
     r_copies = [chunk_copy(chunk) for chunk in range(CHUNKS)]
     x_copies = [tile_copy(tile) for tile in range(tiles)]
-    for copy in r_copies[:2] + x_copies[:1] + r_copies[2:] + x_copies[1:]:
+    for copy in r_copies[:4] + x_copies[:1] + r_copies[4:] + x_copies[1:]:
         copy.start()
     for chunk in range(2):
         r_copies[chunk].wait()

time: 87.2 us -> 87.2 us (level)
  no operation moved by 1% of the time
where the time goes in v7:
time: 87.2 us; the launch traced here: 86.9 us
  Pallas kernels  40.6 us (47%)
  starting transfers between devices  28.9 us (33%)
  waiting for transfers between devices  16.5 us (19%)
    pallas_call x1, Pallas kernels, projections(): pl.pallas_call(projections_kernel, grid=(1,), in_specs=[anywhere, full((1...  16.3 us
    all_to_all x1, waiting for transfers between devices, body(): lax.all_to_all(attended.reshape(8, 256, 256), 'mp', 0, 0, tiled=True)  15.1 us
    ppermute x5, starting transfers between devices, along_seq(): lax.ppermute(block.astype(BF16), 'seq', [(i, to(i)) for i in range(sender...  14.8 us
    pallas_call x4, Pallas kernels, local_levels(): pl.pallas_call(lambda *refs: local_kernel(part * (ROWS // TILE), picks, *...  11.8 us
    ppermute x4, starting transfers between devices, other_core(): return lax.ppermute(block, 'mp', [(m, m ^ 1) for m in range(8)])  5.19 us
    pallas_call x1, Pallas kernels, project(): pl.pallas_call(project_kernel, grid=(1,), in_specs=[pl.BlockSpec(memory_s...  5.04 us
    ppermute x3, starting transfers between devices, along_x(): lax.ppermute(block, 'mp', [(m, (m // 2 + by) % 4 * 2 + m % 2) for m in ra...  5.04 us
    pallas_call x1, Pallas kernels, attend(): pl.pallas_call(lambda *refs: attend_kernel(rows, *refs), grid=(rows // ti...  4.6 us
  transfers between devices with their start and end apart: 13, of which 2 were waited for; matrix products, arithmetic and copies ran while one was open for 0% of the time, Pallas kernels for 38%

profile of v7, /device:TPU:1, one launch (start us, length us, event | category | flops | bytes accessed | tf_op | source)
XLA Modules:
  0.0 86.9 jit_solution(10732905656931414097)
XLA Ops:
  0.0 2.8 %decode_weight.1.refs_0_ = bf16[256,2048]{1,0:T(8,128)(2,1)} custom-call(s32[2,16]{1,0:T(2,128)} %exponent_ref.1, s32[256,2048]{1,0:T(8,128)} %codes_ref.1), custom_call_target="tpu_custom_call" | custom-call | flops 8000000 | bytes 3145728 | tf_op jit(solution)/shard_map/decode_weight/pallas_call | solution.py:51
  2.8 2.0 %collective-permute-start.5 = (bf16[256,2048]{1,0:T(8,128)(2,1)}, bf16[256,2048]{1,0:T(8,128)(2,1)S(1)}, u32[]{:S(2)}, u32[]{:S(2)}) collective-permute-start(bf16[256,2048]{1,0:T(8,128)(2,1)} %decode_weight.1.refs_0_), channel_id=1, source_target_pairs={{0,2},{1,3},{2,4},{3,5},{4,6},{5,7},{6,0},{7,1},{8,10},{9,11},{10,... | collective-permute-start | bytes 3145736 | tf_op jit(solution)/shard_map/ppermute | solution.py:372
  4.9 1.3 %collective-permute-start.6 = (bf16[256,2048]{1,0:T(8,128)(2,1)}, bf16[256,2048]{1,0:T(8,128)(2,1)}, u32[]{:S(2)}, u32[]{:S(2)}) collective-permute-start(bf16[256,2048]{1,0:T(8,128)(2,1)} %decode_weight.1.refs_0_), channel_id=1, source_target_pairs={{0,6},{1,7},{2,0},{3,1},{4,2},{5,3},{6,4},{7,5},{8,14},{9,15},{10,... | collective-permute-start | bytes 3145736 | tf_op jit(solution)/shard_map/ppermute | solution.py:372
  6.1 1.7 %collective-permute-start.7 = (bf16[256,2048]{1,0:T(8,128)(2,1)}, bf16[256,2048]{1,0:T(8,128)(2,1)}, u32[]{:S(2)}, u32[]{:S(2)}) collective-permute-start(bf16[256,2048]{1,0:T(8,128)(2,1)} %decode_weight.1.refs_0_), channel_id=1, source_target_pairs={{0,4},{1,5},{2,6},{3,7},{4,0},{5,1},{6,2},{7,3},{8,12},{9,13},{10,... | collective-permute-start | bytes 3145736 | tf_op jit(solution)/shard_map/ppermute | solution.py:372
  7.9 16.3 %projections.1 = (bf16[2048,256]{1,0:T(8,128)(2,1)}, bf16[256,2048]{1,0:T(8,128)(2,1)}, bf16[2048,256]{1,0:T(8,128)(2,1)}, bf16[2048,256]{1,0:T(8,128)(2,1)}, bf...) custom-call(bf16[16384,128]{1,0:T(8,128)(2,1)} %bitcast.10, f32[1,256]{1,0:T(1,128)} %bitcast.11, ...), custom_call_target="tpu_custom_call" | custom-call | flops 8589934592 | bytes 18874368 | tf_op jit(solution)/shard_map/projections/pallas_call | solution.py:180
  24.2 1.6 %collective-permute-start = (bf16[2,128,128]{2,1,0:T(8,128)(2,1)}, bf16[2,128,128]{2,1,0:T(8,128)(2,1)S(1)}, u32[]{:S(2)}, u32[]{:S(2)}) collective-permute-start(bf16[2,128,128]{2,1,0:T(8,128)(2,1)} %get-tuple-element.28), channel_id=1, source_target_pairs={{0,8},{8,0},{16,24},{24,16},{32,40},{40,32},{48,56},{56,48},{64,72... | collective-permute-start | bytes 196616 | tf_op jit(solution)/shard_map/ppermute | solution.py:378
  25.7 0.0 copy-start.2
  25.7 3.0 %local_levels_0.1.refs_6_ = bf16[256,2048]{1,0:T(8,128)(2,1)} custom-call(bf16[2048,256]{1,0:T(8,128)(2,1)} %get-tuple-element.27.refs_0_.refs_1_, bf16[2048,256]{1,0:T(8,128)(2,1)} %get-tuple-element.29.refs_1_, bf16[256,2048]{1,0:T(8,128)(2,1)} %get-tuple-element.30.refs_2_, s32[11,2,2048]{2,1,0:T(2,128)} %refs_4_.1, ...), custom_call_target="tpu_custom_call" | custom-call | flops 3000000000 | bytes 2097152 | tf_op jit(solution)/shard_map/local_levels_0/pallas_call | solution.py:255
  28.7 0.0 collective-permute-done.refs_5_
  28.7 0.0 copy-done.2
  28.7 0.0 copy-start.1
  28.7 2.7 %collective-permute-start.1 = (bf16[2,128,128]{2,1,0:T(8,128)(2,1)S(1)}, bf16[2,128,128]{2,1,0:T(8,128)(2,1)S(1)}, u32[]{:S(2)}, u32[]{:S(2)}) collective-permute-start(bf16[2,128,128]{2,1,0:T(8,128)(2,1)S(1)} %fusion), channel_id=1, source_target_pairs={{0,16},{8,24},{16,0},{24,8},{32,48},{40,56},{48,32},{56,40},{64,80... | collective-permute-start | bytes 196616 | tf_op jit(solution)/shard_map/ppermute | solution.py:378
  31.5 2.9 %local_levels_1.1.refs_6_ = bf16[256,2048]{1,0:T(8,128)(2,1)} custom-call(bf16[2048,256]{1,0:T(8,128)(2,1)} %get-tuple-element.27.refs_0_.refs_1_, bf16[2048,256]{1,0:T(8,128)(2,1)} %get-tuple-element.29.refs_1_, bf16[256,2048]{1,0:T(8,128)(2,1)} %get-tuple-element.30.refs_2_, s32[11,2,2048]{2,1,0:T(2,128)} %refs_4_.1, ...), custom_call_target="tpu_custom_call", output_to_operand_aliasing={{}: (6, {})} | custom-call | flops 3000000000 | bytes 2097152 | tf_op jit(solution)/shard_map/local_levels_1/pallas_call | solution.py:255
  34.4 0.0 collective-permute-done.1.refs_6_
  34.4 0.0 copy-start.3
  34.4 1.7 %collective-permute-start.2 = (bf16[2,128,128]{2,1,0:T(8,128)(2,1)S(1)}, bf16[2,128,128]{2,1,0:T(8,128)(2,1)S(1)}, u32[]{:S(2)}, u32[]{:S(2)}) collective-permute-start(bf16[2,128,128]{2,1,0:T(8,128)(2,1)S(1)} %fusion.2), channel_id=1, source_target_pairs={{0,32},{8,40},{16,48},{24,56},{32,0},{40,8},{48,16},{56,24},{64,96... | collective-permute-start | bytes 196616 | tf_op jit(solution)/shard_map/ppermute | solution.py:378
  36.1 2.9 %local_levels_2.1.refs_7_ = bf16[256,2048]{1,0:T(8,128)(2,1)} custom-call(bf16[2048,256]{1,0:T(8,128)(2,1)} %get-tuple-element.27.refs_0_.refs_1_, bf16[2048,256]{1,0:T(8,128)(2,1)} %get-tuple-element.29.refs_1_, bf16[256,2048]{1,0:T(8,128)(2,1)} %get-tuple-element.30.refs_2_, s32[11,2,2048]{2,1,0:T(2,128)} %refs_4_.1, ...), custom_call_target="tpu_custom_call", output_to_operand_aliasing={{}: (6, {})} | custom-call | flops 3000000000 | bytes 2097152 | tf_op jit(solution)/shard_map/local_levels_2/pallas_call | solution.py:255
  39.1 0.0 collective-permute-done.2.refs_7_
  39.1 0.0 copy-start.4
  39.1 3.1 %collective-permute-start.3 = (bf16[2,128,128]{2,1,0:T(8,128)(2,1)S(1)}, bf16[2,128,128]{2,1,0:T(8,128)(2,1)S(1)}, u32[]{:S(2)}, u32[]{:S(2)}) collective-permute-start(bf16[2,128,128]{2,1,0:T(8,128)(2,1)S(1)} %fusion.1), channel_id=1, source_target_pairs={{0,64},{8,72},{16,80},{24,88},{32,96},{40,104},{48,112},{56,120},{... | collective-permute-start | bytes 196616 | tf_op jit(solution)/shard_map/ppermute | solution.py:378
  42.2 3.0 %local_levels_3.1.refs_2_ = bf16[256,2048]{1,0:T(8,128)(2,1)} custom-call(bf16[2048,256]{1,0:T(8,128)(2,1)} %get-tuple-element.27.refs_0_.refs_1_, bf16[2048,256]{1,0:T(8,128)(2,1)} %get-tuple-element.29.refs_1_, bf16[256,2048]{1,0:T(8,128)(2,1)} %get-tuple-element.30.refs_2_, s32[11,2,2048]{2,1,0:T(2,128)} %refs_4_.1, ...), custom_call_target="tpu_custom_call", output_to_operand_aliasing={{}: (7, {})} | custom-call | flops 3000000000 | bytes 2097152 | tf_op jit(solution)/shard_map/local_levels_3/pallas_call | solution.py:255
  45.2 0.0 collective-permute-done.3.refs_8_
  45.2 0.0 copy-done.1
  45.2 0.0 copy-done.3
  45.2 0.0 copy-done.4
  45.2 0.0 copy-start.5
  45.2 0.1 add_convert_fusion
  45.3 5.7 %collective-permute-start.4 = (bf16[2,128,128]{2,1,0:T(8,128)(2,1)S(1)}, bf16[2,128,128]{2,1,0:T(8,128)(2,1)S(1)}, u32[]{:S(2)}, u32[]{:S(2)}) collective-permute-start(bf16[2,128,128]{2,1,0:T(8,128)(2,1)S(1)} %add_convert_fusion), channel_id=1, source_target_pairs={{0,224},{8,232},{16,240},{24,248},{32,192},{40,200},{48,208},{56,2... | collective-permute-start | bytes 196616 | tf_op jit(solution)/shard_map/ppermute | solution.py:378
  51.0 1.3 %collective-permute-done.4.refs_9_ = bf16[2,128,128]{2,1,0:T(8,128)(2,1)S(1)} collective-permute-done((bf16[2,128,128]{2,1,0:T(8,128)(2,1)S(1)}, bf16[2,128,128]{2,1,0:T(8,128)(2,1)S(1)}, u32[]{:S(2)}, u32[]{:S(2)}) %collective-permute-start.4) | collective-permute-done | bytes 65568 | tf_op jit(solution)/shard_map/ppermute | solution.py:378
  52.3 0.0 copy-start.6
  52.3 0.0 copy-done.5
  52.3 0.6 copy-done.6
  52.9 0.0 copy-start
  52.9 4.6 %attend.1 = bf16[2048,256]{1,0:T(8,128)(2,1)} custom-call(s32[1]{0:T(128)} %bitcast.1.refs_0_, bf16[2048,256]{1,0:T(8,128)(2,1)} %get-tuple-element.27.refs_0_.refs_1_, bf16[256,2048]{1,0:T(8,128)(2,1)} %local_levels_3.1.refs_2_, bf16[2048,256]{1,0:T(8,128)(2,1)} %get-tuple-element.39.refs_3_, s32[11,2,2048]{2,1,0:T(2,128)} %refs_4_.1, ...), custom_call_target="tpu_custom_call" | custom-call | flops 3000000000 | bytes 6291456 | tf_op jit(solution)/shard_map/attend/pallas_call | solution.py:304
  57.5 0.0 collective-permute-done.5.refs_1_
  57.5 0.0 collective-permute-done.6.refs_2_
  57.5 0.0 collective-permute-done.7.refs_3_
  57.5 0.0 copy-done
  57.5 4.6 %collective-permute-start.8 = (bf16[256,2048]{1,0:T(8,128)(2,1)S(1)}, bf16[256,2048]{1,0:T(8,128)(2,1)}, u32[]{:S(2)}, u32[]{:S(2)}) collective-permute-start(bf16[256,2048]{1,0:T(8,128)(2,1)S(1)} %copy-done), channel_id=1, source_target_pairs={{0,1},{1,0},{2,3},{3,2},{4,5},{5,4},{6,7},{7,6},{8,9},{9,8},{10,11... | collective-permute-start | bytes 3145736 | tf_op jit(solution)/shard_map/ppermute | solution.py:375
  62.1 0.1 collective-permute-start.9
  62.2 0.4 collective-permute-start.10
  62.6 0.1 collective-permute-start.11
  62.7 3.9 %all-to-all-start = ((bf16[8,256,256]{2,1,0:T(8,128)(2,1)}), bf16[8,256,256]{2,1,0:T(8,128)(2,1)S(1)}, u32[]{:S(2)}, u32[]{:S(2)}) async-start(bf16[8,256,256]{2,1,0:T(8,128)(2,1)} %bitcast.9), calls=%async_computation | async-start | bytes 2097152 | tf_op jit(solution)/shard_map/all_to_all | solution.py:401
  66.6 15.1 %all-to-all-done.a_ref = bf16[8,256,256]{2,1,0:T(8,128)(2,1)S(1)} async-done(((bf16[8,256,256]{2,1,0:T(8,128)(2,1)}), bf16[8,256,256]{2,1,0:T(8,128)(2,1)S(1)}, u32[]{:S(2)}, u32[]{:S(2)}) %all-to-all-start) | async-done | bytes 1048608 | tf_op jit(solution)/shard_map/all_to_all | solution.py:401
  81.7 0.0 collective-permute-done.8.refs_4_
  81.7 0.0 collective-permute-done.9.refs_5_
  81.7 0.0 collective-permute-done.10.refs_6_
  81.7 0.0 collective-permute-done.11.refs_7_
  81.7 5.0 %project.1 = bf16[256,2048]{1,0:T(8,128)(2,1)} custom-call(s32[1]{0:T(128)} %bitcast.at_ref, bf16[8,256,256]{2,1,0:T(8,128)(2,1)S(1)} %all-to-all-done.a_ref, bf16[256,2048]{1,0:T(8,128)(2,1)S(1)} %copy-done, bf16[256,2048]{1,0:T(8,128)(2,1)S(1)} %collective-permute-done.5.refs_1_, bf16[256,2048]{1,0:T(8,128)(2,1)} %collective-permute-done.6.refs_2_, ...), custom_call_target="tpu_custom_call" | custom-call | flops 2147483648 | bytes 10485760 | tf_op jit(solution)/shard_map/project/pallas_call | solution.py:349
  (3 shorter events, 0.1 us)
Async XLA Ops:
  2.8 54.7 %collective-permute-start.5 = (bf16[256,2048]{1,0:T(8,128)(2,1)}, bf16[256,2048]{1,0:T(8,128)(2,1)S(1)}, u32[]{:S(2)}, u32[]{:S(2)}) collective-permute-start(bf16[256,2048]{1,0:T(8,128)(2,1)} %decode_weight.1.refs_0_), channel_id=1, source_target_pairs={{0,2},{1,3},{2,4},{3,5},{4,6},{5,7},{6,0},{7,1},{8,10},{9,11},{10,... | collective-permute-start | bytes 3145736 | tf_op jit(solution)/shard_map/ppermute | solution.py:372
  4.9 52.7 %collective-permute-start.6 = (bf16[256,2048]{1,0:T(8,128)(2,1)}, bf16[256,2048]{1,0:T(8,128)(2,1)}, u32[]{:S(2)}, u32[]{:S(2)}) collective-permute-start(bf16[256,2048]{1,0:T(8,128)(2,1)} %decode_weight.1.refs_0_), channel_id=1, source_target_pairs={{0,6},{1,7},{2,0},{3,1},{4,2},{5,3},{6,4},{7,5},{8,14},{9,15},{10,... | collective-permute-start | bytes 3145736 | tf_op jit(solution)/shard_map/ppermute | solution.py:372
  6.1 51.4 %collective-permute-start.7 = (bf16[256,2048]{1,0:T(8,128)(2,1)}, bf16[256,2048]{1,0:T(8,128)(2,1)}, u32[]{:S(2)}, u32[]{:S(2)}) collective-permute-start(bf16[256,2048]{1,0:T(8,128)(2,1)} %decode_weight.1.refs_0_), channel_id=1, source_target_pairs={{0,4},{1,5},{2,6},{3,7},{4,0},{5,1},{6,2},{7,3},{8,12},{9,13},{10,... | collective-permute-start | bytes 3145736 | tf_op jit(solution)/shard_map/ppermute | solution.py:372
  24.2 4.5 %collective-permute-start = (bf16[2,128,128]{2,1,0:T(8,128)(2,1)}, bf16[2,128,128]{2,1,0:T(8,128)(2,1)S(1)}, u32[]{:S(2)}, u32[]{:S(2)}) collective-permute-start(bf16[2,128,128]{2,1,0:T(8,128)(2,1)} %get-tuple-element.28), channel_id=1, source_target_pairs={{0,8},{8,0},{16,24},{24,16},{32,40},{40,32},{48,56},{56,48},{64,72... | collective-permute-start | bytes 196616 | tf_op jit(solution)/shard_map/ppermute | solution.py:378
  25.7 3.0 %copy-start.2 = (bf16[2,128,128]{2,1,0:T(8,128)(2,1)S(1)}, bf16[2,128,128]{2,1,0:T(8,128)(2,1)}, u32[]{:S(2)}) copy-start(bf16[2,128,128]{2,1,0:T(8,128)(2,1)} %get-tuple-element.28) | copy-start | bytes 196612
  28.7 16.5 %copy-start.1 = (bf16[2,128,128]{2,1,0:T(8,128)(2,1)}, bf16[2,128,128]{2,1,0:T(8,128)(2,1)S(1)}, u32[]{:S(2)}) copy-start(bf16[2,128,128]{2,1,0:T(8,128)(2,1)S(1)} %collective-permute-done.refs_5_) | copy-start | bytes 196612
  28.7 5.6 %collective-permute-start.1 = (bf16[2,128,128]{2,1,0:T(8,128)(2,1)S(1)}, bf16[2,128,128]{2,1,0:T(8,128)(2,1)S(1)}, u32[]{:S(2)}, u32[]{:S(2)}) collective-permute-start(bf16[2,128,128]{2,1,0:T(8,128)(2,1)S(1)} %fusion), channel_id=1, source_target_pairs={{0,16},{8,24},{16,0},{24,8},{32,48},{40,56},{48,32},{56,40},{64,80... | collective-permute-start | bytes 196616 | tf_op jit(solution)/shard_map/ppermute | solution.py:378
  34.4 10.8 %copy-start.3 = (bf16[2,128,128]{2,1,0:T(8,128)(2,1)}, bf16[2,128,128]{2,1,0:T(8,128)(2,1)S(1)}, u32[]{:S(2)}) copy-start(bf16[2,128,128]{2,1,0:T(8,128)(2,1)S(1)} %collective-permute-done.1.refs_6_) | copy-start | bytes 196612
  34.4 4.7 %collective-permute-start.2 = (bf16[2,128,128]{2,1,0:T(8,128)(2,1)S(1)}, bf16[2,128,128]{2,1,0:T(8,128)(2,1)S(1)}, u32[]{:S(2)}, u32[]{:S(2)}) collective-permute-start(bf16[2,128,128]{2,1,0:T(8,128)(2,1)S(1)} %fusion.2), channel_id=1, source_target_pairs={{0,32},{8,40},{16,48},{24,56},{32,0},{40,8},{48,16},{56,24},{64,96... | collective-permute-start | bytes 196616 | tf_op jit(solution)/shard_map/ppermute | solution.py:378
  39.1 6.1 %copy-start.4 = (bf16[2,128,128]{2,1,0:T(8,128)(2,1)}, bf16[2,128,128]{2,1,0:T(8,128)(2,1)S(1)}, u32[]{:S(2)}) copy-start(bf16[2,128,128]{2,1,0:T(8,128)(2,1)S(1)} %collective-permute-done.2.refs_7_) | copy-start | bytes 196612
  39.1 6.1 %collective-permute-start.3 = (bf16[2,128,128]{2,1,0:T(8,128)(2,1)S(1)}, bf16[2,128,128]{2,1,0:T(8,128)(2,1)S(1)}, u32[]{:S(2)}, u32[]{:S(2)}) collective-permute-start(bf16[2,128,128]{2,1,0:T(8,128)(2,1)S(1)} %fusion.1), channel_id=1, source_target_pairs={{0,64},{8,72},{16,80},{24,88},{32,96},{40,104},{48,112},{56,120},{... | collective-permute-start | bytes 196616 | tf_op jit(solution)/shard_map/ppermute | solution.py:378
  45.2 7.1 %copy-start.5 = (bf16[2,128,128]{2,1,0:T(8,128)(2,1)}, bf16[2,128,128]{2,1,0:T(8,128)(2,1)S(1)}, u32[]{:S(2)}) copy-start(bf16[2,128,128]{2,1,0:T(8,128)(2,1)S(1)} %collective-permute-done.3.refs_8_) | copy-start | bytes 196612
  45.3 7.0 %collective-permute-start.4 = (bf16[2,128,128]{2,1,0:T(8,128)(2,1)S(1)}, bf16[2,128,128]{2,1,0:T(8,128)(2,1)S(1)}, u32[]{:S(2)}, u32[]{:S(2)}) collective-permute-start(bf16[2,128,128]{2,1,0:T(8,128)(2,1)S(1)} %add_convert_fusion), channel_id=1, source_target_pairs={{0,224},{8,232},{16,240},{24,248},{32,192},{40,200},{48,208},{56,2... | collective-permute-start | bytes 196616 | tf_op jit(solution)/shard_map/ppermute | solution.py:378
  52.3 0.6 copy-start.6
  52.9 4.6 %copy-start = (bf16[256,2048]{1,0:T(8,128)(2,1)S(1)}, bf16[256,2048]{1,0:T(8,128)(2,1)}, u32[]{:S(2)}) copy-start(bf16[256,2048]{1,0:T(8,128)(2,1)} %decode_weight.1.refs_0_) | copy-start | bytes 3145732
  57.5 24.2 %collective-permute-start.8 = (bf16[256,2048]{1,0:T(8,128)(2,1)S(1)}, bf16[256,2048]{1,0:T(8,128)(2,1)}, u32[]{:S(2)}, u32[]{:S(2)}) collective-permute-start(bf16[256,2048]{1,0:T(8,128)(2,1)S(1)} %copy-done), channel_id=1, source_target_pairs={{0,1},{1,0},{2,3},{3,2},{4,5},{5,4},{6,7},{7,6},{8,9},{9,8},{10,11... | collective-permute-start | bytes 3145736 | tf_op jit(solution)/shard_map/ppermute | solution.py:375
  62.1 19.6 %collective-permute-start.9 = (bf16[256,2048]{1,0:T(8,128)(2,1)S(1)}, bf16[256,2048]{1,0:T(8,128)(2,1)}, u32[]{:S(2)}, u32[]{:S(2)}) collective-permute-start(bf16[256,2048]{1,0:T(8,128)(2,1)S(1)} %collective-permute-done.5.refs_1_), channel_id=1, source_target_pairs={{0,1},{1,0},{2,3},{3,2},{4,5},{5,4},{6,7},{7,6},{8,9},{9,8},{10,11... | collective-permute-start | bytes 3145736 | tf_op jit(solution)/shard_map/ppermute | solution.py:375
  62.2 19.5 %collective-permute-start.10 = (bf16[256,2048]{1,0:T(8,128)(2,1)}, bf16[256,2048]{1,0:T(8,128)(2,1)}, u32[]{:S(2)}, u32[]{:S(2)}) collective-permute-start(bf16[256,2048]{1,0:T(8,128)(2,1)} %collective-permute-done.6.refs_2_), channel_id=1, source_target_pairs={{0,1},{1,0},{2,3},{3,2},{4,5},{5,4},{6,7},{7,6},{8,9},{9,8},{10,11... | collective-permute-start | bytes 3145736 | tf_op jit(solution)/shard_map/ppermute | solution.py:375
  62.6 19.1 %collective-permute-start.11 = (bf16[256,2048]{1,0:T(8,128)(2,1)}, bf16[256,2048]{1,0:T(8,128)(2,1)}, u32[]{:S(2)}, u32[]{:S(2)}) collective-permute-start(bf16[256,2048]{1,0:T(8,128)(2,1)} %collective-permute-done.7.refs_3_), channel_id=1, source_target_pairs={{0,1},{1,0},{2,3},{3,2},{4,5},{5,4},{6,7},{7,6},{8,9},{9,8},{10,11... | collective-permute-start | bytes 3145736 | tf_op jit(solution)/shard_map/ppermute | solution.py:375
  62.7 19.0 %all-to-all-start = ((bf16[8,256,256]{2,1,0:T(8,128)(2,1)}), bf16[8,256,256]{2,1,0:T(8,128)(2,1)S(1)}, u32[]{:S(2)}, u32[]{:S(2)}) async-start(bf16[8,256,256]{2,1,0:T(8,128)(2,1)} %bitcast.9), calls=%async_computation | async-start | bytes 2097152 | tf_op jit(solution)/shard_map/all_to_all | solution.py:401
